TPU v7x, 32 devices: a whole 2x2x4 slice. The times are simulated.
32 devices in a mesh: dp: 2 (over x), ctx: 16 (over z, y, core).
Axes of the slice: x: 2, y: 2, z: 4, core: 2. Of those that a mesh axis runs over, the one named last changes fastest.
Arguments:
- layer_input: bfloat16 [2, 2048, 8192], P('dp', 'ctx'), may hold values from -6 to 6
- queries: bfloat16 [2, 2048, 1024], P('dp', 'ctx'), may hold values from -6 to 6
- keys: bfloat16 [2, 2048, 128], P('dp', 'ctx'), may hold values from -6 to 6
- values: bfloat16 [2, 2048, 128], P('dp', 'ctx'), may hold values from -6 to 6
- d_out: bfloat16 [2, 2048, 1024], P('dp', 'ctx'), may hold values from -6 to 6
- doc_lengths: int32 [2, 8], P('dp'), may hold values from 1 to 512, 2048 in all within a row
- block_order: int32 [32], replicated, may hold values from 0 to 31, as said below
Outputs:
- query_grad: bfloat16 [2, 2048, 1024], P('dp', 'ctx')
- key_grad: bfloat16 [2, 2048, 128], P('dp', 'ctx')
- value_grad: bfloat16 [2, 2048, 128], P('dp', 'ctx')
- kv_weight_grad: float32 [16, 512, 256], P('ctx', 'dp')
Inputs may be any that keep to these rules, and one draw needn't show every extreme that they name: `block_order`: entries 2r and 2r+1 are the blocks stored in rows 2r*64 to 2r*64 + 2*64 - 1; they sum to 31, and every block appears once.
All inputs are finite; a program needn't handle non-finite values.
Results may differ from a plain program's by a relative error of at most 0.012.
Values may be sent and summed in bfloat16 or wider, within the bound.
No kernel may reach another device: no remote copies, remote signals or barrier semaphores. Data moves between devices by JAX's collectives and lax.ppermute only.
A program may use at most 64 MiB of HBM per device.

v0:
```python
import math

import jax
import jax.numpy as jnp
from jax import lax
from jax.sharding import PartitionSpec as P

big_negative = -1e30


def per_device(layer_input, queries, keys, values, d_out, doc_lengths, block_order):
    local_len = queries.shape[1]
    head_dim = keys.shape[2]
    heads = queries.shape[2] // head_dim
    ctx_size = lax.axis_size("ctx")
    seq_len = local_len * ctx_size
    half = local_len // 2
    rank = lax.axis_index("ctx")
    scale = 1.0 / math.sqrt(head_dim)
    key_pos = (block_order[:, None] * half + jnp.arange(half, dtype=jnp.int32)[None, :]).reshape(
        seq_len
    )
    ends = jnp.cumsum(doc_lengths[0])
    key_doc = jnp.sum((key_pos[:, None] >= ends[None, :]).astype(jnp.int32), axis=1)
    query_pos = lax.dynamic_slice_in_dim(key_pos, rank * local_len, local_len)
    query_doc = lax.dynamic_slice_in_dim(key_doc, rank * local_len, local_len)
    local_rows = layer_input[0]
    all_keys, all_values = (
        lax.all_gather(keys[0], "ctx", axis=0, tiled=True),
        lax.all_gather(values[0], "ctx", axis=0, tiled=True),
    )
    block = 512
    nblocks = seq_len // block
    key_blocks = all_keys.reshape(nblocks, block, head_dim)
    value_blocks = all_values.reshape(nblocks, block, head_dim)
    pos_blocks = key_pos.reshape(nblocks, block)
    doc_blocks = key_doc.reshape(nblocks, block)
    q_heads = queries[0].reshape(local_len, heads, head_dim)
    d_heads = d_out[0].reshape(local_len, heads, head_dim)

    def visible(kpos, kdoc):
        return ((kpos[None, :] <= query_pos[:, None]) & (kdoc[None, :] == query_doc[:, None]))[None]

    def scores(kblock):
        return (
            jnp.einsum("thd,kd->htk", q_heads, kblock, preferred_element_type=jnp.float32) * scale
        )

    def prob_grads(vblock):
        return jnp.einsum("thd,kd->htk", d_heads, vblock, preferred_element_type=jnp.float32)

    def stats_step(carry, item):
        run_max, run_sum, run_dot = carry
        kblock, vblock, kpos, kdoc = item
        mask = visible(kpos, kdoc)
        s = scores(kblock)
        new_max = jnp.maximum(run_max, jnp.max(jnp.where(mask, s, big_negative), axis=2))
        terms = jnp.where(mask, jnp.exp(s - new_max[..., None]), 0.0)
        factor = jnp.exp(run_max - new_max)
        run_sum = run_sum * factor + jnp.sum(terms, axis=2)
        run_dot = run_dot * factor + jnp.sum(terms * prob_grads(vblock), axis=2)
        return ((new_max, run_sum, run_dot), None)

    items = (key_blocks, value_blocks, pos_blocks, doc_blocks)
    zeros_stat = jnp.zeros((heads, local_len), jnp.float32)
    start_stats = (jnp.full((heads, local_len), big_negative, jnp.float32), zeros_stat, zeros_stat)
    (run_max, run_sum, run_dot), _ = lax.scan(stats_step, start_stats, items)
    lse = run_max + jnp.log(run_sum)
    delta = run_dot / run_sum

    def grad_step(dq_acc, item):
        kblock, vblock, kpos, kdoc = item
        p = jnp.where(visible(kpos, kdoc), jnp.exp(scores(kblock) - lse[..., None]), 0.0)
        weights = p.astype(jnp.bfloat16)
        dprob = prob_grads(vblock)
        dscore = (p * (dprob - delta[..., None])).astype(jnp.bfloat16)
        dq_acc = dq_acc + jnp.einsum(
            "htk,kd->thd", dscore, kblock, preferred_element_type=jnp.float32
        )
        dk_part = (
            jnp.einsum("htk,thd->kd", dscore, q_heads, preferred_element_type=jnp.float32) * scale
        )
        dv_part = jnp.einsum("htk,thd->kd", weights, d_heads, preferred_element_type=jnp.float32)
        return (dq_acc, jnp.concatenate([dk_part, dv_part], axis=1))

    dq_acc, partials = lax.scan(
        grad_step, jnp.zeros((local_len, heads, head_dim), jnp.float32), items
    )
    owned = lax.psum_scatter(
        partials.reshape(seq_len, 2 * head_dim), "ctx", scatter_dimension=0, tiled=True
    )
    kv_grad = owned.astype(jnp.bfloat16)
    query_grad = (dq_acc * scale).astype(jnp.bfloat16).reshape(1, local_len, heads * head_dim)
    contract = (((0,), (0,)), ((), ()))
    exact = lax.Precision.HIGHEST
    cols = local_rows.astype(jnp.float32)
    term = lax.psum_scatter(
        lax.dot_general(cols, owned, contract, precision=exact, preferred_element_type=jnp.float32),
        "ctx",
        scatter_dimension=0,
        tiled=True,
    )
    weight_grad = lax.psum_scatter(term, "dp", scatter_dimension=0, tiled=True)
    weight_grad = weight_grad * (1.0 / math.sqrt(lax.axis_size("dp") * seq_len))
    key_grad = kv_grad[:, :head_dim].reshape(1, local_len, head_dim)
    value_grad = kv_grad[:, head_dim:].reshape(1, local_len, head_dim)
    return (
        query_grad,
        key_grad,
        value_grad,
        weight_grad.reshape(1, weight_grad.shape[0], 2 * head_dim),
    )


def solution(mesh):
    placed = (
        P("dp", "ctx", None),
        P("dp", "ctx", None),
        P("dp", "ctx", None),
        P("dp", "ctx", None),
        P("dp", "ctx", None),
        P("dp", None),
        P(),
    )
    return jax.shard_map(
        per_device,
        mesh=mesh,
        in_specs=placed,
        out_specs=(
            P("dp", "ctx", None),
            P("dp", "ctx", None),
            P("dp", "ctx", None),
            P("ctx", "dp", None),
        ),
        check_vma=False,
    )
```

profile of v0, /device:TPU:0, one launch (start us, length us, event | category | flops | bytes accessed | tf_op | source)
XLA Modules:
  0.0 304.4 jit_solution(1409123645463635209)
XLA Ops:
  7.3 0.8 broadcast_multiply_fusion
  8.2 0.8 reduce-window.8
  9.6 1.8 copy.30
  11.4 1.1 copy.32
  12.5 1.1 copy.31
  13.9 26.1 %all-gather = bf16[1,2048,128]{2,1,0:T(8,128)(2,1)} all-gather(bf16[1,128,128]{2,1,0:T(8,128)(2,1)S(1)} %copy-done.2), channel_id=2, replica_groups=mesh['dp'=2,'ctx'=16] {'ctx'}, dimensions={1}, use_global_device_ids=true | all-gather | bytes 557056 | tf_op jit(solution)/shard_map/all_gather | solution.py:29
  39.9 20.3 %all-gather.1 = bf16[1,2048,128]{2,1,0:T(8,128)(2,1)} all-gather(bf16[1,128,128]{2,1,0:T(8,128)(2,1)S(1)} %copy-done.3), channel_id=3, replica_groups=mesh['dp'=2,'ctx'=16] {'ctx'}, dimensions={1}, use_global_device_ids=true | all-gather | bytes 557056 | tf_op jit(solution)/shard_map/all_gather | solution.py:30
  60.2 14.7 %while.28 = (s32[]{:T(128)}, f32[8,128]{1,0:T(8,128)S(1)}, f32[8,128]{1,0:T(8,128)S(1)}, f32[8,128]{1,0:T(8,128)S(1)}, s32[4,512]{1,0:T(4,128)S(1)}, /*index=5*/...) while((s32[]{:T(128)}, f32[8,128]{1,0:T(8,128)S(1)}, ...), condition=%wide.region_6.7_spmd.clone, body=%wide.region_2.6_spmd.clone.sunk | while | flops 274930688 | bytes 7427236 | solution.py:67
  60.2 0.2 compare_and_fusion.4
  60.4 1.4 fusion.65
  61.8 1.6 fusion.66
  63.4 0.4 fusion.67
  63.9 0.2 compare_and_fusion.4
  64.1 1.4 fusion.65
  65.5 1.6 fusion.66
  67.1 0.4 fusion.67
  67.6 0.2 compare_and_fusion.4
  67.8 1.4 fusion.65
  69.2 1.6 fusion.66
  70.7 0.4 fusion.67
  71.2 0.2 compare_and_fusion.4
  71.4 1.4 fusion.65
  72.8 1.6 fusion.66
  74.4 0.4 fusion.67
  74.9 33.6 %while.29 = (s32[]{:T(128)}, f32[128,8,128]{0,2,1:T(8,128)}, f32[4,512,256]{2,1,0:T(8,128)}, bf16[4,512,128]{2,1,0:T(8,128)(2,1)}, s32[4,512]{1,0:T(4,128)S(1)},...) while((s32[]{:T(128)}, f32[128,8,128]{0,2,1:T(8,128)}, ...), condition=%wide.region_8.9_spmd.clone, body=%wide.region_7.8_spmd.clone.sunk | while | flops 675414016 | bytes 15750323 | solution.py:86
  74.9 0.2 compare_and_fusion.5
  75.1 1.6 fusion.79
  76.7 0.5 convolution_bitcast_fusion.5
  77.2 1.3 fusion.80
  78.5 1.4 fusion.82
  80.0 2.1 fusion.81
  82.1 0.2 copy.48
  82.3 0.8 constant_dynamic-update-slice_fusion.2
  83.1 0.2 compare_and_fusion.5
  83.4 1.6 fusion.79
  84.9 0.5 convolution_bitcast_fusion.5
  85.4 1.3 fusion.80
  86.8 1.4 fusion.82
  88.2 2.3 fusion.81
  90.7 0.8 constant_dynamic-update-slice_fusion.2
  91.6 0.2 compare_and_fusion.5
  91.8 1.6 fusion.79
  93.4 0.5 convolution_bitcast_fusion.5
  93.9 1.3 fusion.80
  95.2 1.4 fusion.82
  96.6 2.3 fusion.81
  99.2 0.9 constant_dynamic-update-slice_fusion.2
  100.1 0.2 compare_and_fusion.5
  100.3 1.6 fusion.79
  101.8 0.5 convolution_bitcast_fusion.5
  102.3 1.3 fusion.80
  103.7 1.4 fusion.82
  105.1 2.3 fusion.81
  107.4 0.2 copy.48
  107.7 0.9 constant_dynamic-update-slice_fusion.2
  108.6 60.3 %reduce-scatter.4.cloned.1.call-done = f32[128,256]{1,0:T(8,128)} async-done(((f32[2048,256]{1,0:T(8,128)}), f32[128,256]{1,0:T(8,128)}) %reduce-scatter.4.cloned.1.call-update) | async-done | bytes 131088 | tf_op jit(solution)/shard_map/reduce_scatter | solution.py:89
  168.8 6.5 %convolution_bitcast_fusion.3 = f32[8192,256]{0,1:T(8,128)} fusion(f32[128,256]{1,0:T(8,128)} %reduce-scatter.4.cloned.1.call-done, bf16[1,128,8192]{2,1,0:T(8,128)(2,1)S(1)} %copy-done), kind=kOutput, calls=%fused_computation.50 | convolution fusion | flops 3221225472 | bytes 10616832 | tf_op jit(solution)/shard_map/dot_general | solution.py:98
  175.5 103.9 %reduce-scatter.6.cloned.1.call-done = f32[512,256]{0,1:T(8,128)} async-done(((f32[8192,256]{0,1:T(8,128)}), f32[512,256]{0,1:T(8,128)}) %reduce-scatter.6.cloned.1.call-update) | async-done | bytes 524304 | tf_op jit(solution)/shard_map/reduce_scatter | solution.py:97
  279.4 1.1 multiply_convert_fusion
  280.5 0.9 copy.43
  281.4 0.6 slice_bitcast_fusion
  282.0 14.0 %reduce-scatter.8.cloned.1.call-done = f32[256,256]{0,1:T(8,128)} async-done(((f32[512,256]{0,1:T(8,128)}), f32[256,256]{0,1:T(8,128)}) %reduce-scatter.8.cloned.1.call-update) | async-done | bytes 262160 | tf_op jit(solution)/shard_map/reduce_scatter | solution.py:103
  296.1 1.0 multiply_bitcast_fusion
  297.0 0.8 copy.36
  (60 shorter events, 1.8 us)
Async XLA Ops:
  7.2 161.7 %copy-start = (bf16[1,128,8192]{2,1,0:T(8,128)(2,1)S(1)}, bf16[1,128,8192]{2,1,0:T(8,128)(2,1)}, u32[]{:S(2)}) copy-start(bf16[1,128,8192]{2,1,0:T(8,128)(2,1)} %param.11) | copy-start | bytes 6291460
  7.2 6.7 %copy-start.2 = (bf16[1,128,128]{2,1,0:T(8,128)(2,1)S(1)}, bf16[1,128,128]{2,1,0:T(8,128)(2,1)}, u32[]{:S(2)}) copy-start(bf16[1,128,128]{2,1,0:T(8,128)(2,1)} %param.13) | copy-start | bytes 98308
  7.2 32.8 %copy-start.3 = (bf16[1,128,128]{2,1,0:T(8,128)(2,1)S(1)}, bf16[1,128,128]{2,1,0:T(8,128)(2,1)}, u32[]{:S(2)}) copy-start(bf16[1,128,128]{2,1,0:T(8,128)(2,1)} %param.14) | copy-start | bytes 98308
  7.2 161.6 %reduce-scatter.4.cloned.1.call-start = ((), (), s32[]{:S(2)}) async-start(), calls=%async_computation.3 | async-start | bytes 2228224 | tf_op jit(solution)/shard_map/reduce_scatter | solution.py:89
  108.5 170.9 %reduce-scatter.6.cloned.1.call-start = ((), (), s32[]{:S(2)}) async-start(), calls=%async_computation.4 | async-start | bytes 8912896 | tf_op jit(solution)/shard_map/reduce_scatter | solution.py:97
  175.4 106.0 %copy-start.1 = (f32[128,256]{1,0:T(8,128)S(1)}, f32[128,256]{1,0:T(8,128)}, u32[]{:S(2)}) copy-start(f32[128,256]{1,0:T(8,128)} %reduce-scatter.4.cloned.1.call-done) | copy-start | bytes 393220
  175.4 120.6 %reduce-scatter.8.cloned.1.call-start = ((), (), s32[]{:S(2)}) async-start(), calls=%async_computation.5 | async-start | bytes 786432 | tf_op jit(solution)/shard_map/reduce_scatter | solution.py:103
Sparse Core Ops, SparseCore 0:
  108.6 60.1 reduce-scatter.3
  175.5 103.7 reduce-scatter.5
  281.7 14.2 reduce-scatter.7
where the time goes:
time: 305 us; the launch traced here: 304 us
  waiting for transfers between devices  178 us (58%)
  matrix products  46.5 us (15%)
  blocking collectives  46.3 us (15%)
  between operations  13.9 us (5%)
  local copies, waits for them, and re-layouts  11.4 us (4%)
  other arithmetic  7.46 us (2%)
    reduce_scatter x1, waiting for transfers between devices, per_device(): lax.psum_scatter(lax.dot_general(cols, owned, contract, precision=exact,...  104 us
    reduce_scatter x1, waiting for transfers between devices, per_device(): lax.psum_scatter(partials.reshape(seq_len, 2 * head_dim), 'ctx', scatter_...  60.3 us
    all_gather x1, blocking collectives, per_device(): lax.all_gather(keys[0], 'ctx', axis=0, tiled=True)  26.1 us
    all_gather x1, blocking collectives, per_device(): lax.all_gather(values[0], 'ctx', axis=0, tiled=True)  20.3 us
    reduce_scatter x1, waiting for transfers between devices, per_device(): weight_grad = lax.psum_scatter(term, 'dp', scatter_dimension=0, tiled=True)  14 us
    dot_general x8, matrix products, scores(): jnp.einsum('thd,kd->htk', q_heads, kblock, preferred_element_type=jnp.flo...  11.7 us
    dot_general x8, matrix products, prob_grads(): jnp.einsum('thd,kd->htk', d_heads, vblock, preferred_element_type=jnp.flo...  11.6 us
    dot_general x4, matrix products, grad_step(): jnp.einsum('htk,kd->thd', dscore, kblock, preferred_element_type=jnp.floa...  9 us
  transfers between devices with their start and end apart: 3, of which 3 were waited for; matrix products, arithmetic and copies ran while one was open for 1% of the time, Pallas kernels for 0%

commit v1 on v0

v1 whole, which is shorter than its diff:
```python
import functools
import math

import jax
import jax.numpy as jnp
from jax import lax
from jax.experimental import pallas as pl
from jax.experimental.pallas import tpu as pltpu
from jax.sharding import PartitionSpec as P

NEG = -1e30
NT = (((1,), (1,)), ((), ()))
TN = (((0,), (0,)), ((), ()))


def attention_kernel(
    order, lengths, q_ref, d_ref, *refs, n, mid, top, heads, head_dim, half, blocks, window, group
):
    count = 2 * mid
    kv_refs = refs[:count]
    dq_ref = refs[count]
    out_refs = refs[count + 1 : 2 * count + 1]
    kv, kw, acc, inverse = refs[2 * count + 1 :]
    rank = lax.axis_index("ctx")
    rows = 2 * half
    share = top * rows
    for part in range(count):
        kv[part * share : (part + 1) * share, :] = kv_refs[part][...].reshape(share, 2 * head_dim)
    acc[...] = jnp.zeros_like(acc)

    def invert(i, carry):
        rel = jnp.bitwise_xor(i // 2, rank)
        core_rel = rel % 2
        mid_rel = (rel // 2) % mid
        top_rel = rel // (2 * mid)
        inverse[order[i]] = ((core_rel * mid + mid_rel) * top + top_rel) * rows + (i % 2) * half
        return carry

    lax.fori_loop(0, blocks, invert, 0)
    ends = []
    total = 0
    for k in range(lengths.shape[1]):
        total = total + lengths[0, k]
        ends.append(total)
    span = window * half
    scale = 1.0 / math.sqrt(head_dim)
    factor = scale * math.log2(math.e)
    lanes = group * half

    for t in range(2):
        block = order[2 * rank + t]
        first = jnp.clip(block - (window - 1), 0, blocks - window)
        for w in range(window):
            source = pl.multiple_of(inverse[first + w], half)
            kw[w * half : (w + 1) * half, :] = kv[pl.ds(source, half), :]
        k = kw[:, :head_dim]
        v = kw[:, head_dim:]
        kpos = first * half + lax.broadcasted_iota(jnp.int32, (span, lanes), 0)
        qpos = block * half + lax.broadcasted_iota(jnp.int32, (1, lanes), 1) % half
        start = jnp.zeros((1, lanes), jnp.int32)
        for end in ends:
            start = jnp.where(qpos >= end, end, start)
        mask = (kpos <= qpos) & (kpos >= start)
        dk = jnp.zeros((span, head_dim), jnp.float32)
        dv = jnp.zeros((span, head_dim), jnp.float32)
        trows = slice(t * half, (t + 1) * half)
        for g in range(heads // group):
            cols = [slice(h * head_dim, (h + 1) * head_dim) for h in range(g * group, (g + 1) * group)]
            q = jnp.concatenate([q_ref[trows, c] for c in cols], axis=0)
            d = jnp.concatenate([d_ref[trows, c] for c in cols], axis=0)
            s = lax.dot_general(k, q, NT, preferred_element_type=jnp.float32) * factor
            s = jnp.where(mask, s, NEG)
            e = jnp.exp2(s - jnp.max(s, axis=0, keepdims=True))
            inv = 1.0 / jnp.sum(e, axis=0, keepdims=True)
            p = e * inv
            dp = lax.dot_general(v, d, NT, preferred_element_type=jnp.float32)
            delta = jnp.sum(p * dp, axis=0, keepdims=True)
            ds = (p * (dp - delta)).astype(jnp.bfloat16)
            pb = p.astype(jnp.bfloat16)
            dv = dv + jnp.dot(pb, d, preferred_element_type=jnp.float32)
            dk = dk + jnp.dot(ds, q, preferred_element_type=jnp.float32)
            dq = lax.dot_general(k, ds, TN, preferred_element_type=jnp.float32) * scale
            dq = dq.T.astype(jnp.bfloat16)
            for i, c in enumerate(cols):
                dq_ref[trows, c] = dq[i * half : (i + 1) * half, :]
        dk = dk * scale
        for w in range(window):
            target = pl.ds(pl.multiple_of(inverse[first + w], half), half)
            acc[target, :head_dim] += dk[w * half : (w + 1) * half]
            acc[target, head_dim:] += dv[w * half : (w + 1) * half]
    for part in range(count):
        piece = acc[part * share : (part + 1) * share, :]
        out_refs[part][...] = piece.reshape(out_refs[part].shape).astype(out_refs[part].dtype)


def attention(order, lengths, q, d, kv_parts, *, n, mid, top):
    rows, width = q.shape
    head_dim = kv_parts[0].shape[2] // 2
    heads = width // head_dim
    half = rows // 2
    blocks = order.shape[0]
    window = min(blocks, 2 * ((blocks // 4 + 2) // 2))
    count = 2 * mid
    part = (top, rows, 2 * head_dim)
    body = functools.partial(
        attention_kernel,
        n=n,
        mid=mid,
        top=top,
        heads=heads,
        head_dim=head_dim,
        half=half,
        blocks=blocks,
        window=window,
        group=min(heads, 4),
    )
    vmem = pl.BlockSpec(memory_space=pltpu.VMEM)
    smem = pl.BlockSpec(memory_space=pltpu.SMEM)
    elements = 2 * heads * half * window * half
    return pl.pallas_call(
        body,
        out_shape=[jax.ShapeDtypeStruct((rows, width), jnp.bfloat16)]
        + [
            jax.ShapeDtypeStruct(part, jnp.float32 if i == 0 else jnp.bfloat16)
            for i in range(count)
        ],
        in_specs=[smem, smem, vmem, vmem] + [vmem] * count,
        out_specs=[vmem] * (count + 1),
        scratch_shapes=[
            pltpu.VMEM((n * rows, 2 * head_dim), jnp.bfloat16),
            pltpu.VMEM((window * half, 2 * head_dim), jnp.bfloat16),
            pltpu.VMEM((n * rows, 2 * head_dim), jnp.float32),
            pltpu.SMEM((blocks,), jnp.int32),
        ],
        cost_estimate=pl.CostEstimate(
            flops=10 * elements * head_dim, bytes_accessed=4 << 20, transcendentals=elements
        ),
        compiler_params=pltpu.CompilerParams(vmem_limit_bytes=40 << 20),
        name="attention_grads",
    )(order, lengths, q, d, *kv_parts)


def weight_kernel(x_ref, *refs, low):
    g_refs = refs[:low]
    out_refs = refs[low:-1]
    g_all = refs[-1]
    me = lax.axis_index("ctx") % low
    rows = g_refs[0].shape[0]
    for rel in range(low):
        place = pl.multiple_of(jnp.bitwise_xor(me, rel) * rows, rows)
        g_all[pl.ds(place, rows), :] = g_refs[rel][...]
    pieces = len(out_refs)
    height = x_ref.shape[1] // pieces
    for i in range(pieces):
        total = jnp.zeros((height, g_all.shape[1]), jnp.float32)
        for src in range(low):
            total = total + jnp.dot(
                x_ref[src, i * height : (i + 1) * height, :],
                g_all[src * rows : (src + 1) * rows, :],
                preferred_element_type=jnp.float32,
            )
        out_refs[i][...] = total.astype(out_refs[i].dtype)


def weight_terms(x, g_parts, pieces):
    low, height, rows = x.shape
    width = g_parts[0].shape[1]
    vmem = pl.BlockSpec(memory_space=pltpu.VMEM)
    shape = (height // pieces, width)
    return pl.pallas_call(
        functools.partial(weight_kernel, low=low),
        out_shape=[jax.ShapeDtypeStruct(shape, jnp.bfloat16)] * pieces,
        in_specs=[vmem] * (low + 1),
        out_specs=[vmem] * pieces,
        scratch_shapes=[pltpu.VMEM((low * rows, width), jnp.bfloat16)],
        cost_estimate=pl.CostEstimate(
            flops=2 * low * height * rows * width, bytes_accessed=4 << 20, transcendentals=0
        ),
        compiler_params=pltpu.CompilerParams(vmem_limit_bytes=24 << 20),
        name="weight_terms",
    )(x, *g_parts)


def per_device(layer_input, queries, keys, values, d_out, doc_lengths, block_order):
    n = lax.axis_size("ctx")
    dps = lax.axis_size("dp")
    rows = queries.shape[1]
    head_dim = keys.shape[2]
    width = layer_input.shape[2]
    top = 4
    mid = n // (2 * top)
    low = n // 2

    def swap(x, k):
        return lax.ppermute(x, "ctx", [(i, i ^ k) for i in range(n)])

    xt = layer_input[0].T.reshape(2, low, width // n, rows).transpose(1, 0, 2, 3)
    halves = [list(range(low)), list(range(low, n))]
    xt = lax.all_to_all(xt, "ctx", 0, 0, axis_index_groups=halves, tiled=True)
    xt = xt.reshape(low, 2 * (width // n), rows)

    kv = jnp.concatenate([keys[0], values[0]], axis=1)
    base = jnp.stack([kv] + [swap(kv, 2 * mid * j) for j in range(1, top)])
    near = [base] + [swap(base, 2 * j) for j in range(1, mid)]
    far = [swap(part, 1) for part in near]

    dq, *parts = attention(
        block_order, doc_lengths, queries[0], d_out[0], near + far, n=n, mid=mid, top=top
    )

    mine, others = parts[:mid], parts[mid:]
    received = [swap(p, 1) for p in reversed(others)][::-1]
    sends = [
        (mine[j].astype(jnp.float32) + received[j].astype(jnp.float32)).astype(jnp.bfloat16)
        for j in range(1, mid)
    ]
    total = mine[0].astype(jnp.float32) + received[0].astype(jnp.float32)
    for j in range(1, mid):
        total = total + swap(sends[j - 1], 2 * j).astype(jnp.float32)
    grad = total[0]
    for j in range(1, top):
        grad = grad + swap(total[j].astype(jnp.bfloat16), 2 * mid * j).astype(jnp.float32)
    grad16 = grad.astype(jnp.bfloat16)

    even = [grad16] + [swap(grad16, k) for k in range(2, low, 2)]
    gathered = [None] * low
    for i, g in enumerate(even):
        gathered[2 * i] = g
        gathered[2 * i + 1] = swap(g, 1)

    pieces = weight_terms(xt, gathered, 2 * dps)
    rank = lax.axis_index("ctx")
    side, mine_dp = rank // low, lax.axis_index("dp")
    pieces = jnp.stack(pieces).reshape(2, dps, width // n // dps, 2 * head_dim)
    weight = jnp.zeros(pieces.shape[2:], jnp.float32)
    for a in range(2):
        for b in range(dps):
            piece = lax.dynamic_slice(
                pieces, (side ^ a, mine_dp ^ b, 0, 0), (1, 1) + pieces.shape[2:]
            )[0, 0]
            if a or b:
                piece = lax.ppermute(
                    piece,
                    ("dp", "ctx"),
                    [(i * n + j, (i ^ b) * n + (j ^ (a * low))) for i in range(dps) for j in range(n)],
                )
            weight = weight + piece.astype(jnp.float32)
    weight = weight * (1.0 / math.sqrt(dps * rows * n))
    return (
        dq[None],
        grad16[None, :, :head_dim],
        grad16[None, :, head_dim:],
        weight[None],
    )


def solution(mesh):
    placed = (
        P("dp", "ctx", None),
        P("dp", "ctx", None),
        P("dp", "ctx", None),
        P("dp", "ctx", None),
        P("dp", "ctx", None),
        P("dp", None),
        P(),
    )
    return jax.shard_map(
        per_device,
        mesh=mesh,
        in_specs=placed,
        out_specs=(
            P("dp", "ctx", None),
            P("dp", "ctx", None),
            P("dp", "ctx", None),
            P("ctx", "dp", None),
        ),
        check_vma=False,
    )
```

time: 305 us -> 102 us (0.33)
  waiting for transfers between devices: 178 us -> 60.4 us
  matrix products: 46.5 us -> 0 us
  blocking collectives: 46.3 us -> 0 us
  starting transfers between devices: 0.12 us -> 26.3 us
  between operations: 13.9 us -> 0.76 us
  Pallas kernels: 0 us -> 6.6 us
  other arithmetic: 7.46 us -> 1.07 us
  local copies, waits for them, and re-layouts: 11.4 us -> 6.21 us
    reduce_scatter x3 -> x0, waiting for transfers between devices: 178 us -> none  [the longest x1 104 us: per_device(): lax.psum_scatter(lax.dot_general(cols, owned, contract, precision=exact,...]
    ppermute x0 -> x22, waiting for transfers between devices: none -> 60.4 us  [the longest x19 49.7 us: swap(): return lax.ppermute(x, 'ctx', [(i, i ^ k) for i in range(n)])]
    dot_general x29 -> x0, matrix products: 46.5 us -> none  [the longest x8 11.7 us: scores(): jnp.einsum('thd,kd->htk', q_heads, kblock, preferred_element_type=jnp.flo...]
    all_gather x2 -> x0, blocking collectives: 46.3 us -> none  [the longest x1 26.1 us: per_device(): lax.all_gather(keys[0], 'ctx', axis=0, tiled=True)]
    ppermute x0 -> x22, starting transfers between devices: none -> 20.9 us  [the longest x19 16.3 us: swap(): return lax.ppermute(x, 'ctx', [(i, i ^ k) for i in range(n)])]
    pallas_call x0 -> x2, Pallas kernels: none -> 6.6 us  [the longest x1 5.34 us: attention(): pl.pallas_call(body, out_shape=[jax.ShapeDtypeStruct((rows, width), jnp.b...]
    all_to_all x0 -> x1, starting transfers between devices: none -> 5.4 us  [per_device(): xt = lax.all_to_all(xt, 'ctx', 0, 0, axis_index_groups=halves, tiled=True)]
    dynamic_update_slice x8 -> x0, local copies, waits for them, and re-layouts: 4.17 us -> none  [per_device(): lax.scan(grad_step, jnp.zeros((local_len, heads, head_dim), jnp.float32),...]
  transfers between devices with their start and end apart: 3 -> 23, of which waited for: 3 -> 15; matrix products, arithmetic and copies ran while one was open for 1% -> 1% of each run, Pallas kernels for 0% -> 5%
where the time goes in v1:
time: 102 us; the launch traced here: 101 us
  waiting for transfers between devices  60.4 us (59%)
  starting transfers between devices  26.3 us (26%)
  Pallas kernels  6.6 us (6%)
  local copies, waits for them, and re-layouts  6.21 us (6%)
  other arithmetic  1.07 us (1%)
    ppermute x19, waiting for transfers between devices, swap(): return lax.ppermute(x, 'ctx', [(i, i ^ k) for i in range(n)])  49.7 us
    ppermute x19, starting transfers between devices, swap(): return lax.ppermute(x, 'ctx', [(i, i ^ k) for i in range(n)])  16.3 us
    ppermute x3, waiting for transfers between devices, per_device(): lax.ppermute(piece, ('dp', 'ctx'), [(i * n + j, (i ^ b) * n + (j ^ a * lo...  10.7 us
    all_to_all x1, starting transfers between devices, per_device(): xt = lax.all_to_all(xt, 'ctx', 0, 0, axis_index_groups=halves, tiled=True)  5.4 us
    pallas_call x1, Pallas kernels, attention(): pl.pallas_call(body, out_shape=[jax.ShapeDtypeStruct((rows, width), jnp.b...  5.34 us
    ppermute x3, starting transfers between devices, per_device(): lax.ppermute(piece, ('dp', 'ctx'), [(i * n + j, (i ^ b) * n + (j ^ a * lo...  4.59 us
    reshape x1, local copies, waits for them, and re-layouts, per_device(): layer_input[0].T.reshape(2, low, width // n, rows).transpose(1, 0, 2, 3)  3.08 us
    unnamed x13, local copies, waits for them, and re-layouts  2.45 us
  transfers between devices with their start and end apart: 23, of which 15 were waited for; matrix products, arithmetic and copies ran while one was open for 1% of the time, Pallas kernels for 5%

profile of v1, /device:TPU:0, one launch (start us, length us, event | category | flops | bytes accessed | tf_op | source)
XLA Modules:
  0.0 101.4 jit_solution(10911916379038595424)
XLA Ops:
  0.6 2.4 %copy.12 = bf16[16,8,16,512]{3,2,1,0:T(8,128)(2,1)S(1)} copy(bf16[16,8,16,512]{3,1,2,0:T(8,128)(2,1)} %bitcast.65) | data formatting | bytes 4194304
  3.1 3.1 %copy.11 = bf16[2,8,512,128]{3,2,0,1:T(8,128)(2,1)} copy(bf16[2,8,512,128]{2,1,0,3:T(8,128)(2,1)S(1)} %bitcast.64) | data formatting | bytes 4194304 | tf_op jit(solution)/shard_map/reshape | solution.py:197
  6.1 0.0 copy-start.4
  6.1 0.0 copy-start.2
  6.2 0.0 copy-start.3
  6.2 5.4 %all-to-all-start = ((bf16[8,2,512,128]{3,2,1,0:T(8,128)(2,1)}), bf16[8,2,512,128]{3,2,1,0:T(8,128)(2,1)S(1)}, u32[]{:S(2)}, u32[]{:S(2)}) async-start(bf16[8,2,512,128]{3,2,1,0:T(8,128)(2,1)} %bitcast.63), calls=%async_computation | async-start | bytes 4194304 | tf_op jit(solution)/shard_map/all_to_all | solution.py:199
  11.6 0.0 copy-done.4
  11.6 0.0 copy-done.5
  11.6 4.1 %collective-permute-start.2 = (bf16[128,256]{1,0:T(8,128)(2,1)S(1)}, bf16[128,256]{1,0:T(8,128)(2,1)S(1)}, u32[]{:S(2)}, u32[]{:S(2)}) collective-permute-start(bf16[128,256]{1,0:T(8,128)(2,1)S(1)} %get-tuple-element.33), channel_id=1, source_target_pairs={{0,12},{1,13},{2,14},{3,15},{4,8},{5,9},{6,10},{7,11},{8,4},{9,5},... | collective-permute-start | bytes 196616 | tf_op jit(solution)/shard_map/ppermute | solution.py:195
  15.7 0.0 collective-permute-start.1
  15.7 0.6 collective-permute-start
  16.4 24.8 %collective-permute-done.2 = bf16[128,256]{1,0:T(8,128)(2,1)S(1)} collective-permute-done((bf16[128,256]{1,0:T(8,128)(2,1)S(1)}, bf16[128,256]{1,0:T(8,128)(2,1)S(1)}, u32[]{:S(2)}, u32[]{:S(2)}) %collective-permute-start.2) | collective-permute-done | bytes 65568 | tf_op jit(solution)/shard_map/ppermute | solution.py:195
  41.2 0.0 collective-permute-done.1
  41.2 0.3 collective-permute-done
  41.6 1.5 %collective-permute-start.3 = (bf16[4,128,256]{2,1,0:T(8,128)(2,1)S(1)}, bf16[4,128,256]{2,1,0:T(8,128)(2,1)S(1)}, u32[]{:S(2)}, u32[]{:S(2)}) collective-permute-start(bf16[4,128,256]{2,1,0:T(8,128)(2,1)S(1)} %pad_maximum_fusion.1.refs_0_), channel_id=1, source_target_pairs={{0,2},{1,3},{2,0},{3,1},{4,6},{5,7},{6,4},{7,5},{8,10},{9,11},{10,... | collective-permute-start | bytes 786440 | tf_op jit(solution)/shard_map/ppermute | solution.py:195
  43.1 0.0 collective-permute-start.4
  43.1 6.2 %collective-permute-done.3.refs_1_ = bf16[4,128,256]{2,1,0:T(8,128)(2,1)S(1)} collective-permute-done((bf16[4,128,256]{2,1,0:T(8,128)(2,1)S(1)}, bf16[4,128,256]{2,1,0:T(8,128)(2,1)S(1)}, u32[]{:S(2)}, u32[]{:S(2)}) %collective-permute-start.3) | collective-permute-done | bytes 262176 | tf_op jit(solution)/shard_map/ppermute | solution.py:195
  49.3 0.0 collective-permute-start.5
  49.3 0.0 collective-permute-done.4.refs_2_
  49.4 1.5 %collective-permute-done.5.refs_3_ = bf16[4,128,256]{2,1,0:T(8,128)(2,1)S(1)} collective-permute-done((bf16[4,128,256]{2,1,0:T(8,128)(2,1)S(1)}, bf16[4,128,256]{2,1,0:T(8,128)(2,1)S(1)}, u32[]{:S(2)}, u32[]{:S(2)}) %collective-permute-start.5) | collective-permute-done | bytes 262176 | tf_op jit(solution)/shard_map/ppermute | solution.py:195
  50.9 0.0 copy-done
  50.9 0.0 copy-done.1
  50.9 0.0 copy-done.2
  50.9 0.0 copy-done.3
  50.9 5.3 %attention_grads.1 = (bf16[128,1024]{1,0:T(8,128)(2,1)}, f32[4,128,256]{2,1,0:T(8,128)S(1)}, bf16[4,128,256]{2,1,0:T(8,128)(2,1)S(1)}, bf16[4,128,256]{2,1,0:T(8,128)(2,1)S(1)}, bf16[4,128,256]{2,1,0:T(8,128)(2,1)S(1)}) custom-call(s32[32]{0:T(128)S(1)} %copy-done.2, s32[1,8]{1,0:T(1,128)S(1)} %copy-done.3, bf16[128,1024]{1,0:T(8,128)(2,1)S(1)} %bitcast.61, ...), custom_call_target="tpu_custom_call" | custom-call | flops 838860800 | bytes 4194304 | tf_op jit(solution)/shard_map/attention_grads/pallas_call | solution.py:120
  56.2 0.1 collective-permute-start.7
  56.4 0.4 collective-permute-start.6
  56.7 1.0 %collective-permute-done.7 = bf16[4,128,256]{2,1,0:T(8,128)(2,1)S(1)} collective-permute-done((bf16[4,128,256]{2,1,0:T(8,128)(2,1)S(1)}, bf16[4,128,256]{2,1,0:T(8,128)(2,1)S(1)}, u32[]{:S(2)}, u32[]{:S(2)}) %collective-permute-start.7) | collective-permute-done | bytes 262176 | tf_op jit(solution)/shard_map/ppermute | solution.py:195
  57.8 0.1 add_convert_fusion
  57.8 1.5 %collective-permute-start.8 = (bf16[4,128,256]{2,1,0:T(8,128)(2,1)S(1)}, bf16[4,128,256]{2,1,0:T(8,128)(2,1)S(1)}, u32[]{:S(2)}, u32[]{:S(2)}) collective-permute-start(bf16[4,128,256]{2,1,0:T(8,128)(2,1)S(1)} %add_convert_fusion), channel_id=1, source_target_pairs={{0,2},{1,3},{2,0},{3,1},{4,6},{5,7},{6,4},{7,5},{8,10},{9,11},{10,... | collective-permute-start | bytes 786440 | tf_op jit(solution)/shard_map/ppermute | solution.py:195
  59.4 0.0 collective-permute-done.6
  59.4 6.9 %collective-permute-done.8 = bf16[4,128,256]{2,1,0:T(8,128)(2,1)S(1)} collective-permute-done((bf16[4,128,256]{2,1,0:T(8,128)(2,1)S(1)}, bf16[4,128,256]{2,1,0:T(8,128)(2,1)S(1)}, u32[]{:S(2)}, u32[]{:S(2)}) %collective-permute-start.8) | collective-permute-done | bytes 262176 | tf_op jit(solution)/shard_map/ppermute | solution.py:195
  66.3 0.1 fusion.9
  66.4 2.9 %collective-permute-start.11 = (bf16[128,256]{1,0:T(8,128)(2,1)S(1)}, bf16[128,256]{1,0:T(8,128)(2,1)S(1)}, u32[]{:S(2)}, u32[]{:S(2)}) collective-permute-start(bf16[128,256]{1,0:T(8,128)(2,1)S(1)} %get-tuple-element.28), channel_id=1, source_target_pairs={{0,12},{1,13},{2,14},{3,15},{4,8},{5,9},{6,10},{7,11},{8,4},{9,5},... | collective-permute-start | bytes 196616 | tf_op jit(solution)/shard_map/ppermute | solution.py:195
  69.2 0.0 collective-permute-start.10
  69.2 1.6 %collective-permute-start.9 = (bf16[128,256]{1,0:T(8,128)(2,1)S(1)}, bf16[128,256]{1,0:T(8,128)(2,1)S(1)}, u32[]{:S(2)}, u32[]{:S(2)}) collective-permute-start(bf16[128,256]{1,0:T(8,128)(2,1)S(1)} %get-tuple-element.27), channel_id=1, source_target_pairs={{0,4},{1,5},{2,6},{3,7},{4,0},{5,1},{6,2},{7,3},{8,12},{9,13},{10,... | collective-permute-start | bytes 196616 | tf_op jit(solution)/shard_map/ppermute | solution.py:195
  70.8 2.4 %collective-permute-done.11 = bf16[128,256]{1,0:T(8,128)(2,1)S(1)} collective-permute-done((bf16[128,256]{1,0:T(8,128)(2,1)S(1)}, bf16[128,256]{1,0:T(8,128)(2,1)S(1)}, u32[]{:S(2)}, u32[]{:S(2)}) %collective-permute-start.11) | collective-permute-done | bytes 65568 | tf_op jit(solution)/shard_map/ppermute | solution.py:195
  73.2 1.9 %collective-permute-done.10 = bf16[128,256]{1,0:T(8,128)(2,1)S(1)} collective-permute-done((bf16[128,256]{1,0:T(8,128)(2,1)S(1)}, bf16[128,256]{1,0:T(8,128)(2,1)S(1)}, u32[]{:S(2)}, u32[]{:S(2)}) %collective-permute-start.10) | collective-permute-done | bytes 65568 | tf_op jit(solution)/shard_map/ppermute | solution.py:195
  75.1 0.0 collective-permute-done.9
  75.2 1.5 %collective-permute-start.13 = (bf16[128,256]{1,0:T(8,128)(2,1)S(1)}, bf16[128,256]{1,0:T(8,128)(2,1)S(1)}, u32[]{:S(2)}, u32[]{:S(2)}) collective-permute-start(bf16[128,256]{1,0:T(8,128)(2,1)S(1)} %fusion.7.refs_0_), channel_id=1, source_target_pairs={{0,2},{1,3},{2,0},{3,1},{4,6},{5,7},{6,4},{7,5},{8,10},{9,11},{10,... | collective-permute-start | bytes 196616 | tf_op jit(solution)/shard_map/ppermute | solution.py:195
  76.7 0.2 collective-permute-start.15
  76.9 1.9 %collective-permute-start.17 = (bf16[128,256]{1,0:T(8,128)(2,1)S(1)}, bf16[128,256]{1,0:T(8,128)(2,1)S(1)}, u32[]{:S(2)}, u32[]{:S(2)}) collective-permute-start(bf16[128,256]{1,0:T(8,128)(2,1)S(1)} %fusion.7.refs_0_), channel_id=1, source_target_pairs={{0,6},{1,7},{2,4},{3,5},{4,2},{5,3},{6,0},{7,1},{8,14},{9,15},{10,... | collective-permute-start | bytes 196616 | tf_op jit(solution)/shard_map/ppermute | solution.py:195
  78.7 0.0 collective-permute-start.12
  78.7 1.5 %collective-permute-done.13.refs_2_ = bf16[128,256]{1,0:T(8,128)(2,1)S(1)} collective-permute-done((bf16[128,256]{1,0:T(8,128)(2,1)S(1)}, bf16[128,256]{1,0:T(8,128)(2,1)S(1)}, u32[]{:S(2)}, u32[]{:S(2)}) %collective-permute-start.13) | collective-permute-done | bytes 65568 | tf_op jit(solution)/shard_map/ppermute | solution.py:195
  80.2 0.0 collective-permute-start.14
  80.2 0.8 collective-permute-done.15.refs_4_
  81.0 0.0 collective-permute-start.16
  81.0 1.1 %collective-permute-done.17.refs_6_ = bf16[128,256]{1,0:T(8,128)(2,1)S(1)} collective-permute-done((bf16[128,256]{1,0:T(8,128)(2,1)S(1)}, bf16[128,256]{1,0:T(8,128)(2,1)S(1)}, u32[]{:S(2)}, u32[]{:S(2)}) %collective-permute-start.17) | collective-permute-done | bytes 65568 | tf_op jit(solution)/shard_map/ppermute | solution.py:195
  82.0 0.0 collective-permute-start.18
  82.0 0.0 collective-permute-done.12.refs_1_
  82.0 0.0 collective-permute-done.14.refs_3_
  82.1 0.2 collective-permute-done.16.refs_5_
  82.2 1.1 %collective-permute-done.18.refs_7_ = bf16[128,256]{1,0:T(8,128)(2,1)S(1)} collective-permute-done((bf16[128,256]{1,0:T(8,128)(2,1)S(1)}, bf16[128,256]{1,0:T(8,128)(2,1)S(1)}, u32[]{:S(2)}, u32[]{:S(2)}) %collective-permute-start.18) | collective-permute-done | bytes 65568 | tf_op jit(solution)/shard_map/ppermute | solution.py:195
  83.3 0.0 all-to-all-done
  83.3 1.3 %weight_terms.1 = (bf16[256,256]{1,0:T(8,128)(2,1)S(1)}, bf16[256,256]{1,0:T(8,128)(2,1)S(1)}, bf16[256,256]{1,0:T(8,128)(2,1)S(1)}, bf16[256,256]{1,0:T(8,128)(2,1)S(1)}) custom-call(bf16[8,1024,128]{2,1,0:T(8,128)(2,1)S(1)} %bitcast.56, bf16[128,256]{1,0:T(8,128)(2,1)S(1)} %fusion.7.refs_0_, bf16[128,256]{1,0:T(8,128)(2,1)S(1)} %collective-permute-done.12.refs_1_, ...), custom_call_target="tpu_custom_call" | custom-call | flops 536870912 | bytes 4194304 | tf_op jit(solution)/shard_map/weight_terms/pallas_call | solution.py:170
  84.6 0.1 pad_maximum_fusion
  84.7 4.0 %collective-permute-start.21 = (bf16[256,256]{1,0:T(8,128)(2,1)S(1)}, bf16[256,256]{1,0:T(8,128)(2,1)S(1)}, u32[]{:S(2)}, u32[]{:S(2)}) collective-permute-start(bf16[256,256]{1,0:T(8,128)(2,1)S(1)} %get-tuple-element.25), channel_id=1, source_target_pairs={{0,24},{1,25},{2,26},{3,27},{4,28},{5,29},{6,30},{7,31},{8,16},{9,... | collective-permute-start | bytes 393224 | tf_op jit(solution)/shard_map/ppermute | solution.py:242
  88.6 0.0 collective-permute-start.20
  88.7 0.6 collective-permute-start.19
  89.3 0.6 slice_bitcast_fusion.4
  89.9 8.6 %collective-permute-done.21 = bf16[256,256]{1,0:T(8,128)(2,1)S(1)} collective-permute-done((bf16[256,256]{1,0:T(8,128)(2,1)S(1)}, bf16[256,256]{1,0:T(8,128)(2,1)S(1)}, u32[]{:S(2)}, u32[]{:S(2)}) %collective-permute-start.21) | collective-permute-done | bytes 131104 | tf_op jit(solution)/shard_map/ppermute | solution.py:242
  98.6 2.0 %collective-permute-done.20 = bf16[256,256]{1,0:T(8,128)(2,1)S(1)} collective-permute-done((bf16[256,256]{1,0:T(8,128)(2,1)S(1)}, bf16[256,256]{1,0:T(8,128)(2,1)S(1)}, u32[]{:S(2)}, u32[]{:S(2)}) %collective-permute-start.20) | collective-permute-done | bytes 131104 | tf_op jit(solution)/shard_map/ppermute | solution.py:242
  100.6 0.0 collective-permute-done.19
  100.6 0.8 fusion.3
  (8 shorter events, 0.1 us)
Async XLA Ops:
  6.1 5.4 %copy-start.4 = (bf16[1,128,128]{2,1,0:T(8,128)(2,1)S(1)}, bf16[1,128,128]{2,1,0:T(8,128)(2,1)}, u32[]{:S(2)}) copy-start(bf16[1,128,128]{2,1,0:T(8,128)(2,1)} %param.10) | copy-start | bytes 98308
  6.1 5.4 %copy-start.5 = (bf16[1,128,128]{2,1,0:T(8,128)(2,1)S(1)}, bf16[1,128,128]{2,1,0:T(8,128)(2,1)}, u32[]{:S(2)}) copy-start(bf16[1,128,128]{2,1,0:T(8,128)(2,1)} %param.9) | copy-start | bytes 98308
  6.1 44.7 %copy-start = (bf16[1,128,1024]{2,1,0:T(8,128)(2,1)S(1)}, bf16[1,128,1024]{2,1,0:T(8,128)(2,1)}, u32[]{:S(2)}) copy-start(bf16[1,128,1024]{2,1,0:T(8,128)(2,1)} %param.8) | copy-start | bytes 786436
  6.1 44.7 %copy-start.1 = (bf16[1,128,1024]{2,1,0:T(8,128)(2,1)S(1)}, bf16[1,128,1024]{2,1,0:T(8,128)(2,1)}, u32[]{:S(2)}) copy-start(bf16[1,128,1024]{2,1,0:T(8,128)(2,1)} %param.11) | copy-start | bytes 786436
  6.1 44.7 %copy-start.2 = (s32[32]{0:T(128)S(1)}, s32[32]{0:T(128)}, u32[]{:S(2)}) copy-start(s32[32]{0:T(128)} %order.1) | copy-start | bytes 388
  6.2 44.7 %copy-start.3 = (s32[1,8]{1,0:T(1,128)S(1)}, s32[1,8]{1,0:T(1,128)}, u32[]{:S(2)}) copy-start(s32[1,8]{1,0:T(1,128)} %lengths.1) | copy-start | bytes 100
  6.2 77.1 %all-to-all-start = ((bf16[8,2,512,128]{3,2,1,0:T(8,128)(2,1)}), bf16[8,2,512,128]{3,2,1,0:T(8,128)(2,1)S(1)}, u32[]{:S(2)}, u32[]{:S(2)}) async-start(bf16[8,2,512,128]{3,2,1,0:T(8,128)(2,1)} %bitcast.63), calls=%async_computation | async-start | bytes 4194304 | tf_op jit(solution)/shard_map/all_to_all | solution.py:199
  11.6 29.6 %collective-permute-start.2 = (bf16[128,256]{1,0:T(8,128)(2,1)S(1)}, bf16[128,256]{1,0:T(8,128)(2,1)S(1)}, u32[]{:S(2)}, u32[]{:S(2)}) collective-permute-start(bf16[128,256]{1,0:T(8,128)(2,1)S(1)} %get-tuple-element.33), channel_id=1, source_target_pairs={{0,12},{1,13},{2,14},{3,15},{4,8},{5,9},{6,10},{7,11},{8,4},{9,5},... | collective-permute-start | bytes 196616 | tf_op jit(solution)/shard_map/ppermute | solution.py:195
  15.7 25.5 %collective-permute-start.1 = (bf16[128,256]{1,0:T(8,128)(2,1)S(1)}, bf16[128,256]{1,0:T(8,128)(2,1)S(1)}, u32[]{:S(2)}, u32[]{:S(2)}) collective-permute-start(bf16[128,256]{1,0:T(8,128)(2,1)S(1)} %get-tuple-element.33), channel_id=1, source_target_pairs={{0,8},{1,9},{2,10},{3,11},{4,12},{5,13},{6,14},{7,15},{8,0},{9,1},... | collective-permute-start | bytes 196616 | tf_op jit(solution)/shard_map/ppermute | solution.py:195
  15.7 25.8 %collective-permute-start = (bf16[128,256]{1,0:T(8,128)(2,1)S(1)}, bf16[128,256]{1,0:T(8,128)(2,1)S(1)}, u32[]{:S(2)}, u32[]{:S(2)}) collective-permute-start(bf16[128,256]{1,0:T(8,128)(2,1)S(1)} %get-tuple-element.33), channel_id=1, source_target_pairs={{0,4},{1,5},{2,6},{3,7},{4,0},{5,1},{6,2},{7,3},{8,12},{9,13},{10,... | collective-permute-start | bytes 196616 | tf_op jit(solution)/shard_map/ppermute | solution.py:195
  41.6 7.8 %collective-permute-start.3 = (bf16[4,128,256]{2,1,0:T(8,128)(2,1)S(1)}, bf16[4,128,256]{2,1,0:T(8,128)(2,1)S(1)}, u32[]{:S(2)}, u32[]{:S(2)}) collective-permute-start(bf16[4,128,256]{2,1,0:T(8,128)(2,1)S(1)} %pad_maximum_fusion.1.refs_0_), channel_id=1, source_target_pairs={{0,2},{1,3},{2,0},{3,1},{4,6},{5,7},{6,4},{7,5},{8,10},{9,11},{10,... | collective-permute-start | bytes 786440 | tf_op jit(solution)/shard_map/ppermute | solution.py:195
  43.1 6.3 %collective-permute-start.4 = (bf16[4,128,256]{2,1,0:T(8,128)(2,1)S(1)}, bf16[4,128,256]{2,1,0:T(8,128)(2,1)S(1)}, u32[]{:S(2)}, u32[]{:S(2)}) collective-permute-start(bf16[4,128,256]{2,1,0:T(8,128)(2,1)S(1)} %pad_maximum_fusion.1.refs_0_), channel_id=1, source_target_pairs={{0,1},{1,0},{2,3},{3,2},{4,5},{5,4},{6,7},{7,6},{8,9},{9,8},{10,11... | collective-permute-start | bytes 786440 | tf_op jit(solution)/shard_map/ppermute | solution.py:195
  49.3 1.5 %collective-permute-start.5 = (bf16[4,128,256]{2,1,0:T(8,128)(2,1)S(1)}, bf16[4,128,256]{2,1,0:T(8,128)(2,1)S(1)}, u32[]{:S(2)}, u32[]{:S(2)}) collective-permute-start(bf16[4,128,256]{2,1,0:T(8,128)(2,1)S(1)} %collective-permute-done.3.refs_1_), channel_id=1, source_target_pairs={{0,1},{1,0},{2,3},{3,2},{4,5},{5,4},{6,7},{7,6},{8,9},{9,8},{10,11... | collective-permute-start | bytes 786440 | tf_op jit(solution)/shard_map/ppermute | solution.py:195
  56.2 1.5 %collective-permute-start.7 = (bf16[4,128,256]{2,1,0:T(8,128)(2,1)S(1)}, bf16[4,128,256]{2,1,0:T(8,128)(2,1)S(1)}, u32[]{:S(2)}, u32[]{:S(2)}) collective-permute-start(bf16[4,128,256]{2,1,0:T(8,128)(2,1)S(1)} %get-tuple-element.17), channel_id=1, source_target_pairs={{0,1},{1,0},{2,3},{3,2},{4,5},{5,4},{6,7},{7,6},{8,9},{9,8},{10,11... | collective-permute-start | bytes 786440 | tf_op jit(solution)/shard_map/ppermute | solution.py:195
  56.4 3.0 %collective-permute-start.6 = (bf16[4,128,256]{2,1,0:T(8,128)(2,1)S(1)}, bf16[4,128,256]{2,1,0:T(8,128)(2,1)S(1)}, u32[]{:S(2)}, u32[]{:S(2)}) collective-permute-start(bf16[4,128,256]{2,1,0:T(8,128)(2,1)S(1)} %get-tuple-element.15), channel_id=1, source_target_pairs={{0,1},{1,0},{2,3},{3,2},{4,5},{5,4},{6,7},{7,6},{8,9},{9,8},{10,11... | collective-permute-start | bytes 786440 | tf_op jit(solution)/shard_map/ppermute | solution.py:195
  57.8 8.4 %collective-permute-start.8 = (bf16[4,128,256]{2,1,0:T(8,128)(2,1)S(1)}, bf16[4,128,256]{2,1,0:T(8,128)(2,1)S(1)}, u32[]{:S(2)}, u32[]{:S(2)}) collective-permute-start(bf16[4,128,256]{2,1,0:T(8,128)(2,1)S(1)} %add_convert_fusion), channel_id=1, source_target_pairs={{0,2},{1,3},{2,0},{3,1},{4,6},{5,7},{6,4},{7,5},{8,10},{9,11},{10,... | collective-permute-start | bytes 786440 | tf_op jit(solution)/shard_map/ppermute | solution.py:195
  66.4 6.9 %collective-permute-start.11 = (bf16[128,256]{1,0:T(8,128)(2,1)S(1)}, bf16[128,256]{1,0:T(8,128)(2,1)S(1)}, u32[]{:S(2)}, u32[]{:S(2)}) collective-permute-start(bf16[128,256]{1,0:T(8,128)(2,1)S(1)} %get-tuple-element.28), channel_id=1, source_target_pairs={{0,12},{1,13},{2,14},{3,15},{4,8},{5,9},{6,10},{7,11},{8,4},{9,5},... | collective-permute-start | bytes 196616 | tf_op jit(solution)/shard_map/ppermute | solution.py:195
  69.2 5.9 %collective-permute-start.10 = (bf16[128,256]{1,0:T(8,128)(2,1)S(1)}, bf16[128,256]{1,0:T(8,128)(2,1)S(1)}, u32[]{:S(2)}, u32[]{:S(2)}) collective-permute-start(bf16[128,256]{1,0:T(8,128)(2,1)S(1)} %get-tuple-element.29), channel_id=1, source_target_pairs={{0,8},{1,9},{2,10},{3,11},{4,12},{5,13},{6,14},{7,15},{8,0},{9,1},... | collective-permute-start | bytes 196616 | tf_op jit(solution)/shard_map/ppermute | solution.py:195
  69.2 5.9 %collective-permute-start.9 = (bf16[128,256]{1,0:T(8,128)(2,1)S(1)}, bf16[128,256]{1,0:T(8,128)(2,1)S(1)}, u32[]{:S(2)}, u32[]{:S(2)}) collective-permute-start(bf16[128,256]{1,0:T(8,128)(2,1)S(1)} %get-tuple-element.27), channel_id=1, source_target_pairs={{0,4},{1,5},{2,6},{3,7},{4,0},{5,1},{6,2},{7,3},{8,12},{9,13},{10,... | collective-permute-start | bytes 196616 | tf_op jit(solution)/shard_map/ppermute | solution.py:195
  75.2 5.0 %collective-permute-start.13 = (bf16[128,256]{1,0:T(8,128)(2,1)S(1)}, bf16[128,256]{1,0:T(8,128)(2,1)S(1)}, u32[]{:S(2)}, u32[]{:S(2)}) collective-permute-start(bf16[128,256]{1,0:T(8,128)(2,1)S(1)} %fusion.7.refs_0_), channel_id=1, source_target_pairs={{0,2},{1,3},{2,0},{3,1},{4,6},{5,7},{6,4},{7,5},{8,10},{9,11},{10,... | collective-permute-start | bytes 196616 | tf_op jit(solution)/shard_map/ppermute | solution.py:195
  76.7 4.3 %collective-permute-start.15 = (bf16[128,256]{1,0:T(8,128)(2,1)S(1)}, bf16[128,256]{1,0:T(8,128)(2,1)S(1)}, u32[]{:S(2)}, u32[]{:S(2)}) collective-permute-start(bf16[128,256]{1,0:T(8,128)(2,1)S(1)} %fusion.7.refs_0_), channel_id=1, source_target_pairs={{0,4},{1,5},{2,6},{3,7},{4,0},{5,1},{6,2},{7,3},{8,12},{9,13},{10,... | collective-permute-start | bytes 196616 | tf_op jit(solution)/shard_map/ppermute | solution.py:195
  76.9 5.2 %collective-permute-start.17 = (bf16[128,256]{1,0:T(8,128)(2,1)S(1)}, bf16[128,256]{1,0:T(8,128)(2,1)S(1)}, u32[]{:S(2)}, u32[]{:S(2)}) collective-permute-start(bf16[128,256]{1,0:T(8,128)(2,1)S(1)} %fusion.7.refs_0_), channel_id=1, source_target_pairs={{0,6},{1,7},{2,4},{3,5},{4,2},{5,3},{6,0},{7,1},{8,14},{9,15},{10,... | collective-permute-start | bytes 196616 | tf_op jit(solution)/shard_map/ppermute | solution.py:195
  78.7 3.3 %collective-permute-start.12 = (bf16[128,256]{1,0:T(8,128)(2,1)S(1)}, bf16[128,256]{1,0:T(8,128)(2,1)S(1)}, u32[]{:S(2)}, u32[]{:S(2)}) collective-permute-start(bf16[128,256]{1,0:T(8,128)(2,1)S(1)} %fusion.7.refs_0_), channel_id=1, source_target_pairs={{0,1},{1,0},{2,3},{3,2},{4,5},{5,4},{6,7},{7,6},{8,9},{9,8},{10,11... | collective-permute-start | bytes 196616 | tf_op jit(solution)/shard_map/ppermute | solution.py:195
  80.2 1.8 %collective-permute-start.14 = (bf16[128,256]{1,0:T(8,128)(2,1)S(1)}, bf16[128,256]{1,0:T(8,128)(2,1)S(1)}, u32[]{:S(2)}, u32[]{:S(2)}) collective-permute-start(bf16[128,256]{1,0:T(8,128)(2,1)S(1)} %collective-permute-done.13.refs_2_), channel_id=1, source_target_pairs={{0,1},{1,0},{2,3},{3,2},{4,5},{5,4},{6,7},{7,6},{8,9},{9,8},{10,11... | collective-permute-start | bytes 196616 | tf_op jit(solution)/shard_map/ppermute | solution.py:195
  81.0 1.3 %collective-permute-start.16 = (bf16[128,256]{1,0:T(8,128)(2,1)S(1)}, bf16[128,256]{1,0:T(8,128)(2,1)S(1)}, u32[]{:S(2)}, u32[]{:S(2)}) collective-permute-start(bf16[128,256]{1,0:T(8,128)(2,1)S(1)} %collective-permute-done.15.refs_4_), channel_id=1, source_target_pairs={{0,1},{1,0},{2,3},{3,2},{4,5},{5,4},{6,7},{7,6},{8,9},{9,8},{10,11... | collective-permute-start | bytes 196616 | tf_op jit(solution)/shard_map/ppermute | solution.py:195
  82.0 1.3 %collective-permute-start.18 = (bf16[128,256]{1,0:T(8,128)(2,1)S(1)}, bf16[128,256]{1,0:T(8,128)(2,1)S(1)}, u32[]{:S(2)}, u32[]{:S(2)}) collective-permute-start(bf16[128,256]{1,0:T(8,128)(2,1)S(1)} %collective-permute-done.17.refs_6_), channel_id=1, source_target_pairs={{0,1},{1,0},{2,3},{3,2},{4,5},{5,4},{6,7},{7,6},{8,9},{9,8},{10,11... | collective-permute-start | bytes 196616 | tf_op jit(solution)/shard_map/ppermute | solution.py:195
  84.7 13.9 %collective-permute-start.21 = (bf16[256,256]{1,0:T(8,128)(2,1)S(1)}, bf16[256,256]{1,0:T(8,128)(2,1)S(1)}, u32[]{:S(2)}, u32[]{:S(2)}) collective-permute-start(bf16[256,256]{1,0:T(8,128)(2,1)S(1)} %get-tuple-element.25), channel_id=1, source_target_pairs={{0,24},{1,25},{2,26},{3,27},{4,28},{5,29},{6,30},{7,31},{8,16},{9,... | collective-permute-start | bytes 393224 | tf_op jit(solution)/shard_map/ppermute | solution.py:242
  88.6 11.9 %collective-permute-start.20 = (bf16[256,256]{1,0:T(8,128)(2,1)S(1)}, bf16[256,256]{1,0:T(8,128)(2,1)S(1)}, u32[]{:S(2)}, u32[]{:S(2)}) collective-permute-start(bf16[256,256]{1,0:T(8,128)(2,1)S(1)} %get-tuple-element.26), channel_id=1, source_target_pairs={{0,8},{1,9},{2,10},{3,11},{4,12},{5,13},{6,14},{7,15},{8,0},{9,1},... | collective-permute-start | bytes 393224 | tf_op jit(solution)/shard_map/ppermute | solution.py:242
  88.7 11.9 %collective-permute-start.19 = (bf16[256,256]{1,0:T(8,128)(2,1)S(1)}, bf16[256,256]{1,0:T(8,128)(2,1)S(1)}, u32[]{:S(2)}, u32[]{:S(2)}) collective-permute-start(bf16[256,256]{1,0:T(8,128)(2,1)S(1)} %get-tuple-element.24), channel_id=1, source_target_pairs={{0,16},{1,17},{2,18},{3,19},{4,20},{5,21},{6,22},{7,23},{8,24},{9,... | collective-permute-start | bytes 393224 | tf_op jit(solution)/shard_map/ppermute | solution.py:242

commit v2 on v1

--- a/solution.py
+++ b/solution.py
@@ -140,45 +140,60 @@
     )(order, lengths, q, d, *kv_parts)
 
 
-def weight_kernel(x_ref, *refs, low):
-    g_refs = refs[:low]
-    out_refs = refs[low:-1]
+def weight_kernel(x_ref, *refs, members, spread):
+    count = len(members)
+    g_refs = refs[:count]
+    out_refs = refs[count:-1]
     g_all = refs[-1]
-    me = lax.axis_index("ctx") % low
+    my_dp, my_ctx = lax.axis_index("dp"), lax.axis_index("ctx")
+    mine = jnp.int32(0)
+    for place, (i, m) in enumerate(members):
+        hit = (my_dp == i) & ((my_ctx & members[-1][1]) == m)
+        mine = jnp.where(hit, place, mine)
     rows = g_refs[0].shape[0]
-    for rel in range(low):
-        place = pl.multiple_of(jnp.bitwise_xor(me, rel) * rows, rows)
+    for rel in range(count):
+        place = pl.multiple_of(jnp.bitwise_xor(mine, rel) * rows, rows)
         g_all[pl.ds(place, rows), :] = g_refs[rel][...]
     pieces = len(out_refs)
     height = x_ref.shape[1] // pieces
+    me = my_ctx & ~members[-1][1]
     for i in range(pieces):
+        image = jnp.int32(0)
+        for place, s in enumerate(spread):
+            image = jnp.where(jnp.bitwise_xor(me, spread[i]) == s, place, image)
+        begin = pl.multiple_of(image * height, height)
         total = jnp.zeros((height, g_all.shape[1]), jnp.float32)
-        for src in range(low):
+        for src in range(count):
             total = total + jnp.dot(
-                x_ref[src, i * height : (i + 1) * height, :],
+                x_ref[src, pl.ds(begin, height), :],
                 g_all[src * rows : (src + 1) * rows, :],
                 preferred_element_type=jnp.float32,
             )
         out_refs[i][...] = total.astype(out_refs[i].dtype)
 
 
-def weight_terms(x, g_parts, pieces):
-    low, height, rows = x.shape
+def weight_terms(x, g_parts, members, spread):
+    count, height, rows = x.shape
     width = g_parts[0].shape[1]
     vmem = pl.BlockSpec(memory_space=pltpu.VMEM)
+    pieces = len(spread)
     shape = (height // pieces, width)
     return pl.pallas_call(
-        functools.partial(weight_kernel, low=low),
+        functools.partial(weight_kernel, members=members, spread=spread),
         out_shape=[jax.ShapeDtypeStruct(shape, jnp.bfloat16)] * pieces,
-        in_specs=[vmem] * (low + 1),
+        in_specs=[vmem] * (count + 1),
         out_specs=[vmem] * pieces,
-        scratch_shapes=[pltpu.VMEM((low * rows, width), jnp.bfloat16)],
+        scratch_shapes=[pltpu.VMEM((count * rows, width), jnp.bfloat16)],
         cost_estimate=pl.CostEstimate(
-            flops=2 * low * height * rows * width, bytes_accessed=4 << 20, transcendentals=0
+            flops=2 * count * height * rows * width, bytes_accessed=4 << 20, transcendentals=0
         ),
         compiler_params=pltpu.CompilerParams(vmem_limit_bytes=24 << 20),
         name="weight_terms",
     )(x, *g_parts)
+
+
+def after(x, *earlier):
+    return lax.optimization_barrier((x, *earlier))[0]
 
 
 def per_device(layer_input, queries, keys, values, d_out, doc_lengths, block_order):
@@ -189,20 +204,32 @@
     width = layer_input.shape[2]
     top = 4
     mid = n // (2 * top)
-    low = n // 2
 
     def swap(x, k):
         return lax.ppermute(x, "ctx", [(i, i ^ k) for i in range(n)])
 
-    xt = layer_input[0].T.reshape(2, low, width // n, rows).transpose(1, 0, 2, 3)
-    halves = [list(range(low)), list(range(low, n))]
-    xt = lax.all_to_all(xt, "ctx", 0, 0, axis_index_groups=halves, tiled=True)
-    xt = xt.reshape(low, 2 * (width // n), rows)
+    joint = ("dp", "ctx")
+    kept = 5 if n >= 8 else n - 1
+    spread = [m for m in range(n) if not m & kept]
+    members = [(i, m) for i in range(dps) for m in range(n) if not m & ~kept]
+
+    def cross(x, i, m):
+        return lax.ppermute(
+            x, joint, [(a * n + b, (a ^ i) * n + (b ^ m)) for a in range(dps) for b in range(n)]
+        )
 
     kv = jnp.concatenate([keys[0], values[0]], axis=1)
     base = jnp.stack([kv] + [swap(kv, 2 * mid * j) for j in range(1, top)])
     near = [base] + [swap(base, 2 * j) for j in range(1, mid)]
     far = [swap(part, 1) for part in near]
+
+    x = after(layer_input[0], kv)
+    xt = x.T.reshape(n, dps, width // n // dps, rows)
+    xt = jnp.stack([jnp.stack([xt[m | s, i] for s in spread]) for i, m in members])
+    xt = after(xt, base)
+    groups = [[i * n + (m | s) for i, m in members] for s in spread]
+    xt = lax.all_to_all(xt, joint, 0, 0, axis_index_groups=groups, tiled=True)
+    xt = xt.reshape(len(members), -1, rows)
 
     dq, *parts = attention(
         block_order, doc_lengths, queries[0], d_out[0], near + far, n=n, mid=mid, top=top
@@ -222,29 +249,18 @@
         grad = grad + swap(total[j].astype(jnp.bfloat16), 2 * mid * j).astype(jnp.float32)
     grad16 = grad.astype(jnp.bfloat16)
 
-    even = [grad16] + [swap(grad16, k) for k in range(2, low, 2)]
-    gathered = [None] * low
-    for i, g in enumerate(even):
-        gathered[2 * i] = g
-        gathered[2 * i + 1] = swap(g, 1)
-
-    pieces = weight_terms(xt, gathered, 2 * dps)
-    rank = lax.axis_index("ctx")
-    side, mine_dp = rank // low, lax.axis_index("dp")
-    pieces = jnp.stack(pieces).reshape(2, dps, width // n // dps, 2 * head_dim)
-    weight = jnp.zeros(pieces.shape[2:], jnp.float32)
-    for a in range(2):
-        for b in range(dps):
-            piece = lax.dynamic_slice(
-                pieces, (side ^ a, mine_dp ^ b, 0, 0), (1, 1) + pieces.shape[2:]
-            )[0, 0]
-            if a or b:
-                piece = lax.ppermute(
-                    piece,
-                    ("dp", "ctx"),
-                    [(i * n + j, (i ^ b) * n + (j ^ (a * low))) for i in range(dps) for j in range(n)],
-                )
-            weight = weight + piece.astype(jnp.float32)
+    gathered = {}
+    for i, m in members:
+        if not m & 1:
+            gathered[i, m] = cross(grad16, i, m) if i or m else grad16
+    for i, m in members:
+        if m & 1:
+            gathered[i, m] = swap(gathered[i, m ^ 1], 1)
+
+    pieces = weight_terms(xt, [gathered[k] for k in members], members, spread)
+    weight = pieces[0].astype(jnp.float32)
+    for s, piece in zip(spread[1:], pieces[1:]):
+        weight = weight + swap(piece, s).astype(jnp.float32)
     weight = weight * (1.0 / math.sqrt(dps * rows * n))
     return (
         dq[None],

time: 102 us -> 78.7 us (0.77)
  waiting for transfers between devices: 60.4 us -> 39.5 us
  local copies, waits for them, and re-layouts: 6.21 us -> 4.06 us
    ppermute x19, waiting for transfers between devices: 49.7 us -> 35.9 us  [swap(): return lax.ppermute(x, 'ctx', [(i, i ^ k) for i in range(n)])]
    ppermute x3, waiting for transfers between devices: 10.7 us -> 3.63 us  [cross(): lax.ppermute(x, joint, [(a * n + b, (a ^ i) * n + (b ^ m)) for a in range...]
    unnamed x13 -> x10, local copies, waits for them, and re-layouts: 2.45 us -> 0.03 us
    all_to_all x1, starting transfers between devices: 5.4 us -> 3.75 us  [per_device(): xt = lax.all_to_all(xt, joint, 0, 0, axis_index_groups=groups, tiled=True)]
    ppermute x19, starting transfers between devices: 16.3 us -> 18 us  [swap(): return lax.ppermute(x, 'ctx', [(i, i ^ k) for i in range(n)])]
    ppermute x3, starting transfers between devices: 4.59 us -> 3.55 us  [cross(): lax.ppermute(x, joint, [(a * n + b, (a ^ i) * n + (b ^ m)) for a in range...]
  transfers between devices with their start and end apart: 23 -> 23, of which waited for: 15 -> 16; matrix products, arithmetic and copies ran while one was open for 1% -> 6% of each run, Pallas kernels for 5% -> 7%
where the time goes in v2:
time: 78.7 us; the launch traced here: 78.4 us
  waiting for transfers between devices  39.5 us (50%)
  starting transfers between devices  25.3 us (32%)
  Pallas kernels  6.6 us (8%)
  local copies, waits for them, and re-layouts  4.06 us (5%)
  other arithmetic  2.06 us (3%)
  between operations  0.85 us (1%)
    ppermute x19, waiting for transfers between devices, swap(): return lax.ppermute(x, 'ctx', [(i, i ^ k) for i in range(n)])  35.9 us
    ppermute x19, starting transfers between devices, swap(): return lax.ppermute(x, 'ctx', [(i, i ^ k) for i in range(n)])  18 us
    pallas_call x1, Pallas kernels, attention(): pl.pallas_call(body, out_shape=[jax.ShapeDtypeStruct((rows, width), jnp.b...  5.34 us
    all_to_all x1, starting transfers between devices, per_device(): xt = lax.all_to_all(xt, joint, 0, 0, axis_index_groups=groups, tiled=True)  3.75 us
    ppermute x3, waiting for transfers between devices, cross(): lax.ppermute(x, joint, [(a * n + b, (a ^ i) * n + (b ^ m)) for a in range...  3.63 us
    ppermute x3, starting transfers between devices, cross(): lax.ppermute(x, joint, [(a * n + b, (a ^ i) * n + (b ^ m)) for a in range...  3.55 us
    reshape x1, local copies, waits for them, and re-layouts, per_device(): xt = x.T.reshape(n, dps, width // n // dps, rows)  3.22 us
  transfers between devices with their start and end apart: 23, of which 16 were waited for; matrix products, arithmetic and copies ran while one was open for 6% of the time, Pallas kernels for 7%

profile of v2, /device:TPU:0, one launch (start us, length us, event | category | flops | bytes accessed | tf_op | source)
XLA Modules:
  0.0 78.4 jit_solution(11072705857671435126)
XLA Ops:
  0.6 0.8 %fusion.12 = (bf16[1,128,256]{2,1,0:T(8,128)(2,1)S(1)}, bf16[128,256]{1,0:T(8,128)(2,1)S(1)}) fusion(bf16[128,128]{1,0:T(8,128)(2,1)} %bitcast.141, bf16[128,128]{1,0:T(8,128)(2,1)} %bitcast.142), kind=kLoop, calls=%fused_computation.63 | loop fusion | flops 131072 | bytes 196608 | tf_op jit(solution)/shard_map/stack | solution.py:222
  1.4 3.1 %collective-permute-start = (bf16[128,256]{1,0:T(8,128)(2,1)S(1)}, bf16[128,256]{1,0:T(8,128)(2,1)S(1)}, u32[]{:S(2)}, u32[]{:S(2)}) collective-permute-start(bf16[128,256]{1,0:T(8,128)(2,1)S(1)} %get-tuple-element.66), channel_id=1, source_target_pairs={{0,4},{1,5},{2,6},{3,7},{4,0},{5,1},{6,2},{7,3},{8,12},{9,13},{10,... | collective-permute-start | bytes 196616 | tf_op jit(solution)/shard_map/ppermute | solution.py:209
  4.5 2.6 %collective-permute-start.1 = (bf16[128,256]{1,0:T(8,128)(2,1)S(1)}, bf16[128,256]{1,0:T(8,128)(2,1)S(1)}, u32[]{:S(2)}, u32[]{:S(2)}) collective-permute-start(bf16[128,256]{1,0:T(8,128)(2,1)S(1)} %get-tuple-element.66), channel_id=1, source_target_pairs={{0,8},{1,9},{2,10},{3,11},{4,12},{5,13},{6,14},{7,15},{8,0},{9,1},... | collective-permute-start | bytes 196616 | tf_op jit(solution)/shard_map/ppermute | solution.py:209
  7.1 0.0 collective-permute-start.2
  7.1 3.2 %copy.43 = bf16[8192,128]{1,0:T(8,128)(2,1)S(1)} copy(bf16[8192,128]{0,1:T(8,128)(2,1)} %bitcast.137) | data formatting | bytes 4194304 | tf_op jit(solution)/shard_map/reshape | solution.py:227
  10.3 0.1 slice_bitcast_fusion.20
  10.4 0.1 slice_bitcast_fusion.4
  10.9 0.0 copy-start.4
  10.9 0.0 collective-permute-done
  10.9 0.9 %collective-permute-done.1 = bf16[128,256]{1,0:T(8,128)(2,1)S(1)} collective-permute-done((bf16[128,256]{1,0:T(8,128)(2,1)S(1)}, bf16[128,256]{1,0:T(8,128)(2,1)S(1)}, u32[]{:S(2)}, u32[]{:S(2)}) %collective-permute-start.1) | collective-permute-done | bytes 65568 | tf_op jit(solution)/shard_map/ppermute | solution.py:209
  11.8 1.4 %collective-permute-done.2 = bf16[128,256]{1,0:T(8,128)(2,1)S(1)} collective-permute-done((bf16[128,256]{1,0:T(8,128)(2,1)S(1)}, bf16[128,256]{1,0:T(8,128)(2,1)S(1)}, u32[]{:S(2)}, u32[]{:S(2)}) %collective-permute-start.2) | collective-permute-done | bytes 65568 | tf_op jit(solution)/shard_map/ppermute | solution.py:209
  13.2 0.0 copy-done.4
  13.2 0.0 copy-start
  13.2 0.0 copy-start.1
  13.2 0.0 copy-start.2
  13.3 0.0 copy-start.3
  13.3 3.7 %all-to-all-start = ((bf16[8,4,256,128]{3,2,1,0:T(8,128)(2,1)}), bf16[8,4,256,128]{3,2,1,0:T(8,128)(2,1)S(1)}, u32[]{:S(2)}, u32[]{:S(2)}) async-start(bf16[8,4,256,128]{3,2,1,0:T(8,128)(2,1)} %copy-done.4), calls=%async_computation | async-start | bytes 4194304 | tf_op jit(solution)/shard_map/all_to_all | solution.py:231
  17.0 1.6 %collective-permute-start.3 = (bf16[4,128,256]{2,1,0:T(8,128)(2,1)S(1)}, bf16[4,128,256]{2,1,0:T(8,128)(2,1)S(1)}, u32[]{:S(2)}, u32[]{:S(2)}) collective-permute-start(bf16[4,128,256]{2,1,0:T(8,128)(2,1)S(1)} %pad_maximum_fusion.refs_0_), channel_id=1, source_target_pairs={{0,2},{1,3},{2,0},{3,1},{4,6},{5,7},{6,4},{7,5},{8,10},{9,11},{10,... | collective-permute-start | bytes 786440 | tf_op jit(solution)/shard_map/ppermute | solution.py:209
  18.6 0.1 collective-permute-start.4
  18.7 7.0 %collective-permute-done.3.refs_1_ = bf16[4,128,256]{2,1,0:T(8,128)(2,1)S(1)} collective-permute-done((bf16[4,128,256]{2,1,0:T(8,128)(2,1)S(1)}, bf16[4,128,256]{2,1,0:T(8,128)(2,1)S(1)}, u32[]{:S(2)}, u32[]{:S(2)}) %collective-permute-start.3) | collective-permute-done | bytes 262176 | tf_op jit(solution)/shard_map/ppermute | solution.py:209
  25.6 0.0 collective-permute-start.5
  25.6 0.0 collective-permute-done.4.refs_2_
  25.6 1.5 %collective-permute-done.5.refs_3_ = bf16[4,128,256]{2,1,0:T(8,128)(2,1)S(1)} collective-permute-done((bf16[4,128,256]{2,1,0:T(8,128)(2,1)S(1)}, bf16[4,128,256]{2,1,0:T(8,128)(2,1)S(1)}, u32[]{:S(2)}, u32[]{:S(2)}) %collective-permute-start.5) | collective-permute-done | bytes 262176 | tf_op jit(solution)/shard_map/ppermute | solution.py:209
  27.2 0.0 copy-done
  27.2 0.0 copy-done.1
  27.2 5.3 %attention_grads.1 = (bf16[128,1024]{1,0:T(8,128)(2,1)}, f32[4,128,256]{2,1,0:T(8,128)S(1)}, bf16[4,128,256]{2,1,0:T(8,128)(2,1)S(1)}, bf16[4,128,256]{2,1,0:T(8,128)(2,1)S(1)}, bf16[4,128,256]{2,1,0:T(8,128)(2,1)S(1)}) custom-call(s32[32]{0:T(128)S(1)} %copy-done.2, s32[1,8]{1,0:T(1,128)S(1)} %copy-done.3, bf16[128,1024]{1,0:T(8,128)(2,1)S(1)} %bitcast.133, ...), custom_call_target="tpu_custom_call" | custom-call | flops 838860800 | bytes 4194304 | tf_op jit(solution)/shard_map/attention_grads/pallas_call | solution.py:120
  32.5 0.1 collective-permute-start.7
  32.7 0.4 collective-permute-start.6
  33.0 1.0 %collective-permute-done.7 = bf16[4,128,256]{2,1,0:T(8,128)(2,1)S(1)} collective-permute-done((bf16[4,128,256]{2,1,0:T(8,128)(2,1)S(1)}, bf16[4,128,256]{2,1,0:T(8,128)(2,1)S(1)}, u32[]{:S(2)}, u32[]{:S(2)}) %collective-permute-start.7) | collective-permute-done | bytes 262176 | tf_op jit(solution)/shard_map/ppermute | solution.py:209
  34.1 0.1 add_convert_fusion
  34.1 1.6 %collective-permute-start.8 = (bf16[4,128,256]{2,1,0:T(8,128)(2,1)S(1)}, bf16[4,128,256]{2,1,0:T(8,128)(2,1)S(1)}, u32[]{:S(2)}, u32[]{:S(2)}) collective-permute-start(bf16[4,128,256]{2,1,0:T(8,128)(2,1)S(1)} %add_convert_fusion), channel_id=1, source_target_pairs={{0,2},{1,3},{2,0},{3,1},{4,6},{5,7},{6,4},{7,5},{8,10},{9,11},{10,... | collective-permute-start | bytes 786440 | tf_op jit(solution)/shard_map/ppermute | solution.py:209
  35.7 0.0 collective-permute-done.6
  35.7 6.8 %collective-permute-done.8 = bf16[4,128,256]{2,1,0:T(8,128)(2,1)S(1)} collective-permute-done((bf16[4,128,256]{2,1,0:T(8,128)(2,1)S(1)}, bf16[4,128,256]{2,1,0:T(8,128)(2,1)S(1)}, u32[]{:S(2)}, u32[]{:S(2)}) %collective-permute-start.8) | collective-permute-done | bytes 262176 | tf_op jit(solution)/shard_map/ppermute | solution.py:209
  42.5 0.1 fusion.13
  42.7 2.2 %collective-permute-start.10 = (bf16[128,256]{1,0:T(8,128)(2,1)S(1)}, bf16[128,256]{1,0:T(8,128)(2,1)S(1)}, u32[]{:S(2)}, u32[]{:S(2)}) collective-permute-start(bf16[128,256]{1,0:T(8,128)(2,1)S(1)} %get-tuple-element.62), channel_id=1, source_target_pairs={{0,8},{1,9},{2,10},{3,11},{4,12},{5,13},{6,14},{7,15},{8,0},{9,1},... | collective-permute-start | bytes 196616 | tf_op jit(solution)/shard_map/ppermute | solution.py:209
  44.8 1.9 %collective-permute-start.11 = (bf16[128,256]{1,0:T(8,128)(2,1)S(1)}, bf16[128,256]{1,0:T(8,128)(2,1)S(1)}, u32[]{:S(2)}, u32[]{:S(2)}) collective-permute-start(bf16[128,256]{1,0:T(8,128)(2,1)S(1)} %get-tuple-element.61), channel_id=1, source_target_pairs={{0,12},{1,13},{2,14},{3,15},{4,8},{5,9},{6,10},{7,11},{8,4},{9,5},... | collective-permute-start | bytes 196616 | tf_op jit(solution)/shard_map/ppermute | solution.py:209
  46.8 0.0 collective-permute-start.9
  46.8 3.2 %collective-permute-done.10 = bf16[128,256]{1,0:T(8,128)(2,1)S(1)} collective-permute-done((bf16[128,256]{1,0:T(8,128)(2,1)S(1)}, bf16[128,256]{1,0:T(8,128)(2,1)S(1)}, u32[]{:S(2)}, u32[]{:S(2)}) %collective-permute-start.10) | collective-permute-done | bytes 65568 | tf_op jit(solution)/shard_map/ppermute | solution.py:209
  49.9 1.3 %collective-permute-done.11 = bf16[128,256]{1,0:T(8,128)(2,1)S(1)} collective-permute-done((bf16[128,256]{1,0:T(8,128)(2,1)S(1)}, bf16[128,256]{1,0:T(8,128)(2,1)S(1)}, u32[]{:S(2)}, u32[]{:S(2)}) %collective-permute-start.11) | collective-permute-done | bytes 65568 | tf_op jit(solution)/shard_map/ppermute | solution.py:209
  51.2 0.4 collective-permute-done.9
  51.7 0.5 collective-permute-start.13
  52.2 1.5 %collective-permute-start.15 = (bf16[128,256]{1,0:T(8,128)(2,1)S(1)}, bf16[128,256]{1,0:T(8,128)(2,1)S(1)}, u32[]{:S(2)}, u32[]{:S(2)}) collective-permute-start(bf16[128,256]{1,0:T(8,128)(2,1)S(1)} %fusion.11.refs_0_), channel_id=1, source_target_pairs={{0,16},{1,17},{2,18},{3,19},{4,20},{5,21},{6,22},{7,23},{8,24},{9,... | collective-permute-start | bytes 196616 | tf_op jit(solution)/shard_map/ppermute | solution.py:217
  53.8 1.5 %collective-permute-start.17 = (bf16[128,256]{1,0:T(8,128)(2,1)S(1)}, bf16[128,256]{1,0:T(8,128)(2,1)S(1)}, u32[]{:S(2)}, u32[]{:S(2)}) collective-permute-start(bf16[128,256]{1,0:T(8,128)(2,1)S(1)} %fusion.11.refs_0_), channel_id=1, source_target_pairs={{0,20},{1,21},{2,22},{3,23},{4,16},{5,17},{6,18},{7,19},{8,28},{9,... | collective-permute-start | bytes 196616 | tf_op jit(solution)/shard_map/ppermute | solution.py:217
  55.3 0.0 collective-permute-start.12
  55.3 0.9 %collective-permute-done.13.refs_2_ = bf16[128,256]{1,0:T(8,128)(2,1)S(1)} collective-permute-done((bf16[128,256]{1,0:T(8,128)(2,1)S(1)}, bf16[128,256]{1,0:T(8,128)(2,1)S(1)}, u32[]{:S(2)}, u32[]{:S(2)}) %collective-permute-start.13) | collective-permute-done | bytes 65568 | tf_op jit(solution)/shard_map/ppermute | solution.py:217
  56.1 0.0 collective-permute-start.14
  56.1 0.8 %collective-permute-done.15.refs_4_ = bf16[128,256]{1,0:T(8,128)(2,1)S(1)} collective-permute-done((bf16[128,256]{1,0:T(8,128)(2,1)S(1)}, bf16[128,256]{1,0:T(8,128)(2,1)S(1)}, u32[]{:S(2)}, u32[]{:S(2)}) %collective-permute-start.15) | collective-permute-done | bytes 65568 | tf_op jit(solution)/shard_map/ppermute | solution.py:217
  56.9 0.0 collective-permute-start.16
  56.9 2.0 %collective-permute-done.17.refs_6_ = bf16[128,256]{1,0:T(8,128)(2,1)S(1)} collective-permute-done((bf16[128,256]{1,0:T(8,128)(2,1)S(1)}, bf16[128,256]{1,0:T(8,128)(2,1)S(1)}, u32[]{:S(2)}, u32[]{:S(2)}) %collective-permute-start.17) | collective-permute-done | bytes 65568 | tf_op jit(solution)/shard_map/ppermute | solution.py:217
  58.9 0.0 collective-permute-start.18
  58.9 0.0 collective-permute-done.12.refs_1_
  58.9 0.0 collective-permute-done.14.refs_3_
  58.9 0.0 collective-permute-done.16.refs_5_
  58.9 1.2 %collective-permute-done.18.refs_7_ = bf16[128,256]{1,0:T(8,128)(2,1)S(1)} collective-permute-done((bf16[128,256]{1,0:T(8,128)(2,1)S(1)}, bf16[128,256]{1,0:T(8,128)(2,1)S(1)}, u32[]{:S(2)}, u32[]{:S(2)}) %collective-permute-start.18) | collective-permute-done | bytes 65568 | tf_op jit(solution)/shard_map/ppermute | solution.py:209
  60.2 0.0 all-to-all-done
  60.2 1.3 %weight_terms.1 = (bf16[256,256]{1,0:T(8,128)(2,1)S(1)}, bf16[256,256]{1,0:T(8,128)(2,1)S(1)}, bf16[256,256]{1,0:T(8,128)(2,1)S(1)}, bf16[256,256]{1,0:T(8,128)(2,1)S(1)}) custom-call(bf16[8,1024,128]{2,1,0:T(8,128)(2,1)S(1)} %bitcast.132, bf16[128,256]{1,0:T(8,128)(2,1)S(1)} %fusion.11.refs_0_, bf16[128,256]{1,0:T(8,128)(2,1)S(1)} %collective-permute-done.12.refs_1_, ...), custom_call_target="tpu_custom_call" | custom-call | flops 536870912 | bytes 4194304 | tf_op jit(solution)/shard_map/weight_terms/pallas_call | solution.py:181
  61.5 1.6 %collective-permute-start.19 = (bf16[256,256]{1,0:T(8,128)(2,1)S(1)}, bf16[256,256]{1,0:T(8,128)(2,1)S(1)}, u32[]{:S(2)}, u32[]{:S(2)}) collective-permute-start(bf16[256,256]{1,0:T(8,128)(2,1)S(1)} %get-tuple-element.23), channel_id=1, source_target_pairs={{0,2},{1,3},{2,0},{3,1},{4,6},{5,7},{6,4},{7,5},{8,10},{9,11},{10,... | collective-permute-start | bytes 393224 | tf_op jit(solution)/shard_map/ppermute | solution.py:209
  63.0 2.5 %collective-permute-start.20 = (bf16[256,256]{1,0:T(8,128)(2,1)S(1)}, bf16[256,256]{1,0:T(8,128)(2,1)S(1)}, u32[]{:S(2)}, u32[]{:S(2)}) collective-permute-start(bf16[256,256]{1,0:T(8,128)(2,1)S(1)} %get-tuple-element.24), channel_id=1, source_target_pairs={{0,8},{1,9},{2,10},{3,11},{4,12},{5,13},{6,14},{7,15},{8,0},{9,1},... | collective-permute-start | bytes 393224 | tf_op jit(solution)/shard_map/ppermute | solution.py:209
  65.6 0.3 collective-permute-start.21
  65.9 0.6 slice_bitcast_fusion.36
  66.5 0.5 collective-permute-done.19
  67.1 8.8 %collective-permute-done.20 = bf16[256,256]{1,0:T(8,128)(2,1)S(1)} collective-permute-done((bf16[256,256]{1,0:T(8,128)(2,1)S(1)}, bf16[256,256]{1,0:T(8,128)(2,1)S(1)}, u32[]{:S(2)}, u32[]{:S(2)}) %collective-permute-start.20) | collective-permute-done | bytes 131104 | tf_op jit(solution)/shard_map/ppermute | solution.py:209
  75.9 1.7 %collective-permute-done.21 = bf16[256,256]{1,0:T(8,128)(2,1)S(1)} collective-permute-done((bf16[256,256]{1,0:T(8,128)(2,1)S(1)}, bf16[256,256]{1,0:T(8,128)(2,1)S(1)}, u32[]{:S(2)}, u32[]{:S(2)}) %collective-permute-start.21) | collective-permute-done | bytes 131104 | tf_op jit(solution)/shard_map/ppermute | solution.py:209
  77.6 0.8 multiply_bitcast_fusion
  (13 shorter events, 0.4 us)
Async XLA Ops:
  1.4 9.4 %collective-permute-start = (bf16[128,256]{1,0:T(8,128)(2,1)S(1)}, bf16[128,256]{1,0:T(8,128)(2,1)S(1)}, u32[]{:S(2)}, u32[]{:S(2)}) collective-permute-start(bf16[128,256]{1,0:T(8,128)(2,1)S(1)} %get-tuple-element.66), channel_id=1, source_target_pairs={{0,4},{1,5},{2,6},{3,7},{4,0},{5,1},{6,2},{7,3},{8,12},{9,13},{10,... | collective-permute-start | bytes 196616 | tf_op jit(solution)/shard_map/ppermute | solution.py:209
  4.5 7.3 %collective-permute-start.1 = (bf16[128,256]{1,0:T(8,128)(2,1)S(1)}, bf16[128,256]{1,0:T(8,128)(2,1)S(1)}, u32[]{:S(2)}, u32[]{:S(2)}) collective-permute-start(bf16[128,256]{1,0:T(8,128)(2,1)S(1)} %get-tuple-element.66), channel_id=1, source_target_pairs={{0,8},{1,9},{2,10},{3,11},{4,12},{5,13},{6,14},{7,15},{8,0},{9,1},... | collective-permute-start | bytes 196616 | tf_op jit(solution)/shard_map/ppermute | solution.py:209
  7.1 6.1 %collective-permute-start.2 = (bf16[128,256]{1,0:T(8,128)(2,1)S(1)}, bf16[128,256]{1,0:T(8,128)(2,1)S(1)}, u32[]{:S(2)}, u32[]{:S(2)}) collective-permute-start(bf16[128,256]{1,0:T(8,128)(2,1)S(1)} %get-tuple-element.66), channel_id=1, source_target_pairs={{0,12},{1,13},{2,14},{3,15},{4,8},{5,9},{6,10},{7,11},{8,4},{9,5},... | collective-permute-start | bytes 196616 | tf_op jit(solution)/shard_map/ppermute | solution.py:209
  10.9 2.3 %copy-start.4 = (bf16[8,4,256,128]{3,2,1,0:T(8,128)(2,1)}, bf16[8,4,256,128]{3,2,1,0:T(8,128)(2,1)S(1)}, u32[]{:S(2)}) copy-start(bf16[8,4,256,128]{3,2,1,0:T(8,128)(2,1)S(1)} %fusion.7) | copy-start | bytes 6291460
  13.2 14.0 %copy-start = (bf16[1,128,1024]{2,1,0:T(8,128)(2,1)S(1)}, bf16[1,128,1024]{2,1,0:T(8,128)(2,1)}, u32[]{:S(2)}) copy-start(bf16[1,128,1024]{2,1,0:T(8,128)(2,1)} %param.8) | copy-start | bytes 786436
  13.2 13.9 %copy-start.1 = (bf16[1,128,1024]{2,1,0:T(8,128)(2,1)S(1)}, bf16[1,128,1024]{2,1,0:T(8,128)(2,1)}, u32[]{:S(2)}) copy-start(bf16[1,128,1024]{2,1,0:T(8,128)(2,1)} %param.11) | copy-start | bytes 786436
  13.2 13.9 %copy-start.2 = (s32[32]{0:T(128)S(1)}, s32[32]{0:T(128)}, u32[]{:S(2)}) copy-start(s32[32]{0:T(128)} %order.1) | copy-start | bytes 388
  13.3 13.9 %copy-start.3 = (s32[1,8]{1,0:T(1,128)S(1)}, s32[1,8]{1,0:T(1,128)}, u32[]{:S(2)}) copy-start(s32[1,8]{1,0:T(1,128)} %lengths.1) | copy-start | bytes 100
  13.3 46.9 %all-to-all-start = ((bf16[8,4,256,128]{3,2,1,0:T(8,128)(2,1)}), bf16[8,4,256,128]{3,2,1,0:T(8,128)(2,1)S(1)}, u32[]{:S(2)}, u32[]{:S(2)}) async-start(bf16[8,4,256,128]{3,2,1,0:T(8,128)(2,1)} %copy-done.4), calls=%async_computation | async-start | bytes 4194304 | tf_op jit(solution)/shard_map/all_to_all | solution.py:231
  17.0 8.6 %collective-permute-start.3 = (bf16[4,128,256]{2,1,0:T(8,128)(2,1)S(1)}, bf16[4,128,256]{2,1,0:T(8,128)(2,1)S(1)}, u32[]{:S(2)}, u32[]{:S(2)}) collective-permute-start(bf16[4,128,256]{2,1,0:T(8,128)(2,1)S(1)} %pad_maximum_fusion.refs_0_), channel_id=1, source_target_pairs={{0,2},{1,3},{2,0},{3,1},{4,6},{5,7},{6,4},{7,5},{8,10},{9,11},{10,... | collective-permute-start | bytes 786440 | tf_op jit(solution)/shard_map/ppermute | solution.py:209
  18.6 7.0 %collective-permute-start.4 = (bf16[4,128,256]{2,1,0:T(8,128)(2,1)S(1)}, bf16[4,128,256]{2,1,0:T(8,128)(2,1)S(1)}, u32[]{:S(2)}, u32[]{:S(2)}) collective-permute-start(bf16[4,128,256]{2,1,0:T(8,128)(2,1)S(1)} %pad_maximum_fusion.refs_0_), channel_id=1, source_target_pairs={{0,1},{1,0},{2,3},{3,2},{4,5},{5,4},{6,7},{7,6},{8,9},{9,8},{10,11... | collective-permute-start | bytes 786440 | tf_op jit(solution)/shard_map/ppermute | solution.py:209
  25.6 1.5 %collective-permute-start.5 = (bf16[4,128,256]{2,1,0:T(8,128)(2,1)S(1)}, bf16[4,128,256]{2,1,0:T(8,128)(2,1)S(1)}, u32[]{:S(2)}, u32[]{:S(2)}) collective-permute-start(bf16[4,128,256]{2,1,0:T(8,128)(2,1)S(1)} %collective-permute-done.3.refs_1_), channel_id=1, source_target_pairs={{0,1},{1,0},{2,3},{3,2},{4,5},{5,4},{6,7},{7,6},{8,9},{9,8},{10,11... | collective-permute-start | bytes 786440 | tf_op jit(solution)/shard_map/ppermute | solution.py:209
  32.5 1.5 %collective-permute-start.7 = (bf16[4,128,256]{2,1,0:T(8,128)(2,1)S(1)}, bf16[4,128,256]{2,1,0:T(8,128)(2,1)S(1)}, u32[]{:S(2)}, u32[]{:S(2)}) collective-permute-start(bf16[4,128,256]{2,1,0:T(8,128)(2,1)S(1)} %get-tuple-element.19), channel_id=1, source_target_pairs={{0,1},{1,0},{2,3},{3,2},{4,5},{5,4},{6,7},{7,6},{8,9},{9,8},{10,11... | collective-permute-start | bytes 786440 | tf_op jit(solution)/shard_map/ppermute | solution.py:209
  32.7 3.1 %collective-permute-start.6 = (bf16[4,128,256]{2,1,0:T(8,128)(2,1)S(1)}, bf16[4,128,256]{2,1,0:T(8,128)(2,1)S(1)}, u32[]{:S(2)}, u32[]{:S(2)}) collective-permute-start(bf16[4,128,256]{2,1,0:T(8,128)(2,1)S(1)} %get-tuple-element.17), channel_id=1, source_target_pairs={{0,1},{1,0},{2,3},{3,2},{4,5},{5,4},{6,7},{7,6},{8,9},{9,8},{10,11... | collective-permute-start | bytes 786440 | tf_op jit(solution)/shard_map/ppermute | solution.py:209
  34.1 8.4 %collective-permute-start.8 = (bf16[4,128,256]{2,1,0:T(8,128)(2,1)S(1)}, bf16[4,128,256]{2,1,0:T(8,128)(2,1)S(1)}, u32[]{:S(2)}, u32[]{:S(2)}) collective-permute-start(bf16[4,128,256]{2,1,0:T(8,128)(2,1)S(1)} %add_convert_fusion), channel_id=1, source_target_pairs={{0,2},{1,3},{2,0},{3,1},{4,6},{5,7},{6,4},{7,5},{8,10},{9,11},{10,... | collective-permute-start | bytes 786440 | tf_op jit(solution)/shard_map/ppermute | solution.py:209
  42.7 7.3 %collective-permute-start.10 = (bf16[128,256]{1,0:T(8,128)(2,1)S(1)}, bf16[128,256]{1,0:T(8,128)(2,1)S(1)}, u32[]{:S(2)}, u32[]{:S(2)}) collective-permute-start(bf16[128,256]{1,0:T(8,128)(2,1)S(1)} %get-tuple-element.62), channel_id=1, source_target_pairs={{0,8},{1,9},{2,10},{3,11},{4,12},{5,13},{6,14},{7,15},{8,0},{9,1},... | collective-permute-start | bytes 196616 | tf_op jit(solution)/shard_map/ppermute | solution.py:209
  44.8 6.4 %collective-permute-start.11 = (bf16[128,256]{1,0:T(8,128)(2,1)S(1)}, bf16[128,256]{1,0:T(8,128)(2,1)S(1)}, u32[]{:S(2)}, u32[]{:S(2)}) collective-permute-start(bf16[128,256]{1,0:T(8,128)(2,1)S(1)} %get-tuple-element.61), channel_id=1, source_target_pairs={{0,12},{1,13},{2,14},{3,15},{4,8},{5,9},{6,10},{7,11},{8,4},{9,5},... | collective-permute-start | bytes 196616 | tf_op jit(solution)/shard_map/ppermute | solution.py:209
  46.8 4.9 %collective-permute-start.9 = (bf16[128,256]{1,0:T(8,128)(2,1)S(1)}, bf16[128,256]{1,0:T(8,128)(2,1)S(1)}, u32[]{:S(2)}, u32[]{:S(2)}) collective-permute-start(bf16[128,256]{1,0:T(8,128)(2,1)S(1)} %get-tuple-element.60), channel_id=1, source_target_pairs={{0,4},{1,5},{2,6},{3,7},{4,0},{5,1},{6,2},{7,3},{8,12},{9,13},{10,... | collective-permute-start | bytes 196616 | tf_op jit(solution)/shard_map/ppermute | solution.py:209
  51.7 4.4 %collective-permute-start.13 = (bf16[128,256]{1,0:T(8,128)(2,1)S(1)}, bf16[128,256]{1,0:T(8,128)(2,1)S(1)}, u32[]{:S(2)}, u32[]{:S(2)}) collective-permute-start(bf16[128,256]{1,0:T(8,128)(2,1)S(1)} %fusion.11.refs_0_), channel_id=1, source_target_pairs={{0,4},{1,5},{2,6},{3,7},{4,0},{5,1},{6,2},{7,3},{8,12},{9,13},{10,... | collective-permute-start | bytes 196616 | tf_op jit(solution)/shard_map/ppermute | solution.py:217
  52.2 4.7 %collective-permute-start.15 = (bf16[128,256]{1,0:T(8,128)(2,1)S(1)}, bf16[128,256]{1,0:T(8,128)(2,1)S(1)}, u32[]{:S(2)}, u32[]{:S(2)}) collective-permute-start(bf16[128,256]{1,0:T(8,128)(2,1)S(1)} %fusion.11.refs_0_), channel_id=1, source_target_pairs={{0,16},{1,17},{2,18},{3,19},{4,20},{5,21},{6,22},{7,23},{8,24},{9,... | collective-permute-start | bytes 196616 | tf_op jit(solution)/shard_map/ppermute | solution.py:217
  53.8 5.2 %collective-permute-start.17 = (bf16[128,256]{1,0:T(8,128)(2,1)S(1)}, bf16[128,256]{1,0:T(8,128)(2,1)S(1)}, u32[]{:S(2)}, u32[]{:S(2)}) collective-permute-start(bf16[128,256]{1,0:T(8,128)(2,1)S(1)} %fusion.11.refs_0_), channel_id=1, source_target_pairs={{0,20},{1,21},{2,22},{3,23},{4,16},{5,17},{6,18},{7,19},{8,28},{9,... | collective-permute-start | bytes 196616 | tf_op jit(solution)/shard_map/ppermute | solution.py:217
  55.3 3.6 %collective-permute-start.12 = (bf16[128,256]{1,0:T(8,128)(2,1)S(1)}, bf16[128,256]{1,0:T(8,128)(2,1)S(1)}, u32[]{:S(2)}, u32[]{:S(2)}) collective-permute-start(bf16[128,256]{1,0:T(8,128)(2,1)S(1)} %fusion.11.refs_0_), channel_id=1, source_target_pairs={{0,1},{1,0},{2,3},{3,2},{4,5},{5,4},{6,7},{7,6},{8,9},{9,8},{10,11... | collective-permute-start | bytes 196616 | tf_op jit(solution)/shard_map/ppermute | solution.py:209
  56.1 2.8 %collective-permute-start.14 = (bf16[128,256]{1,0:T(8,128)(2,1)S(1)}, bf16[128,256]{1,0:T(8,128)(2,1)S(1)}, u32[]{:S(2)}, u32[]{:S(2)}) collective-permute-start(bf16[128,256]{1,0:T(8,128)(2,1)S(1)} %collective-permute-done.13.refs_2_), channel_id=1, source_target_pairs={{0,1},{1,0},{2,3},{3,2},{4,5},{5,4},{6,7},{7,6},{8,9},{9,8},{10,11... | collective-permute-start | bytes 196616 | tf_op jit(solution)/shard_map/ppermute | solution.py:209
  56.9 2.0 %collective-permute-start.16 = (bf16[128,256]{1,0:T(8,128)(2,1)S(1)}, bf16[128,256]{1,0:T(8,128)(2,1)S(1)}, u32[]{:S(2)}, u32[]{:S(2)}) collective-permute-start(bf16[128,256]{1,0:T(8,128)(2,1)S(1)} %collective-permute-done.15.refs_4_), channel_id=1, source_target_pairs={{0,1},{1,0},{2,3},{3,2},{4,5},{5,4},{6,7},{7,6},{8,9},{9,8},{10,11... | collective-permute-start | bytes 196616 | tf_op jit(solution)/shard_map/ppermute | solution.py:209
  58.9 1.3 %collective-permute-start.18 = (bf16[128,256]{1,0:T(8,128)(2,1)S(1)}, bf16[128,256]{1,0:T(8,128)(2,1)S(1)}, u32[]{:S(2)}, u32[]{:S(2)}) collective-permute-start(bf16[128,256]{1,0:T(8,128)(2,1)S(1)} %collective-permute-done.17.refs_6_), channel_id=1, source_target_pairs={{0,1},{1,0},{2,3},{3,2},{4,5},{5,4},{6,7},{7,6},{8,9},{9,8},{10,11... | collective-permute-start | bytes 196616 | tf_op jit(solution)/shard_map/ppermute | solution.py:209
  61.5 5.6 %collective-permute-start.19 = (bf16[256,256]{1,0:T(8,128)(2,1)S(1)}, bf16[256,256]{1,0:T(8,128)(2,1)S(1)}, u32[]{:S(2)}, u32[]{:S(2)}) collective-permute-start(bf16[256,256]{1,0:T(8,128)(2,1)S(1)} %get-tuple-element.23), channel_id=1, source_target_pairs={{0,2},{1,3},{2,0},{3,1},{4,6},{5,7},{6,4},{7,5},{8,10},{9,11},{10,... | collective-permute-start | bytes 393224 | tf_op jit(solution)/shard_map/ppermute | solution.py:209
  63.0 12.9 %collective-permute-start.20 = (bf16[256,256]{1,0:T(8,128)(2,1)S(1)}, bf16[256,256]{1,0:T(8,128)(2,1)S(1)}, u32[]{:S(2)}, u32[]{:S(2)}) collective-permute-start(bf16[256,256]{1,0:T(8,128)(2,1)S(1)} %get-tuple-element.24), channel_id=1, source_target_pairs={{0,8},{1,9},{2,10},{3,11},{4,12},{5,13},{6,14},{7,15},{8,0},{9,1},... | collective-permute-start | bytes 393224 | tf_op jit(solution)/shard_map/ppermute | solution.py:209
  65.6 12.0 %collective-permute-start.21 = (bf16[256,256]{1,0:T(8,128)(2,1)S(1)}, bf16[256,256]{1,0:T(8,128)(2,1)S(1)}, u32[]{:S(2)}, u32[]{:S(2)}) collective-permute-start(bf16[256,256]{1,0:T(8,128)(2,1)S(1)} %get-tuple-element.25), channel_id=1, source_target_pairs={{0,10},{1,11},{2,8},{3,9},{4,14},{5,15},{6,12},{7,13},{8,2},{9,3},... | collective-permute-start | bytes 393224 | tf_op jit(solution)/shard_map/ppermute | solution.py:209

commit v3 on v2

--- a/solution.py
+++ b/solution.py
@@ -133,7 +133,7 @@
             pltpu.SMEM((blocks,), jnp.int32),
         ],
         cost_estimate=pl.CostEstimate(
-            flops=10 * elements * head_dim, bytes_accessed=4 << 20, transcendentals=elements
+            flops=200 * elements * head_dim, bytes_accessed=4 << 20, transcendentals=elements
         ),
         compiler_params=pltpu.CompilerParams(vmem_limit_bytes=40 << 20),
         name="attention_grads",
@@ -143,25 +143,27 @@
 def weight_kernel(x_ref, *refs, members, spread):
     count = len(members)
     g_refs = refs[:count]
-    out_refs = refs[count:-1]
+    keep, near, *rest = refs[count:-1]
     g_all = refs[-1]
+    mask = members[-1][1]
     my_dp, my_ctx = lax.axis_index("dp"), lax.axis_index("ctx")
     mine = jnp.int32(0)
     for place, (i, m) in enumerate(members):
-        hit = (my_dp == i) & ((my_ctx & members[-1][1]) == m)
-        mine = jnp.where(hit, place, mine)
+        mine = jnp.where((my_dp == i) & ((my_ctx & mask) == m), place, mine)
     rows = g_refs[0].shape[0]
     for rel in range(count):
         place = pl.multiple_of(jnp.bitwise_xor(mine, rel) * rows, rows)
         g_all[pl.ds(place, rows), :] = g_refs[rel][...]
-    pieces = len(out_refs)
-    height = x_ref.shape[1] // pieces
-    me = my_ctx & ~members[-1][1]
-    for i in range(pieces):
-        image = jnp.int32(0)
+    height = x_ref.shape[1] // len(spread)
+    part = height // 2
+    me = my_ctx & ~mask
+    far = [s for s in spread if s and not s & 2]
+
+    def terms(image):
+        begin = jnp.int32(0)
         for place, s in enumerate(spread):
-            image = jnp.where(jnp.bitwise_xor(me, spread[i]) == s, place, image)
-        begin = pl.multiple_of(image * height, height)
+            begin = jnp.where(jnp.bitwise_xor(me, image) == s, place * height, begin)
+        begin = pl.multiple_of(begin, height)
         total = jnp.zeros((height, g_all.shape[1]), jnp.float32)
         for src in range(count):
             total = total + jnp.dot(
@@ -169,27 +171,74 @@
                 g_all[src * rows : (src + 1) * rows, :],
                 preferred_element_type=jnp.float32,
             )
-        out_refs[i][...] = total.astype(out_refs[i].dtype)
+        return total
+
+    near[:height, :] = terms(2).astype(near.dtype)
+    for k, s in enumerate(far):
+        straight, across, later = rest[3 * k : 3 * k + 3]
+        total = terms(s | 2)
+        across[...] = total[:part].astype(across.dtype)
+        near[height + k * part : height + (k + 1) * part, :] = total[part:].astype(near.dtype)
+        total = terms(s)
+        straight[...] = total[:part].astype(straight.dtype)
+        later[...] = total[part:]
+    keep[...] = terms(0)
 
 
 def weight_terms(x, g_parts, members, spread):
     count, height, rows = x.shape
     width = g_parts[0].shape[1]
     vmem = pl.BlockSpec(memory_space=pltpu.VMEM)
-    pieces = len(spread)
-    shape = (height // pieces, width)
+    height = height // len(spread)
+    part = height // 2
+    far = len(spread) // 2 - 1
+    out = [
+        jax.ShapeDtypeStruct((height, width), jnp.float32),
+        jax.ShapeDtypeStruct((height + far * part, width), jnp.bfloat16),
+    ]
+    for _ in range(far):
+        out += [jax.ShapeDtypeStruct((part, width), jnp.bfloat16)] * 2
+        out += [jax.ShapeDtypeStruct((part, width), jnp.float32)]
     return pl.pallas_call(
         functools.partial(weight_kernel, members=members, spread=spread),
-        out_shape=[jax.ShapeDtypeStruct(shape, jnp.bfloat16)] * pieces,
+        out_shape=out,
         in_specs=[vmem] * (count + 1),
-        out_specs=[vmem] * pieces,
+        out_specs=[vmem] * len(out),
         scratch_shapes=[pltpu.VMEM((count * rows, width), jnp.bfloat16)],
         cost_estimate=pl.CostEstimate(
-            flops=2 * count * height * rows * width, bytes_accessed=4 << 20, transcendentals=0
+            flops=2 * x.size * width, bytes_accessed=4 << 20, transcendentals=0
         ),
         compiler_params=pltpu.CompilerParams(vmem_limit_bytes=24 << 20),
         name="weight_terms",
     )(x, *g_parts)
+
+
+def columns_kernel(x_ref, out_ref, *, places, height):
+    for (row, line), begin in places:
+        block = x_ref[:, begin : begin + height]
+        out_ref[row, line : line + height, :] = block.T
+
+
+def columns_first(x, members, spread, n, dps):
+    rows, width = x.shape
+    height = width // (n * dps)
+    places = [
+        ((place, k * height), ((m | s) * dps + i) * height)
+        for place, (i, m) in enumerate(members)
+        for k, s in enumerate(spread)
+    ]
+    vmem = pl.BlockSpec(memory_space=pltpu.VMEM)
+    return pl.pallas_call(
+        functools.partial(columns_kernel, places=places, height=height),
+        out_shape=jax.ShapeDtypeStruct((len(members), len(spread) * height, rows), x.dtype),
+        in_specs=[vmem],
+        out_specs=vmem,
+        cost_estimate=pl.CostEstimate(
+            flops=0, bytes_accessed=4 * rows * width, transcendentals=0
+        ),
+        compiler_params=pltpu.CompilerParams(vmem_limit_bytes=16 << 20),
+        name="columns_first",
+    )(x)
 
 
 def after(x, *earlier):
@@ -219,17 +268,16 @@
         )
 
     kv = jnp.concatenate([keys[0], values[0]], axis=1)
-    base = jnp.stack([kv] + [swap(kv, 2 * mid * j) for j in range(1, top)])
+    tops = [kv] + [swap(kv, 2 * mid * j) for j in range(1, top)]
+    base = jnp.stack(tops)
+
+    xt = columns_first(after(layer_input[0], kv), members, spread, n, dps)
+    base, xt = lax.optimization_barrier((base, xt))
+
     near = [base] + [swap(base, 2 * j) for j in range(1, mid)]
     far = [swap(part, 1) for part in near]
-
-    x = after(layer_input[0], kv)
-    xt = x.T.reshape(n, dps, width // n // dps, rows)
-    xt = jnp.stack([jnp.stack([xt[m | s, i] for s in spread]) for i, m in members])
-    xt = after(xt, base)
     groups = [[i * n + (m | s) for i, m in members] for s in spread]
     xt = lax.all_to_all(xt, joint, 0, 0, axis_index_groups=groups, tiled=True)
-    xt = xt.reshape(len(members), -1, rows)
 
     dq, *parts = attention(
         block_order, doc_lengths, queries[0], d_out[0], near + far, n=n, mid=mid, top=top
@@ -237,16 +285,16 @@
 
     mine, others = parts[:mid], parts[mid:]
     received = [swap(p, 1) for p in reversed(others)][::-1]
-    sends = [
-        (mine[j].astype(jnp.float32) + received[j].astype(jnp.float32)).astype(jnp.bfloat16)
-        for j in range(1, mid)
-    ]
-    total = mine[0].astype(jnp.float32) + received[0].astype(jnp.float32)
+    keep = mine[0][0].astype(jnp.float32) + received[0][0].astype(jnp.float32)
+    total = mine[0][1:].astype(jnp.float32) + received[0][1:].astype(jnp.float32)
     for j in range(1, mid):
-        total = total + swap(sends[j - 1], 2 * j).astype(jnp.float32)
-    grad = total[0]
+        sent = (mine[j].astype(jnp.float32) + received[j].astype(jnp.float32)).astype(jnp.bfloat16)
+        total = total + swap(sent[1:], 2 * j).astype(jnp.float32)
+        keep = keep + swap(sent[0], 2 * j).astype(jnp.float32)
+    total = total.astype(jnp.bfloat16)
+    grad = keep
     for j in range(1, top):
-        grad = grad + swap(total[j].astype(jnp.bfloat16), 2 * mid * j).astype(jnp.float32)
+        grad = grad + swap(total[j - 1], 2 * mid * j).astype(jnp.float32)
     grad16 = grad.astype(jnp.bfloat16)
 
     gathered = {}
@@ -257,10 +305,19 @@
         if m & 1:
             gathered[i, m] = swap(gathered[i, m ^ 1], 1)
 
-    pieces = weight_terms(xt, [gathered[k] for k in members], members, spread)
-    weight = pieces[0].astype(jnp.float32)
-    for s, piece in zip(spread[1:], pieces[1:]):
-        weight = weight + swap(piece, s).astype(jnp.float32)
+    keep, close, *rest = weight_terms(xt, [gathered[k] for k in members], members, spread)
+    height = keep.shape[0]
+    part = height // 2
+    came = swap(close, 2).astype(jnp.float32)
+    upper = keep[:part] + came[:part]
+    lower = keep[part:] + came[part:height]
+    for k, s in enumerate(s for s in spread if s and not s & 2):
+        straight, across, later = rest[3 * k : 3 * k + 3]
+        upper = upper + swap(straight, s).astype(jnp.float32)
+        upper = upper + swap(across, s | 2).astype(jnp.float32)
+        later = later + came[height + k * part : height + (k + 1) * part]
+        lower = lower + swap(later.astype(jnp.bfloat16), s).astype(jnp.float32)
+    weight = jnp.concatenate([upper, lower], axis=0)
     weight = weight * (1.0 / math.sqrt(dps * rows * n))
     return (
         dq[None],

time: 78.7 us -> 71.1 us (0.903)
  waiting for transfers between devices: 39.5 us -> 31.4 us
    ppermute x19 -> x21, waiting for transfers between devices: 35.9 us -> 27.7 us  [swap(): return lax.ppermute(x, 'ctx', [(i, i ^ k) for i in range(n)])]
    reshape x1 -> x0, local copies, waits for them, and re-layouts: 3.22 us -> none  [per_device(): xt = x.T.reshape(n, dps, width // n // dps, rows)]
    unnamed x10 -> x12, local copies, waits for them, and re-layouts: 0.03 us -> 2.96 us
    ppermute x19 -> x21, starting transfers between devices: 18 us -> 18.8 us  [swap(): return lax.ppermute(x, 'ctx', [(i, i ^ k) for i in range(n)])]
  transfers between devices with their start and end apart: 23 -> 25, of which waited for: 16 -> 16; matrix products, arithmetic and copies ran while one was open for 6% -> 1% of each run, Pallas kernels for 7% -> 8%
where the time goes in v3:
time: 71.1 us; the launch traced here: 70.9 us
  waiting for transfers between devices  31.4 us (44%)
  starting transfers between devices  26 us (37%)
  Pallas kernels  7.19 us (10%)
  local copies, waits for them, and re-layouts  3.63 us (5%)
  other arithmetic  1.82 us (3%)
  between operations  0.78 us (1%)
    ppermute x21, waiting for transfers between devices, swap(): return lax.ppermute(x, 'ctx', [(i, i ^ k) for i in range(n)])  27.7 us
    ppermute x21, starting transfers between devices, swap(): return lax.ppermute(x, 'ctx', [(i, i ^ k) for i in range(n)])  18.8 us
    pallas_call x1, Pallas kernels, attention(): pl.pallas_call(body, out_shape=[jax.ShapeDtypeStruct((rows, width), jnp.b...  5.34 us
    ppermute x3, waiting for transfers between devices, cross(): lax.ppermute(x, joint, [(a * n + b, (a ^ i) * n + (b ^ m)) for a in range...  3.72 us
    all_to_all x1, starting transfers between devices, per_device(): xt = lax.all_to_all(xt, joint, 0, 0, axis_index_groups=groups, tiled=True)  3.6 us
    ppermute x3, starting transfers between devices, cross(): lax.ppermute(x, joint, [(a * n + b, (a ^ i) * n + (b ^ m)) for a in range...  3.55 us
    unnamed x12, local copies, waits for them, and re-layouts  2.96 us
  transfers between devices with their start and end apart: 25, of which 16 were waited for; matrix products, arithmetic and copies ran while one was open for 1% of the time, Pallas kernels for 8%

profile of v3, /device:TPU:0, one launch (start us, length us, event | category | flops | bytes accessed | tf_op | source)
XLA Modules:
  0.0 70.9 jit_solution(8490290159138270131)
XLA Ops:
  0.6 0.8 %fusion.10 = (bf16[1,128,256]{2,1,0:T(8,128)(2,1)S(1)}, bf16[128,256]{1,0:T(8,128)(2,1)S(1)}) fusion(bf16[128,128]{1,0:T(8,128)(2,1)} %bitcast.43, bf16[128,128]{1,0:T(8,128)(2,1)} %bitcast.44), kind=kLoop, calls=%fused_computation.25 | loop fusion | flops 131072 | bytes 196608 | tf_op jit(solution)/shard_map/stack | solution.py:272
  1.4 5.1 %collective-permute-start.2 = (bf16[128,256]{1,0:T(8,128)(2,1)S(1)}, bf16[128,256]{1,0:T(8,128)(2,1)S(1)}, u32[]{:S(2)}, u32[]{:S(2)}) collective-permute-start(bf16[128,256]{1,0:T(8,128)(2,1)S(1)} %get-tuple-element.38), channel_id=1, source_target_pairs={{0,12},{1,13},{2,14},{3,15},{4,8},{5,9},{6,10},{7,11},{8,4},{9,5},... | collective-permute-start | bytes 196616 | tf_op jit(solution)/shard_map/ppermute | solution.py:258
  6.5 0.0 collective-permute-start.1
  6.5 0.6 collective-permute-start
  7.2 1.6 %copy-done.1 = bf16[1,128,8192]{2,1,0:T(8,128)(2,1)S(1)} copy-done((bf16[1,128,8192]{2,1,0:T(8,128)(2,1)S(1)}, bf16[1,128,8192]{2,1,0:T(8,128)(2,1)}, u32[]{:S(2)}) %copy-start.1) | copy-done | bytes 2097176
  8.8 0.6 columns_first.1
  9.4 1.3 %copy-done = bf16[8,1024,128]{2,1,0:T(8,128)(2,1)} copy-done((bf16[8,1024,128]{2,1,0:T(8,128)(2,1)}, bf16[8,1024,128]{2,1,0:T(8,128)(2,1)S(1)}, u32[]{:S(2)}) %copy-start) | copy-done | bytes 2097176
  10.7 0.0 collective-permute-done.2
  10.7 1.4 %collective-permute-done.1 = bf16[128,256]{1,0:T(8,128)(2,1)S(1)} collective-permute-done((bf16[128,256]{1,0:T(8,128)(2,1)S(1)}, bf16[128,256]{1,0:T(8,128)(2,1)S(1)}, u32[]{:S(2)}, u32[]{:S(2)}) %collective-permute-start.1) | collective-permute-done | bytes 65568 | tf_op jit(solution)/shard_map/ppermute | solution.py:258
  12.1 0.0 collective-permute-done
  12.2 0.0 copy-start.2
  12.2 0.0 copy-start.3
  12.2 0.0 copy-start.4
  12.2 0.0 copy-start.5
  12.2 1.6 %collective-permute-start.3 = (bf16[4,128,256]{2,1,0:T(8,128)(2,1)S(1)}, bf16[4,128,256]{2,1,0:T(8,128)(2,1)S(1)}, u32[]{:S(2)}, u32[]{:S(2)}) collective-permute-start(bf16[4,128,256]{2,1,0:T(8,128)(2,1)S(1)} %pad_maximum_fusion.refs_0_), channel_id=1, source_target_pairs={{0,2},{1,3},{2,0},{3,1},{4,6},{5,7},{6,4},{7,5},{8,10},{9,11},{10,... | collective-permute-start | bytes 786440 | tf_op jit(solution)/shard_map/ppermute | solution.py:258
  13.8 3.6 %all-to-all-start = ((bf16[8,1024,128]{2,1,0:T(8,128)(2,1)}), bf16[8,1024,128]{2,1,0:T(8,128)(2,1)S(1)}, u32[]{:S(2)}, u32[]{:S(2)}) async-start(bf16[8,1024,128]{2,1,0:T(8,128)(2,1)} %copy-done), calls=%async_computation | async-start | bytes 4194304 | tf_op jit(solution)/shard_map/all_to_all | solution.py:280
  17.4 0.4 collective-permute-start.4
  17.8 2.3 %collective-permute-done.3.refs_1_ = bf16[4,128,256]{2,1,0:T(8,128)(2,1)S(1)} collective-permute-done((bf16[4,128,256]{2,1,0:T(8,128)(2,1)S(1)}, bf16[4,128,256]{2,1,0:T(8,128)(2,1)S(1)}, u32[]{:S(2)}, u32[]{:S(2)}) %collective-permute-start.3) | collective-permute-done | bytes 262176 | tf_op jit(solution)/shard_map/ppermute | solution.py:258
  20.2 0.0 collective-permute-start.5
  20.2 0.0 collective-permute-done.4.refs_2_
  20.2 1.5 %collective-permute-done.5.refs_3_ = bf16[4,128,256]{2,1,0:T(8,128)(2,1)S(1)} collective-permute-done((bf16[4,128,256]{2,1,0:T(8,128)(2,1)S(1)}, bf16[4,128,256]{2,1,0:T(8,128)(2,1)S(1)}, u32[]{:S(2)}, u32[]{:S(2)}) %collective-permute-start.5) | collective-permute-done | bytes 262176 | tf_op jit(solution)/shard_map/ppermute | solution.py:258
  21.7 5.3 %attention_grads.1 = (bf16[128,1024]{1,0:T(8,128)(2,1)}, f32[4,128,256]{2,1,0:T(8,128)S(1)}, bf16[4,128,256]{2,1,0:T(8,128)(2,1)S(1)}, bf16[4,128,256]{2,1,0:T(8,128)(2,1)S(1)}, bf16[4,128,256]{2,1,0:T(8,128)(2,1)S(1)}) custom-call(s32[32]{0:T(128)S(1)} %copy-done.4, s32[1,8]{1,0:T(1,128)S(1)} %copy-done.5, bf16[128,1024]{1,0:T(8,128)(2,1)S(1)} %bitcast.38, ...), custom_call_target="tpu_custom_call" | custom-call | flops 16777216000 | bytes 4194304 | tf_op jit(solution)/shard_map/attention_grads/pallas_call | solution.py:120
  27.1 0.1 collective-permute-start.7
  27.2 0.4 collective-permute-start.6
  27.6 1.0 %collective-permute-done.7 = bf16[4,128,256]{2,1,0:T(8,128)(2,1)S(1)} collective-permute-done((bf16[4,128,256]{2,1,0:T(8,128)(2,1)S(1)}, bf16[4,128,256]{2,1,0:T(8,128)(2,1)S(1)}, u32[]{:S(2)}, u32[]{:S(2)}) %collective-permute-start.7) | collective-permute-done | bytes 262176 | tf_op jit(solution)/shard_map/ppermute | solution.py:258
  28.6 0.1 add_convert_fusion
  28.7 1.8 %collective-permute-start.9 = (bf16[3,128,256]{2,1,0:T(8,128)(2,1)S(1)}, bf16[3,128,256]{2,1,0:T(8,128)(2,1)S(1)}, u32[]{:S(2)}, u32[]{:S(2)}) collective-permute-start(bf16[3,128,256]{2,1,0:T(8,128)(2,1)S(1)} %slice.67), channel_id=1, source_target_pairs={{0,2},{1,3},{2,0},{3,1},{4,6},{5,7},{6,4},{7,5},{8,10},{9,11},{10,... | collective-permute-start | bytes 589832 | tf_op jit(solution)/shard_map/ppermute | solution.py:258
  30.5 0.3 collective-permute-start.8
  30.8 0.0 collective-permute-done.6
  30.8 5.6 %collective-permute-done.9 = bf16[3,128,256]{2,1,0:T(8,128)(2,1)S(1)} collective-permute-done((bf16[3,128,256]{2,1,0:T(8,128)(2,1)S(1)}, bf16[3,128,256]{2,1,0:T(8,128)(2,1)S(1)}, u32[]{:S(2)}, u32[]{:S(2)}) %collective-permute-start.9) | collective-permute-done | bytes 196640 | tf_op jit(solution)/shard_map/ppermute | solution.py:258
  36.4 0.1 add_convert_fusion.1
  36.5 0.2 collective-permute-start.10
  36.7 1.8 %collective-permute-start.12 = (bf16[128,256]{1,0:T(8,128)(2,1)S(1)}, bf16[128,256]{1,0:T(8,128)(2,1)S(1)}, u32[]{:S(2)}, u32[]{:S(2)}) collective-permute-start(bf16[128,256]{1,0:T(8,128)(2,1)S(1)} %get-tuple-element.33), channel_id=1, source_target_pairs={{0,12},{1,13},{2,14},{3,15},{4,8},{5,9},{6,10},{7,11},{8,4},{9,5},... | collective-permute-start | bytes 196616 | tf_op jit(solution)/shard_map/ppermute | solution.py:258
  38.5 1.5 %collective-permute-start.11 = (bf16[128,256]{1,0:T(8,128)(2,1)S(1)}, bf16[128,256]{1,0:T(8,128)(2,1)S(1)}, u32[]{:S(2)}, u32[]{:S(2)}) collective-permute-start(bf16[128,256]{1,0:T(8,128)(2,1)S(1)} %get-tuple-element.34), channel_id=1, source_target_pairs={{0,8},{1,9},{2,10},{3,11},{4,12},{5,13},{6,14},{7,15},{8,0},{9,1},... | collective-permute-start | bytes 196616 | tf_op jit(solution)/shard_map/ppermute | solution.py:258
  40.0 0.0 collective-permute-done.8
  40.0 6.3 %collective-permute-done.10 = bf16[128,256]{1,0:T(8,128)(2,1)S(1)} collective-permute-done((bf16[128,256]{1,0:T(8,128)(2,1)S(1)}, bf16[128,256]{1,0:T(8,128)(2,1)S(1)}, u32[]{:S(2)}, u32[]{:S(2)}) %collective-permute-start.10) | collective-permute-done | bytes 65568 | tf_op jit(solution)/shard_map/ppermute | solution.py:258
  46.4 1.4 %collective-permute-done.12 = bf16[128,256]{1,0:T(8,128)(2,1)S(1)} collective-permute-done((bf16[128,256]{1,0:T(8,128)(2,1)S(1)}, bf16[128,256]{1,0:T(8,128)(2,1)S(1)}, u32[]{:S(2)}, u32[]{:S(2)}) %collective-permute-start.12) | collective-permute-done | bytes 65568 | tf_op jit(solution)/shard_map/ppermute | solution.py:258
  47.8 0.1 fusion.9.refs_0_
  47.8 2.5 %collective-permute-start.18 = (bf16[128,256]{1,0:T(8,128)(2,1)S(1)}, bf16[128,256]{1,0:T(8,128)(2,1)S(1)}, u32[]{:S(2)}, u32[]{:S(2)}) collective-permute-start(bf16[128,256]{1,0:T(8,128)(2,1)S(1)} %fusion.9.refs_0_), channel_id=1, source_target_pairs={{0,20},{1,21},{2,22},{3,23},{4,16},{5,17},{6,18},{7,19},{8,28},{9,... | collective-permute-start | bytes 196616 | tf_op jit(solution)/shard_map/ppermute | solution.py:266
  50.3 0.6 collective-permute-start.16
  50.8 0.5 collective-permute-start.14
  51.4 0.0 collective-permute-start.13
  51.4 1.8 %collective-permute-done.18.refs_6_ = bf16[128,256]{1,0:T(8,128)(2,1)S(1)} collective-permute-done((bf16[128,256]{1,0:T(8,128)(2,1)S(1)}, bf16[128,256]{1,0:T(8,128)(2,1)S(1)}, u32[]{:S(2)}, u32[]{:S(2)}) %collective-permute-start.18) | collective-permute-done | bytes 65568 | tf_op jit(solution)/shard_map/ppermute | solution.py:266
  53.2 0.0 collective-permute-start.19
  53.2 1.4 %collective-permute-done.16.refs_4_ = bf16[128,256]{1,0:T(8,128)(2,1)S(1)} collective-permute-done((bf16[128,256]{1,0:T(8,128)(2,1)S(1)}, bf16[128,256]{1,0:T(8,128)(2,1)S(1)}, u32[]{:S(2)}, u32[]{:S(2)}) %collective-permute-start.16) | collective-permute-done | bytes 65568 | tf_op jit(solution)/shard_map/ppermute | solution.py:266
  54.5 0.6 collective-permute-done.14.refs_2_
  55.1 0.0 collective-permute-start.15
  55.1 0.0 collective-permute-done.13.refs_1_
  55.1 0.0 collective-permute-done.19.refs_7_
  55.1 0.7 collective-permute-done.17.refs_5_
  55.8 0.6 collective-permute-done.15.refs_3_
  56.4 0.0 all-to-all-done.x_ref
  56.4 1.3 %weight_terms.1 = (f32[256,256]{1,0:T(8,128)S(1)}, bf16[384,256]{1,0:T(8,128)(2,1)S(1)}, bf16[128,256]{1,0:T(8,128)(2,1)S(1)}, bf16[128,256]{1,0:T(8,128)(2,1)S(1)}, f32[128,256]{1,0:T(8,128)S(1)}) custom-call(bf16[8,1024,128]{2,1,0:T(8,128)(2,1)S(1)} %all-to-all-done.x_ref, bf16[128,256]{1,0:T(8,128)(2,1)S(1)} %fusion.9.refs_0_, ...), custom_call_target="tpu_custom_call" | custom-call | flops 536870912 | bytes 4194304 | tf_op jit(solution)/shard_map/weight_terms/pallas_call | solution.py:202
  57.6 0.6 collective-permute-start.20
  58.2 1.0 %collective-permute-start.21 = (bf16[128,256]{1,0:T(8,128)(2,1)S(1)}, bf16[128,256]{1,0:T(8,128)(2,1)S(1)}, u32[]{:S(2)}, u32[]{:S(2)}) collective-permute-start(bf16[128,256]{1,0:T(8,128)(2,1)S(1)} %get-tuple-element.27), channel_id=1, source_target_pairs={{0,8},{1,9},{2,10},{3,11},{4,12},{5,13},{6,14},{7,15},{8,0},{9,1},... | collective-permute-start | bytes 196616 | tf_op jit(solution)/shard_map/ppermute | solution.py:258
  59.2 2.9 %collective-permute-start.22 = (bf16[128,256]{1,0:T(8,128)(2,1)S(1)}, bf16[128,256]{1,0:T(8,128)(2,1)S(1)}, u32[]{:S(2)}, u32[]{:S(2)}) collective-permute-start(bf16[128,256]{1,0:T(8,128)(2,1)S(1)} %get-tuple-element.28), channel_id=1, source_target_pairs={{0,10},{1,11},{2,8},{3,9},{4,14},{5,15},{6,12},{7,13},{8,2},{9,3},... | collective-permute-start | bytes 196616 | tf_op jit(solution)/shard_map/ppermute | solution.py:258
  62.1 2.6 %collective-permute-done.20 = bf16[384,256]{1,0:T(8,128)(2,1)S(1)} collective-permute-done((bf16[384,256]{1,0:T(8,128)(2,1)S(1)}, bf16[384,256]{1,0:T(8,128)(2,1)S(1)}, u32[]{:S(2)}, u32[]{:S(2)}) %collective-permute-start.20) | collective-permute-done | bytes 196640 | tf_op jit(solution)/shard_map/ppermute | solution.py:258
  64.7 0.5 collective-permute-start.23
  65.2 0.6 slice_bitcast_fusion.4
  65.8 0.4 collective-permute-done.21
  66.2 3.0 %collective-permute-done.22 = bf16[128,256]{1,0:T(8,128)(2,1)S(1)} collective-permute-done((bf16[128,256]{1,0:T(8,128)(2,1)S(1)}, bf16[128,256]{1,0:T(8,128)(2,1)S(1)}, u32[]{:S(2)}, u32[]{:S(2)}) %collective-permute-start.22) | collective-permute-done | bytes 65568 | tf_op jit(solution)/shard_map/ppermute | solution.py:258
  69.1 0.9 %collective-permute-done.23 = bf16[128,256]{1,0:T(8,128)(2,1)S(1)} collective-permute-done((bf16[128,256]{1,0:T(8,128)(2,1)S(1)}, bf16[128,256]{1,0:T(8,128)(2,1)S(1)}, u32[]{:S(2)}, u32[]{:S(2)}) %collective-permute-start.23) | collective-permute-done | bytes 65568 | tf_op jit(solution)/shard_map/ppermute | solution.py:258
  70.1 0.1 fusion.5
  70.1 0.7 %maximum_multiply_fusion = f32[1,256,256]{2,1,0:T(8,128)} fusion(f32[1,128,256]{2,1,0:T(8,128)S(1)} %get-tuple-element.31, f32[1,128,256]{2,1,0:T(8,128)S(1)} %get-tuple-element.30), kind=kLoop, calls=%fused_computation.3 | loop fusion | flops 131072 | bytes 524288 | tf_op jit(solution)/shard_map/mul | solution.py:321
  (14 shorter events, 0.1 us)
Async XLA Ops:
  1.4 9.3 %collective-permute-start.2 = (bf16[128,256]{1,0:T(8,128)(2,1)S(1)}, bf16[128,256]{1,0:T(8,128)(2,1)S(1)}, u32[]{:S(2)}, u32[]{:S(2)}) collective-permute-start(bf16[128,256]{1,0:T(8,128)(2,1)S(1)} %get-tuple-element.38), channel_id=1, source_target_pairs={{0,12},{1,13},{2,14},{3,15},{4,8},{5,9},{6,10},{7,11},{8,4},{9,5},... | collective-permute-start | bytes 196616 | tf_op jit(solution)/shard_map/ppermute | solution.py:258
  6.5 5.6 %collective-permute-start.1 = (bf16[128,256]{1,0:T(8,128)(2,1)S(1)}, bf16[128,256]{1,0:T(8,128)(2,1)S(1)}, u32[]{:S(2)}, u32[]{:S(2)}) collective-permute-start(bf16[128,256]{1,0:T(8,128)(2,1)S(1)} %get-tuple-element.38), channel_id=1, source_target_pairs={{0,8},{1,9},{2,10},{3,11},{4,12},{5,13},{6,14},{7,15},{8,0},{9,1},... | collective-permute-start | bytes 196616 | tf_op jit(solution)/shard_map/ppermute | solution.py:258
  6.5 5.6 %collective-permute-start = (bf16[128,256]{1,0:T(8,128)(2,1)S(1)}, bf16[128,256]{1,0:T(8,128)(2,1)S(1)}, u32[]{:S(2)}, u32[]{:S(2)}) collective-permute-start(bf16[128,256]{1,0:T(8,128)(2,1)S(1)} %get-tuple-element.38), channel_id=1, source_target_pairs={{0,4},{1,5},{2,6},{3,7},{4,0},{5,1},{6,2},{7,3},{8,12},{9,13},{10,... | collective-permute-start | bytes 196616 | tf_op jit(solution)/shard_map/ppermute | solution.py:258
  7.2 1.6 %copy-start.1 = (bf16[1,128,8192]{2,1,0:T(8,128)(2,1)S(1)}, bf16[1,128,8192]{2,1,0:T(8,128)(2,1)}, u32[]{:S(2)}) copy-start(bf16[1,128,8192]{2,1,0:T(8,128)(2,1)} %param.7) | copy-start | bytes 6291460
  9.4 1.4 %copy-start = (bf16[8,1024,128]{2,1,0:T(8,128)(2,1)}, bf16[8,1024,128]{2,1,0:T(8,128)(2,1)S(1)}, u32[]{:S(2)}) copy-start(bf16[8,1024,128]{2,1,0:T(8,128)(2,1)S(1)} %columns_first.1) | copy-start | bytes 6291460
  12.2 9.5 %copy-start.2 = (bf16[1,128,1024]{2,1,0:T(8,128)(2,1)S(1)}, bf16[1,128,1024]{2,1,0:T(8,128)(2,1)}, u32[]{:S(2)}) copy-start(bf16[1,128,1024]{2,1,0:T(8,128)(2,1)} %param.8) | copy-start | bytes 786436
  12.2 9.5 %copy-start.3 = (bf16[1,128,1024]{2,1,0:T(8,128)(2,1)S(1)}, bf16[1,128,1024]{2,1,0:T(8,128)(2,1)}, u32[]{:S(2)}) copy-start(bf16[1,128,1024]{2,1,0:T(8,128)(2,1)} %param.11) | copy-start | bytes 786436
  12.2 9.5 %copy-start.4 = (s32[32]{0:T(128)S(1)}, s32[32]{0:T(128)}, u32[]{:S(2)}) copy-start(s32[32]{0:T(128)} %order.1) | copy-start | bytes 388
  12.2 9.5 %copy-start.5 = (s32[1,8]{1,0:T(1,128)S(1)}, s32[1,8]{1,0:T(1,128)}, u32[]{:S(2)}) copy-start(s32[1,8]{1,0:T(1,128)} %lengths.1) | copy-start | bytes 100
  12.2 7.9 %collective-permute-start.3 = (bf16[4,128,256]{2,1,0:T(8,128)(2,1)S(1)}, bf16[4,128,256]{2,1,0:T(8,128)(2,1)S(1)}, u32[]{:S(2)}, u32[]{:S(2)}) collective-permute-start(bf16[4,128,256]{2,1,0:T(8,128)(2,1)S(1)} %pad_maximum_fusion.refs_0_), channel_id=1, source_target_pairs={{0,2},{1,3},{2,0},{3,1},{4,6},{5,7},{6,4},{7,5},{8,10},{9,11},{10,... | collective-permute-start | bytes 786440 | tf_op jit(solution)/shard_map/ppermute | solution.py:258
  13.8 42.5 %all-to-all-start = ((bf16[8,1024,128]{2,1,0:T(8,128)(2,1)}), bf16[8,1024,128]{2,1,0:T(8,128)(2,1)S(1)}, u32[]{:S(2)}, u32[]{:S(2)}) async-start(bf16[8,1024,128]{2,1,0:T(8,128)(2,1)} %copy-done), calls=%async_computation | async-start | bytes 4194304 | tf_op jit(solution)/shard_map/all_to_all | solution.py:280
  17.4 2.8 %collective-permute-start.4 = (bf16[4,128,256]{2,1,0:T(8,128)(2,1)S(1)}, bf16[4,128,256]{2,1,0:T(8,128)(2,1)S(1)}, u32[]{:S(2)}, u32[]{:S(2)}) collective-permute-start(bf16[4,128,256]{2,1,0:T(8,128)(2,1)S(1)} %pad_maximum_fusion.refs_0_), channel_id=1, source_target_pairs={{0,1},{1,0},{2,3},{3,2},{4,5},{5,4},{6,7},{7,6},{8,9},{9,8},{10,11... | collective-permute-start | bytes 786440 | tf_op jit(solution)/shard_map/ppermute | solution.py:258
  20.2 1.5 %collective-permute-start.5 = (bf16[4,128,256]{2,1,0:T(8,128)(2,1)S(1)}, bf16[4,128,256]{2,1,0:T(8,128)(2,1)S(1)}, u32[]{:S(2)}, u32[]{:S(2)}) collective-permute-start(bf16[4,128,256]{2,1,0:T(8,128)(2,1)S(1)} %collective-permute-done.3.refs_1_), channel_id=1, source_target_pairs={{0,1},{1,0},{2,3},{3,2},{4,5},{5,4},{6,7},{7,6},{8,9},{9,8},{10,11... | collective-permute-start | bytes 786440 | tf_op jit(solution)/shard_map/ppermute | solution.py:258
  27.1 1.5 %collective-permute-start.7 = (bf16[4,128,256]{2,1,0:T(8,128)(2,1)S(1)}, bf16[4,128,256]{2,1,0:T(8,128)(2,1)S(1)}, u32[]{:S(2)}, u32[]{:S(2)}) collective-permute-start(bf16[4,128,256]{2,1,0:T(8,128)(2,1)S(1)} %get-tuple-element.23), channel_id=1, source_target_pairs={{0,1},{1,0},{2,3},{3,2},{4,5},{5,4},{6,7},{7,6},{8,9},{9,8},{10,11... | collective-permute-start | bytes 786440 | tf_op jit(solution)/shard_map/ppermute | solution.py:258
  27.2 3.6 %collective-permute-start.6 = (bf16[4,128,256]{2,1,0:T(8,128)(2,1)S(1)}, bf16[4,128,256]{2,1,0:T(8,128)(2,1)S(1)}, u32[]{:S(2)}, u32[]{:S(2)}) collective-permute-start(bf16[4,128,256]{2,1,0:T(8,128)(2,1)S(1)} %get-tuple-element.21), channel_id=1, source_target_pairs={{0,1},{1,0},{2,3},{3,2},{4,5},{5,4},{6,7},{7,6},{8,9},{9,8},{10,11... | collective-permute-start | bytes 786440 | tf_op jit(solution)/shard_map/ppermute | solution.py:258
  28.7 7.7 %collective-permute-start.9 = (bf16[3,128,256]{2,1,0:T(8,128)(2,1)S(1)}, bf16[3,128,256]{2,1,0:T(8,128)(2,1)S(1)}, u32[]{:S(2)}, u32[]{:S(2)}) collective-permute-start(bf16[3,128,256]{2,1,0:T(8,128)(2,1)S(1)} %slice.67), channel_id=1, source_target_pairs={{0,2},{1,3},{2,0},{3,1},{4,6},{5,7},{6,4},{7,5},{8,10},{9,11},{10,... | collective-permute-start | bytes 589832 | tf_op jit(solution)/shard_map/ppermute | solution.py:258
  30.5 9.6 %collective-permute-start.8 = (bf16[128,256]{1,0:T(8,128)(2,1)S(1)}, bf16[128,256]{1,0:T(8,128)(2,1)S(1)}, u32[]{:S(2)}, u32[]{:S(2)}) collective-permute-start(bf16[128,256]{1,0:T(8,128)(2,1)S(1)} %slice_bitcast_fusion.3), channel_id=1, source_target_pairs={{0,2},{1,3},{2,0},{3,1},{4,6},{5,7},{6,4},{7,5},{8,10},{9,11},{10,... | collective-permute-start | bytes 196616 | tf_op jit(solution)/shard_map/ppermute | solution.py:258
  36.5 9.9 %collective-permute-start.10 = (bf16[128,256]{1,0:T(8,128)(2,1)S(1)}, bf16[128,256]{1,0:T(8,128)(2,1)S(1)}, u32[]{:S(2)}, u32[]{:S(2)}) collective-permute-start(bf16[128,256]{1,0:T(8,128)(2,1)S(1)} %get-tuple-element.32), channel_id=1, source_target_pairs={{0,4},{1,5},{2,6},{3,7},{4,0},{5,1},{6,2},{7,3},{8,12},{9,13},{10,... | collective-permute-start | bytes 196616 | tf_op jit(solution)/shard_map/ppermute | solution.py:258
  36.7 11.1 %collective-permute-start.12 = (bf16[128,256]{1,0:T(8,128)(2,1)S(1)}, bf16[128,256]{1,0:T(8,128)(2,1)S(1)}, u32[]{:S(2)}, u32[]{:S(2)}) collective-permute-start(bf16[128,256]{1,0:T(8,128)(2,1)S(1)} %get-tuple-element.33), channel_id=1, source_target_pairs={{0,12},{1,13},{2,14},{3,15},{4,8},{5,9},{6,10},{7,11},{8,4},{9,5},... | collective-permute-start | bytes 196616 | tf_op jit(solution)/shard_map/ppermute | solution.py:258
  38.5 9.2 %collective-permute-start.11 = (bf16[128,256]{1,0:T(8,128)(2,1)S(1)}, bf16[128,256]{1,0:T(8,128)(2,1)S(1)}, u32[]{:S(2)}, u32[]{:S(2)}) collective-permute-start(bf16[128,256]{1,0:T(8,128)(2,1)S(1)} %get-tuple-element.34), channel_id=1, source_target_pairs={{0,8},{1,9},{2,10},{3,11},{4,12},{5,13},{6,14},{7,15},{8,0},{9,1},... | collective-permute-start | bytes 196616 | tf_op jit(solution)/shard_map/ppermute | solution.py:258
  47.8 5.3 %collective-permute-start.18 = (bf16[128,256]{1,0:T(8,128)(2,1)S(1)}, bf16[128,256]{1,0:T(8,128)(2,1)S(1)}, u32[]{:S(2)}, u32[]{:S(2)}) collective-permute-start(bf16[128,256]{1,0:T(8,128)(2,1)S(1)} %fusion.9.refs_0_), channel_id=1, source_target_pairs={{0,20},{1,21},{2,22},{3,23},{4,16},{5,17},{6,18},{7,19},{8,28},{9,... | collective-permute-start | bytes 196616 | tf_op jit(solution)/shard_map/ppermute | solution.py:266
  50.3 4.3 %collective-permute-start.16 = (bf16[128,256]{1,0:T(8,128)(2,1)S(1)}, bf16[128,256]{1,0:T(8,128)(2,1)S(1)}, u32[]{:S(2)}, u32[]{:S(2)}) collective-permute-start(bf16[128,256]{1,0:T(8,128)(2,1)S(1)} %fusion.9.refs_0_), channel_id=1, source_target_pairs={{0,16},{1,17},{2,18},{3,19},{4,20},{5,21},{6,22},{7,23},{8,24},{9,... | collective-permute-start | bytes 196616 | tf_op jit(solution)/shard_map/ppermute | solution.py:266
  50.8 4.3 %collective-permute-start.14 = (bf16[128,256]{1,0:T(8,128)(2,1)S(1)}, bf16[128,256]{1,0:T(8,128)(2,1)S(1)}, u32[]{:S(2)}, u32[]{:S(2)}) collective-permute-start(bf16[128,256]{1,0:T(8,128)(2,1)S(1)} %fusion.9.refs_0_), channel_id=1, source_target_pairs={{0,4},{1,5},{2,6},{3,7},{4,0},{5,1},{6,2},{7,3},{8,12},{9,13},{10,... | collective-permute-start | bytes 196616 | tf_op jit(solution)/shard_map/ppermute | solution.py:266
  51.4 3.7 %collective-permute-start.13 = (bf16[128,256]{1,0:T(8,128)(2,1)S(1)}, bf16[128,256]{1,0:T(8,128)(2,1)S(1)}, u32[]{:S(2)}, u32[]{:S(2)}) collective-permute-start(bf16[128,256]{1,0:T(8,128)(2,1)S(1)} %fusion.9.refs_0_), channel_id=1, source_target_pairs={{0,1},{1,0},{2,3},{3,2},{4,5},{5,4},{6,7},{7,6},{8,9},{9,8},{10,11... | collective-permute-start | bytes 196616 | tf_op jit(solution)/shard_map/ppermute | solution.py:258
  53.2 2.0 %collective-permute-start.19 = (bf16[128,256]{1,0:T(8,128)(2,1)S(1)}, bf16[128,256]{1,0:T(8,128)(2,1)S(1)}, u32[]{:S(2)}, u32[]{:S(2)}) collective-permute-start(bf16[128,256]{1,0:T(8,128)(2,1)S(1)} %collective-permute-done.18.refs_6_), channel_id=1, source_target_pairs={{0,1},{1,0},{2,3},{3,2},{4,5},{5,4},{6,7},{7,6},{8,9},{9,8},{10,11... | collective-permute-start | bytes 196616 | tf_op jit(solution)/shard_map/ppermute | solution.py:258
  54.5 1.3 %collective-permute-start.17 = (bf16[128,256]{1,0:T(8,128)(2,1)S(1)}, bf16[128,256]{1,0:T(8,128)(2,1)S(1)}, u32[]{:S(2)}, u32[]{:S(2)}) collective-permute-start(bf16[128,256]{1,0:T(8,128)(2,1)S(1)} %collective-permute-done.16.refs_4_), channel_id=1, source_target_pairs={{0,1},{1,0},{2,3},{3,2},{4,5},{5,4},{6,7},{7,6},{8,9},{9,8},{10,11... | collective-permute-start | bytes 196616 | tf_op jit(solution)/shard_map/ppermute | solution.py:258
  55.1 1.3 %collective-permute-start.15 = (bf16[128,256]{1,0:T(8,128)(2,1)S(1)}, bf16[128,256]{1,0:T(8,128)(2,1)S(1)}, u32[]{:S(2)}, u32[]{:S(2)}) collective-permute-start(bf16[128,256]{1,0:T(8,128)(2,1)S(1)} %collective-permute-done.14.refs_2_), channel_id=1, source_target_pairs={{0,1},{1,0},{2,3},{3,2},{4,5},{5,4},{6,7},{7,6},{8,9},{9,8},{10,11... | collective-permute-start | bytes 196616 | tf_op jit(solution)/shard_map/ppermute | solution.py:258
  57.6 7.0 %collective-permute-start.20 = (bf16[384,256]{1,0:T(8,128)(2,1)S(1)}, bf16[384,256]{1,0:T(8,128)(2,1)S(1)}, u32[]{:S(2)}, u32[]{:S(2)}) collective-permute-start(bf16[384,256]{1,0:T(8,128)(2,1)S(1)} %get-tuple-element.26), channel_id=1, source_target_pairs={{0,2},{1,3},{2,0},{3,1},{4,6},{5,7},{6,4},{7,5},{8,10},{9,11},{10,... | collective-permute-start | bytes 589832 | tf_op jit(solution)/shard_map/ppermute | solution.py:258
  58.2 8.0 %collective-permute-start.21 = (bf16[128,256]{1,0:T(8,128)(2,1)S(1)}, bf16[128,256]{1,0:T(8,128)(2,1)S(1)}, u32[]{:S(2)}, u32[]{:S(2)}) collective-permute-start(bf16[128,256]{1,0:T(8,128)(2,1)S(1)} %get-tuple-element.27), channel_id=1, source_target_pairs={{0,8},{1,9},{2,10},{3,11},{4,12},{5,13},{6,14},{7,15},{8,0},{9,1},... | collective-permute-start | bytes 196616 | tf_op jit(solution)/shard_map/ppermute | solution.py:258
  59.2 10.0 %collective-permute-start.22 = (bf16[128,256]{1,0:T(8,128)(2,1)S(1)}, bf16[128,256]{1,0:T(8,128)(2,1)S(1)}, u32[]{:S(2)}, u32[]{:S(2)}) collective-permute-start(bf16[128,256]{1,0:T(8,128)(2,1)S(1)} %get-tuple-element.28), channel_id=1, source_target_pairs={{0,10},{1,11},{2,8},{3,9},{4,14},{5,15},{6,12},{7,13},{8,2},{9,3},... | collective-permute-start | bytes 196616 | tf_op jit(solution)/shard_map/ppermute | solution.py:258
  64.7 5.3 %collective-permute-start.23 = (bf16[128,256]{1,0:T(8,128)(2,1)S(1)}, bf16[128,256]{1,0:T(8,128)(2,1)S(1)}, u32[]{:S(2)}, u32[]{:S(2)}) collective-permute-start(bf16[128,256]{1,0:T(8,128)(2,1)S(1)} %fusion), channel_id=1, source_target_pairs={{0,8},{1,9},{2,10},{3,11},{4,12},{5,13},{6,14},{7,15},{8,0},{9,1},... | collective-permute-start | bytes 196616 | tf_op jit(solution)/shard_map/ppermute | solution.py:258

commit v4 on v3

--- a/solution.py
+++ b/solution.py
@@ -28,15 +28,10 @@
         kv[part * share : (part + 1) * share, :] = kv_refs[part][...].reshape(share, 2 * head_dim)
     acc[...] = jnp.zeros_like(acc)
 
-    def invert(i, carry):
-        rel = jnp.bitwise_xor(i // 2, rank)
-        core_rel = rel % 2
-        mid_rel = (rel // 2) % mid
-        top_rel = rel // (2 * mid)
-        inverse[order[i]] = ((core_rel * mid + mid_rel) * top + top_rel) * rows + (i % 2) * half
-        return carry
-
-    lax.fori_loop(0, blocks, invert, 0)
+    for i in range(blocks):
+        rel = jnp.bitwise_xor(rank, i // 2)
+        part = (rel & 1) * mid + ((rel >> 1) & (mid - 1))
+        inverse[order[i]] = (part * top + (rel >> mid.bit_length())) * rows + (i % 2) * half
     ends = []
     total = 0
     for k in range(lengths.shape[1]):
@@ -55,12 +50,14 @@
             kw[w * half : (w + 1) * half, :] = kv[pl.ds(source, half), :]
         k = kw[:, :head_dim]
         v = kw[:, head_dim:]
-        kpos = first * half + lax.broadcasted_iota(jnp.int32, (span, lanes), 0)
-        qpos = block * half + lax.broadcasted_iota(jnp.int32, (1, lanes), 1) % half
-        start = jnp.zeros((1, lanes), jnp.int32)
+        tile = 2 * half
+        kpos = first * half + lax.broadcasted_iota(jnp.int32, (span, tile), 0)
+        qpos = block * half + lax.broadcasted_iota(jnp.int32, (1, tile), 1) % half
+        start = jnp.zeros((1, tile), jnp.int32)
         for end in ends:
             start = jnp.where(qpos >= end, end, start)
-        mask = (kpos <= qpos) & (kpos >= start)
+        hidden = jnp.where((kpos <= qpos) & (kpos >= start), 0.0, NEG)
+        hidden = jnp.concatenate([hidden] * (lanes // tile), axis=1)
         dk = jnp.zeros((span, head_dim), jnp.float32)
         dv = jnp.zeros((span, head_dim), jnp.float32)
         trows = slice(t * half, (t + 1) * half)
@@ -69,14 +66,14 @@
             q = jnp.concatenate([q_ref[trows, c] for c in cols], axis=0)
             d = jnp.concatenate([d_ref[trows, c] for c in cols], axis=0)
             s = lax.dot_general(k, q, NT, preferred_element_type=jnp.float32) * factor
-            s = jnp.where(mask, s, NEG)
+            s = s + hidden
             e = jnp.exp2(s - jnp.max(s, axis=0, keepdims=True))
             inv = 1.0 / jnp.sum(e, axis=0, keepdims=True)
+            dp = lax.dot_general(v, d, NT, preferred_element_type=jnp.float32)
+            delta = jnp.sum(e * dp, axis=0, keepdims=True) * inv
             p = e * inv
-            dp = lax.dot_general(v, d, NT, preferred_element_type=jnp.float32)
-            delta = jnp.sum(p * dp, axis=0, keepdims=True)
+            pb = p.astype(jnp.bfloat16)
             ds = (p * (dp - delta)).astype(jnp.bfloat16)
-            pb = p.astype(jnp.bfloat16)
             dv = dv + jnp.dot(pb, d, preferred_element_type=jnp.float32)
             dk = dk + jnp.dot(ds, q, preferred_element_type=jnp.float32)
             dq = lax.dot_general(k, ds, TN, preferred_element_type=jnp.float32) * scale
@@ -99,7 +96,7 @@
     heads = width // head_dim
     half = rows // 2
     blocks = order.shape[0]
-    window = min(blocks, 2 * ((blocks // 4 + 2) // 2))
+    window = min(blocks, blocks // 4 + 1)
     count = 2 * mid
     part = (top, rows, 2 * head_dim)
     body = functools.partial(
@@ -112,7 +109,7 @@
         half=half,
         blocks=blocks,
         window=window,
-        group=min(heads, 4),
+        group=min(heads, 8),
     )
     vmem = pl.BlockSpec(memory_space=pltpu.VMEM)
     smem = pl.BlockSpec(memory_space=pltpu.SMEM)
@@ -213,13 +210,35 @@
     )(x, *g_parts)
 
 
-def columns_kernel(x_ref, out_ref, *, places, height):
-    for (row, line), begin in places:
-        block = x_ref[:, begin : begin + height]
-        out_ref[row, line : line + height, :] = block.T
-
-
-def columns_first(x, members, spread, n, dps):
+def columns_kernel(x_hbm, _, out_hbm, x, xt, in_sems, out_sems, *, places, height):
+    rows, width = x.shape
+    step = width // in_sems.shape[0]
+
+    def load(c):
+        cols = pl.ds(c * step, step)
+        return pltpu.make_async_copy(x_hbm.at[:, cols], x.at[:, cols], in_sems.at[c])
+
+    def store(p):
+        (row, line), begin = places[p]
+        return pltpu.make_async_copy(
+            xt.at[pl.ds(begin, height)], out_hbm.at[row, pl.ds(line, height)], out_sems.at[p]
+        )
+
+    chunks = range(in_sems.shape[0])
+    for c in chunks:
+        load(c).start()
+    for c in chunks:
+        load(c).wait()
+        for begin in range(c * step, (c + 1) * step, 256):
+            xt[begin : begin + 256, :] = x[:, begin : begin + 256].T
+        for p, (_, begin) in enumerate(places):
+            if c * step <= begin < (c + 1) * step:
+                store(p).start()
+    for p in range(len(places)):
+        store(p).wait()
+
+
+def columns_first(x, early, members, spread, n, dps):
     rows, width = x.shape
     height = width // (n * dps)
     places = [
@@ -227,18 +246,24 @@
         for place, (i, m) in enumerate(members)
         for k, s in enumerate(spread)
     ]
-    vmem = pl.BlockSpec(memory_space=pltpu.VMEM)
+    hbm = pl.BlockSpec(memory_space=pltpu.HBM)
     return pl.pallas_call(
         functools.partial(columns_kernel, places=places, height=height),
         out_shape=jax.ShapeDtypeStruct((len(members), len(spread) * height, rows), x.dtype),
-        in_specs=[vmem],
-        out_specs=vmem,
+        in_specs=[hbm, pl.BlockSpec(memory_space=pl.ANY)],
+        out_specs=hbm,
+        scratch_shapes=[
+            pltpu.VMEM((rows, width), x.dtype),
+            pltpu.VMEM((width, rows), x.dtype),
+            pltpu.SemaphoreType.DMA((4,)),
+            pltpu.SemaphoreType.DMA((len(places),)),
+        ],
         cost_estimate=pl.CostEstimate(
             flops=0, bytes_accessed=4 * rows * width, transcendentals=0
         ),
-        compiler_params=pltpu.CompilerParams(vmem_limit_bytes=16 << 20),
+        compiler_params=pltpu.CompilerParams(vmem_limit_bytes=60 << 20),
         name="columns_first",
-    )(x)
+    )(x, early)
 
 
 def after(x, *earlier):
@@ -271,8 +296,8 @@
     tops = [kv] + [swap(kv, 2 * mid * j) for j in range(1, top)]
     base = jnp.stack(tops)
 
-    xt = columns_first(after(layer_input[0], kv), members, spread, n, dps)
-    base, xt = lax.optimization_barrier((base, xt))
+    xt = columns_first(layer_input[0], kv, members, spread, n, dps)
+    base = after(base, xt)
 
     near = [base] + [swap(base, 2 * j) for j in range(1, mid)]
     far = [swap(part, 1) for part in near]

time: 71.1 us -> 70.8 us (level)
  starting transfers between devices: 26 us -> 29.6 us
  local copies, waits for them, and re-layouts: 3.63 us -> 0.7 us
  waiting for transfers between devices: 31.4 us -> 29.6 us
  Pallas kernels: 7.19 us -> 8.04 us
    ppermute x21, starting transfers between devices: 18.8 us -> 22.3 us  [swap(): return lax.ppermute(x, 'ctx', [(i, i ^ k) for i in range(n)])]
    unnamed x12 -> x10, local copies, waits for them, and re-layouts: 2.96 us -> 0.03 us
    pallas_call x1, Pallas kernels: 0.59 us -> 2.94 us  [columns_first(): pl.pallas_call(functools.partial(columns_kernel, places=places, height=he...]
    pallas_call x1, Pallas kernels: 5.34 us -> 3.83 us  [attention(): pl.pallas_call(body, out_shape=[jax.ShapeDtypeStruct((rows, width), jnp.b...]
    ppermute x3, waiting for transfers between devices: 3.72 us -> 2.57 us  [cross(): lax.ppermute(x, joint, [(a * n + b, (a ^ i) * n + (b ^ m)) for a in range...]
    ppermute x21, waiting for transfers between devices: 27.7 us -> 27 us  [swap(): return lax.ppermute(x, 'ctx', [(i, i ^ k) for i in range(n)])]
  transfers between devices with their start and end apart: 25 -> 25, of which waited for: 16 -> 15; matrix products, arithmetic and copies ran while one was open for 1% -> 1% of each run, Pallas kernels for 8% -> 10%
where the time goes in v4:
time: 70.8 us; the launch traced here: 70.5 us
  starting transfers between devices  29.6 us (42%)
  waiting for transfers between devices  29.6 us (42%)
  Pallas kernels  8.04 us (11%)
  other arithmetic  1.82 us (3%)
  between operations  0.8 us (1%)
    ppermute x21, waiting for transfers between devices, swap(): return lax.ppermute(x, 'ctx', [(i, i ^ k) for i in range(n)])  27 us
    ppermute x21, starting transfers between devices, swap(): return lax.ppermute(x, 'ctx', [(i, i ^ k) for i in range(n)])  22.3 us
    pallas_call x1, Pallas kernels, attention(): pl.pallas_call(body, out_shape=[jax.ShapeDtypeStruct((rows, width), jnp.b...  3.83 us
    all_to_all x1, starting transfers between devices, per_device(): xt = lax.all_to_all(xt, joint, 0, 0, axis_index_groups=groups, tiled=True)  3.75 us
    ppermute x3, starting transfers between devices, cross(): lax.ppermute(x, joint, [(a * n + b, (a ^ i) * n + (b ^ m)) for a in range...  3.55 us
    pallas_call x1, Pallas kernels, columns_first(): pl.pallas_call(functools.partial(columns_kernel, places=places, height=he...  2.94 us
    ppermute x3, waiting for transfers between devices, cross(): lax.ppermute(x, joint, [(a * n + b, (a ^ i) * n + (b ^ m)) for a in range...  2.57 us
  transfers between devices with their start and end apart: 25, of which 15 were waited for; matrix products, arithmetic and copies ran while one was open for 1% of the time, Pallas kernels for 10%

profile of v4, /device:TPU:0, one launch (start us, length us, event | category | flops | bytes accessed | tf_op | source)
XLA Modules:
  0.0 70.5 jit_solution(8653646486309799409)
XLA Ops:
  0.6 0.8 %fusion.10 = (bf16[1,128,256]{2,1,0:T(8,128)(2,1)S(1)}, bf16[128,256]{1,0:T(8,128)(2,1)S(1)}) fusion(bf16[128,128]{1,0:T(8,128)(2,1)} %bitcast.43, bf16[128,128]{1,0:T(8,128)(2,1)} %bitcast.44), kind=kLoop, calls=%fused_computation.25 | loop fusion | flops 131072 | bytes 196608 | tf_op jit(solution)/shard_map/stack | solution.py:297
  1.4 0.0 copy-start.4
  1.4 5.1 %collective-permute-start.2 = (bf16[128,256]{1,0:T(8,128)(2,1)S(1)}, bf16[128,256]{1,0:T(8,128)(2,1)S(1)}, u32[]{:S(2)}, u32[]{:S(2)}) collective-permute-start(bf16[128,256]{1,0:T(8,128)(2,1)S(1)} %get-tuple-element.34._), channel_id=1, source_target_pairs={{0,12},{1,13},{2,14},{3,15},{4,8},{5,9},{6,10},{7,11},{8,4},{9,5},... | collective-permute-start | bytes 196616 | tf_op jit(solution)/shard_map/ppermute | solution.py:283
  6.5 0.0 collective-permute-start.1
  6.5 0.6 collective-permute-start
  7.2 2.9 %columns_first.1 = bf16[8,1024,128]{2,1,0:T(8,128)(2,1)} custom-call(bf16[128,8192]{1,0:T(8,128)(2,1)} %bitcast.39, bf16[128,256]{1,0:T(8,128)(2,1)} %copy-done.4), custom_call_target="tpu_custom_call" | custom-call | bytes 4194304 | tf_op jit(solution)/shard_map/columns_first/pallas_call | solution.py:250
  10.1 0.0 copy-start
  10.2 0.0 copy-start.1
  10.2 0.0 copy-start.2
  10.2 0.0 copy-start.3
  10.2 3.7 %all-to-all-start = ((bf16[8,1024,128]{2,1,0:T(8,128)(2,1)}), bf16[8,1024,128]{2,1,0:T(8,128)(2,1)S(1)}, u32[]{:S(2)}, u32[]{:S(2)}) async-start(bf16[8,1024,128]{2,1,0:T(8,128)(2,1)} %columns_first.1), calls=%async_computation | async-start | bytes 4194304 | tf_op jit(solution)/shard_map/all_to_all | solution.py:305
  13.9 0.0 collective-permute-done.2
  14.0 0.0 collective-permute-done.1
  14.0 0.0 collective-permute-done
  14.0 1.8 %collective-permute-start.3 = (bf16[4,128,256]{2,1,0:T(8,128)(2,1)S(1)}, bf16[4,128,256]{2,1,0:T(8,128)(2,1)S(1)}, u32[]{:S(2)}, u32[]{:S(2)}) collective-permute-start(bf16[4,128,256]{2,1,0:T(8,128)(2,1)S(1)} %pad_maximum_fusion.refs_0_), channel_id=1, source_target_pairs={{0,2},{1,3},{2,0},{3,1},{4,6},{5,7},{6,4},{7,5},{8,10},{9,11},{10,... | collective-permute-start | bytes 786440 | tf_op jit(solution)/shard_map/ppermute | solution.py:283
  15.8 0.1 collective-permute-start.4
  15.9 6.9 %collective-permute-done.3.refs_1_ = bf16[4,128,256]{2,1,0:T(8,128)(2,1)S(1)} collective-permute-done((bf16[4,128,256]{2,1,0:T(8,128)(2,1)S(1)}, bf16[4,128,256]{2,1,0:T(8,128)(2,1)S(1)}, u32[]{:S(2)}, u32[]{:S(2)}) %collective-permute-start.3) | collective-permute-done | bytes 262176 | tf_op jit(solution)/shard_map/ppermute | solution.py:283
  22.8 0.0 collective-permute-start.5
  22.8 0.0 collective-permute-done.4.refs_2_
  22.8 1.5 %collective-permute-done.5.refs_3_ = bf16[4,128,256]{2,1,0:T(8,128)(2,1)S(1)} collective-permute-done((bf16[4,128,256]{2,1,0:T(8,128)(2,1)S(1)}, bf16[4,128,256]{2,1,0:T(8,128)(2,1)S(1)}, u32[]{:S(2)}, u32[]{:S(2)}) %collective-permute-start.5) | collective-permute-done | bytes 262176 | tf_op jit(solution)/shard_map/ppermute | solution.py:283
  24.3 3.8 %attention_grads.1 = (bf16[128,1024]{1,0:T(8,128)(2,1)}, f32[4,128,256]{2,1,0:T(8,128)S(1)}, bf16[4,128,256]{2,1,0:T(8,128)(2,1)S(1)}, bf16[4,128,256]{2,1,0:T(8,128)(2,1)S(1)}, bf16[4,128,256]{2,1,0:T(8,128)(2,1)S(1)}) custom-call(s32[32]{0:T(128)S(1)} %copy-done.2, s32[1,8]{1,0:T(1,128)S(1)} %copy-done.3, bf16[128,1024]{1,0:T(8,128)(2,1)S(1)} %bitcast.37, ...), custom_call_target="tpu_custom_call" | custom-call | flops 15099494400 | bytes 4194304 | tf_op jit(solution)/shard_map/attention_grads/pallas_call | solution.py:117
  28.2 0.1 collective-permute-start.7
  28.3 0.4 collective-permute-start.6
  28.7 1.0 %collective-permute-done.7 = bf16[4,128,256]{2,1,0:T(8,128)(2,1)S(1)} collective-permute-done((bf16[4,128,256]{2,1,0:T(8,128)(2,1)S(1)}, bf16[4,128,256]{2,1,0:T(8,128)(2,1)S(1)}, u32[]{:S(2)}, u32[]{:S(2)}) %collective-permute-start.7) | collective-permute-done | bytes 262176 | tf_op jit(solution)/shard_map/ppermute | solution.py:283
  29.7 0.1 add_convert_fusion
  29.8 1.7 %collective-permute-start.9 = (bf16[3,128,256]{2,1,0:T(8,128)(2,1)S(1)}, bf16[3,128,256]{2,1,0:T(8,128)(2,1)S(1)}, u32[]{:S(2)}, u32[]{:S(2)}) collective-permute-start(bf16[3,128,256]{2,1,0:T(8,128)(2,1)S(1)} %slice.67), channel_id=1, source_target_pairs={{0,2},{1,3},{2,0},{3,1},{4,6},{5,7},{6,4},{7,5},{8,10},{9,11},{10,... | collective-permute-start | bytes 589832 | tf_op jit(solution)/shard_map/ppermute | solution.py:283
  31.4 0.4 collective-permute-start.8
  31.9 0.0 collective-permute-done.6
  31.9 5.6 %collective-permute-done.9 = bf16[3,128,256]{2,1,0:T(8,128)(2,1)S(1)} collective-permute-done((bf16[3,128,256]{2,1,0:T(8,128)(2,1)S(1)}, bf16[3,128,256]{2,1,0:T(8,128)(2,1)S(1)}, u32[]{:S(2)}, u32[]{:S(2)}) %collective-permute-start.9) | collective-permute-done | bytes 196640 | tf_op jit(solution)/shard_map/ppermute | solution.py:283
  37.5 0.1 add_convert_fusion.1
  37.6 1.7 %collective-permute-start.10 = (bf16[128,256]{1,0:T(8,128)(2,1)S(1)}, bf16[128,256]{1,0:T(8,128)(2,1)S(1)}, u32[]{:S(2)}, u32[]{:S(2)}) collective-permute-start(bf16[128,256]{1,0:T(8,128)(2,1)S(1)} %get-tuple-element.28), channel_id=1, source_target_pairs={{0,4},{1,5},{2,6},{3,7},{4,0},{5,1},{6,2},{7,3},{8,12},{9,13},{10,... | collective-permute-start | bytes 196616 | tf_op jit(solution)/shard_map/ppermute | solution.py:283
  39.3 2.7 %collective-permute-start.12 = (bf16[128,256]{1,0:T(8,128)(2,1)S(1)}, bf16[128,256]{1,0:T(8,128)(2,1)S(1)}, u32[]{:S(2)}, u32[]{:S(2)}) collective-permute-start(bf16[128,256]{1,0:T(8,128)(2,1)S(1)} %get-tuple-element.29), channel_id=1, source_target_pairs={{0,12},{1,13},{2,14},{3,15},{4,8},{5,9},{6,10},{7,11},{8,4},{9,5},... | collective-permute-start | bytes 196616 | tf_op jit(solution)/shard_map/ppermute | solution.py:283
  42.0 0.2 collective-permute-start.11
  42.2 0.0 collective-permute-done.8
  42.2 0.0 collective-permute-done.10
  42.3 3.5 %collective-permute-done.12 = bf16[128,256]{1,0:T(8,128)(2,1)S(1)} collective-permute-done((bf16[128,256]{1,0:T(8,128)(2,1)S(1)}, bf16[128,256]{1,0:T(8,128)(2,1)S(1)}, u32[]{:S(2)}, u32[]{:S(2)}) %collective-permute-start.12) | collective-permute-done | bytes 65568 | tf_op jit(solution)/shard_map/ppermute | solution.py:283
  45.8 2.1 %collective-permute-done.11 = bf16[128,256]{1,0:T(8,128)(2,1)S(1)} collective-permute-done((bf16[128,256]{1,0:T(8,128)(2,1)S(1)}, bf16[128,256]{1,0:T(8,128)(2,1)S(1)}, u32[]{:S(2)}, u32[]{:S(2)}) %collective-permute-start.11) | collective-permute-done | bytes 65568 | tf_op jit(solution)/shard_map/ppermute | solution.py:283
  47.9 0.1 fusion.9.refs_0_
  48.0 1.1 %collective-permute-start.18 = (bf16[128,256]{1,0:T(8,128)(2,1)S(1)}, bf16[128,256]{1,0:T(8,128)(2,1)S(1)}, u32[]{:S(2)}, u32[]{:S(2)}) collective-permute-start(bf16[128,256]{1,0:T(8,128)(2,1)S(1)} %fusion.9.refs_0_), channel_id=1, source_target_pairs={{0,20},{1,21},{2,22},{3,23},{4,16},{5,17},{6,18},{7,19},{8,28},{9,... | collective-permute-start | bytes 196616 | tf_op jit(solution)/shard_map/ppermute | solution.py:291
  49.1 0.7 collective-permute-start.16
  49.8 1.7 %collective-permute-start.14 = (bf16[128,256]{1,0:T(8,128)(2,1)S(1)}, bf16[128,256]{1,0:T(8,128)(2,1)S(1)}, u32[]{:S(2)}, u32[]{:S(2)}) collective-permute-start(bf16[128,256]{1,0:T(8,128)(2,1)S(1)} %fusion.9.refs_0_), channel_id=1, source_target_pairs={{0,4},{1,5},{2,6},{3,7},{4,0},{5,1},{6,2},{7,3},{8,12},{9,13},{10,... | collective-permute-start | bytes 196616 | tf_op jit(solution)/shard_map/ppermute | solution.py:291
  51.5 0.0 collective-permute-start.13
  51.5 1.7 %collective-permute-done.18.refs_6_ = bf16[128,256]{1,0:T(8,128)(2,1)S(1)} collective-permute-done((bf16[128,256]{1,0:T(8,128)(2,1)S(1)}, bf16[128,256]{1,0:T(8,128)(2,1)S(1)}, u32[]{:S(2)}, u32[]{:S(2)}) %collective-permute-start.18) | collective-permute-done | bytes 65568 | tf_op jit(solution)/shard_map/ppermute | solution.py:291
  53.2 0.0 collective-permute-start.19
  53.2 0.6 collective-permute-done.16.refs_4_
  53.9 0.0 collective-permute-start.17
  53.9 0.2 collective-permute-done.14.refs_2_
  54.1 0.3 collective-permute-start.15
  54.4 0.0 collective-permute-done.13.refs_1_
  54.4 0.1 collective-permute-done.19.refs_7_
  54.5 0.6 collective-permute-done.17.refs_5_
  55.1 0.2 collective-permute-done.15.refs_3_
  55.3 1.3 %weight_terms.1 = (f32[256,256]{1,0:T(8,128)S(1)}, bf16[384,256]{1,0:T(8,128)(2,1)S(1)}, bf16[128,256]{1,0:T(8,128)(2,1)S(1)}, bf16[128,256]{1,0:T(8,128)(2,1)S(1)}, f32[128,256]{1,0:T(8,128)S(1)}) custom-call(bf16[8,1024,128]{2,1,0:T(8,128)(2,1)S(1)} %all-to-all-done.x_ref, bf16[128,256]{1,0:T(8,128)(2,1)S(1)} %fusion.9.refs_0_, ...), custom_call_target="tpu_custom_call" | custom-call | flops 536870912 | bytes 4194304 | tf_op jit(solution)/shard_map/weight_terms/pallas_call | solution.py:199
  56.6 1.6 %collective-permute-start.20 = (bf16[384,256]{1,0:T(8,128)(2,1)S(1)}, bf16[384,256]{1,0:T(8,128)(2,1)S(1)}, u32[]{:S(2)}, u32[]{:S(2)}) collective-permute-start(bf16[384,256]{1,0:T(8,128)(2,1)S(1)} %get-tuple-element.22), channel_id=1, source_target_pairs={{0,2},{1,3},{2,0},{3,1},{4,6},{5,7},{6,4},{7,5},{8,10},{9,11},{10,... | collective-permute-start | bytes 589832 | tf_op jit(solution)/shard_map/ppermute | solution.py:283
  58.2 2.0 %collective-permute-start.21 = (bf16[128,256]{1,0:T(8,128)(2,1)S(1)}, bf16[128,256]{1,0:T(8,128)(2,1)S(1)}, u32[]{:S(2)}, u32[]{:S(2)}) collective-permute-start(bf16[128,256]{1,0:T(8,128)(2,1)S(1)} %get-tuple-element.23), channel_id=1, source_target_pairs={{0,8},{1,9},{2,10},{3,11},{4,12},{5,13},{6,14},{7,15},{8,0},{9,1},... | collective-permute-start | bytes 196616 | tf_op jit(solution)/shard_map/ppermute | solution.py:283
  60.2 0.9 %collective-permute-start.22 = (bf16[128,256]{1,0:T(8,128)(2,1)S(1)}, bf16[128,256]{1,0:T(8,128)(2,1)S(1)}, u32[]{:S(2)}, u32[]{:S(2)}) collective-permute-start(bf16[128,256]{1,0:T(8,128)(2,1)S(1)} %get-tuple-element.24), channel_id=1, source_target_pairs={{0,10},{1,11},{2,8},{3,9},{4,14},{5,15},{6,12},{7,13},{8,2},{9,3},... | collective-permute-start | bytes 196616 | tf_op jit(solution)/shard_map/ppermute | solution.py:283
  61.1 2.7 %collective-permute-done.20 = bf16[384,256]{1,0:T(8,128)(2,1)S(1)} collective-permute-done((bf16[384,256]{1,0:T(8,128)(2,1)S(1)}, bf16[384,256]{1,0:T(8,128)(2,1)S(1)}, u32[]{:S(2)}, u32[]{:S(2)}) %collective-permute-start.20) | collective-permute-done | bytes 196640 | tf_op jit(solution)/shard_map/ppermute | solution.py:283
  63.9 2.6 %collective-permute-start.23 = (bf16[128,256]{1,0:T(8,128)(2,1)S(1)}, bf16[128,256]{1,0:T(8,128)(2,1)S(1)}, u32[]{:S(2)}, u32[]{:S(2)}) collective-permute-start(bf16[128,256]{1,0:T(8,128)(2,1)S(1)} %fusion), channel_id=1, source_target_pairs={{0,8},{1,9},{2,10},{3,11},{4,12},{5,13},{6,14},{7,15},{8,0},{9,1},... | collective-permute-start | bytes 196616 | tf_op jit(solution)/shard_map/ppermute | solution.py:283
  66.5 0.6 slice_bitcast_fusion.4
  67.1 0.0 collective-permute-done.21
  67.1 0.4 collective-permute-done.22
  67.5 2.2 %collective-permute-done.23 = bf16[128,256]{1,0:T(8,128)(2,1)S(1)} collective-permute-done((bf16[128,256]{1,0:T(8,128)(2,1)S(1)}, bf16[128,256]{1,0:T(8,128)(2,1)S(1)}, u32[]{:S(2)}, u32[]{:S(2)}) %collective-permute-start.23) | collective-permute-done | bytes 65568 | tf_op jit(solution)/shard_map/ppermute | solution.py:283
  69.7 0.1 fusion.5
  69.7 0.7 %maximum_multiply_fusion = f32[1,256,256]{2,1,0:T(8,128)} fusion(f32[1,128,256]{2,1,0:T(8,128)S(1)} %get-tuple-element.27, f32[1,128,256]{2,1,0:T(8,128)S(1)} %get-tuple-element.26), kind=kLoop, calls=%fused_computation.3 | loop fusion | flops 131072 | bytes 524288 | tf_op jit(solution)/shard_map/mul | solution.py:346
  (12 shorter events, 0.1 us)
Async XLA Ops:
  1.4 5.8 %copy-start.4 = (bf16[128,256]{1,0:T(8,128)(2,1)}, bf16[128,256]{1,0:T(8,128)(2,1)S(1)}, u32[]{:S(2)}) copy-start(bf16[128,256]{1,0:T(8,128)(2,1)S(1)} %get-tuple-element.34._) | copy-start | bytes 196612
  1.4 12.5 %collective-permute-start.2 = (bf16[128,256]{1,0:T(8,128)(2,1)S(1)}, bf16[128,256]{1,0:T(8,128)(2,1)S(1)}, u32[]{:S(2)}, u32[]{:S(2)}) collective-permute-start(bf16[128,256]{1,0:T(8,128)(2,1)S(1)} %get-tuple-element.34._), channel_id=1, source_target_pairs={{0,12},{1,13},{2,14},{3,15},{4,8},{5,9},{6,10},{7,11},{8,4},{9,5},... | collective-permute-start | bytes 196616 | tf_op jit(solution)/shard_map/ppermute | solution.py:283
  6.5 7.4 %collective-permute-start.1 = (bf16[128,256]{1,0:T(8,128)(2,1)S(1)}, bf16[128,256]{1,0:T(8,128)(2,1)S(1)}, u32[]{:S(2)}, u32[]{:S(2)}) collective-permute-start(bf16[128,256]{1,0:T(8,128)(2,1)S(1)} %get-tuple-element.34._), channel_id=1, source_target_pairs={{0,8},{1,9},{2,10},{3,11},{4,12},{5,13},{6,14},{7,15},{8,0},{9,1},... | collective-permute-start | bytes 196616 | tf_op jit(solution)/shard_map/ppermute | solution.py:283
  6.5 7.4 %collective-permute-start = (bf16[128,256]{1,0:T(8,128)(2,1)S(1)}, bf16[128,256]{1,0:T(8,128)(2,1)S(1)}, u32[]{:S(2)}, u32[]{:S(2)}) collective-permute-start(bf16[128,256]{1,0:T(8,128)(2,1)S(1)} %get-tuple-element.34._), channel_id=1, source_target_pairs={{0,4},{1,5},{2,6},{3,7},{4,0},{5,1},{6,2},{7,3},{8,12},{9,13},{10,... | collective-permute-start | bytes 196616 | tf_op jit(solution)/shard_map/ppermute | solution.py:283
  10.1 14.2 %copy-start = (bf16[1,128,1024]{2,1,0:T(8,128)(2,1)S(1)}, bf16[1,128,1024]{2,1,0:T(8,128)(2,1)}, u32[]{:S(2)}) copy-start(bf16[1,128,1024]{2,1,0:T(8,128)(2,1)} %param.8) | copy-start | bytes 786436
  10.2 14.2 %copy-start.1 = (bf16[1,128,1024]{2,1,0:T(8,128)(2,1)S(1)}, bf16[1,128,1024]{2,1,0:T(8,128)(2,1)}, u32[]{:S(2)}) copy-start(bf16[1,128,1024]{2,1,0:T(8,128)(2,1)} %param.11) | copy-start | bytes 786436
  10.2 14.1 %copy-start.2 = (s32[32]{0:T(128)S(1)}, s32[32]{0:T(128)}, u32[]{:S(2)}) copy-start(s32[32]{0:T(128)} %order.1) | copy-start | bytes 388
  10.2 14.1 %copy-start.3 = (s32[1,8]{1,0:T(1,128)S(1)}, s32[1,8]{1,0:T(1,128)}, u32[]{:S(2)}) copy-start(s32[1,8]{1,0:T(1,128)} %lengths.1) | copy-start | bytes 100
  10.2 45.2 %all-to-all-start = ((bf16[8,1024,128]{2,1,0:T(8,128)(2,1)}), bf16[8,1024,128]{2,1,0:T(8,128)(2,1)S(1)}, u32[]{:S(2)}, u32[]{:S(2)}) async-start(bf16[8,1024,128]{2,1,0:T(8,128)(2,1)} %columns_first.1), calls=%async_computation | async-start | bytes 4194304 | tf_op jit(solution)/shard_map/all_to_all | solution.py:305
  14.0 8.8 %collective-permute-start.3 = (bf16[4,128,256]{2,1,0:T(8,128)(2,1)S(1)}, bf16[4,128,256]{2,1,0:T(8,128)(2,1)S(1)}, u32[]{:S(2)}, u32[]{:S(2)}) collective-permute-start(bf16[4,128,256]{2,1,0:T(8,128)(2,1)S(1)} %pad_maximum_fusion.refs_0_), channel_id=1, source_target_pairs={{0,2},{1,3},{2,0},{3,1},{4,6},{5,7},{6,4},{7,5},{8,10},{9,11},{10,... | collective-permute-start | bytes 786440 | tf_op jit(solution)/shard_map/ppermute | solution.py:283
  15.8 7.0 %collective-permute-start.4 = (bf16[4,128,256]{2,1,0:T(8,128)(2,1)S(1)}, bf16[4,128,256]{2,1,0:T(8,128)(2,1)S(1)}, u32[]{:S(2)}, u32[]{:S(2)}) collective-permute-start(bf16[4,128,256]{2,1,0:T(8,128)(2,1)S(1)} %pad_maximum_fusion.refs_0_), channel_id=1, source_target_pairs={{0,1},{1,0},{2,3},{3,2},{4,5},{5,4},{6,7},{7,6},{8,9},{9,8},{10,11... | collective-permute-start | bytes 786440 | tf_op jit(solution)/shard_map/ppermute | solution.py:283
  22.8 1.5 %collective-permute-start.5 = (bf16[4,128,256]{2,1,0:T(8,128)(2,1)S(1)}, bf16[4,128,256]{2,1,0:T(8,128)(2,1)S(1)}, u32[]{:S(2)}, u32[]{:S(2)}) collective-permute-start(bf16[4,128,256]{2,1,0:T(8,128)(2,1)S(1)} %collective-permute-done.3.refs_1_), channel_id=1, source_target_pairs={{0,1},{1,0},{2,3},{3,2},{4,5},{5,4},{6,7},{7,6},{8,9},{9,8},{10,11... | collective-permute-start | bytes 786440 | tf_op jit(solution)/shard_map/ppermute | solution.py:283
  28.2 1.5 %collective-permute-start.7 = (bf16[4,128,256]{2,1,0:T(8,128)(2,1)S(1)}, bf16[4,128,256]{2,1,0:T(8,128)(2,1)S(1)}, u32[]{:S(2)}, u32[]{:S(2)}) collective-permute-start(bf16[4,128,256]{2,1,0:T(8,128)(2,1)S(1)} %get-tuple-element.20), channel_id=1, source_target_pairs={{0,1},{1,0},{2,3},{3,2},{4,5},{5,4},{6,7},{7,6},{8,9},{9,8},{10,11... | collective-permute-start | bytes 786440 | tf_op jit(solution)/shard_map/ppermute | solution.py:283
  28.3 3.6 %collective-permute-start.6 = (bf16[4,128,256]{2,1,0:T(8,128)(2,1)S(1)}, bf16[4,128,256]{2,1,0:T(8,128)(2,1)S(1)}, u32[]{:S(2)}, u32[]{:S(2)}) collective-permute-start(bf16[4,128,256]{2,1,0:T(8,128)(2,1)S(1)} %get-tuple-element.18), channel_id=1, source_target_pairs={{0,1},{1,0},{2,3},{3,2},{4,5},{5,4},{6,7},{7,6},{8,9},{9,8},{10,11... | collective-permute-start | bytes 786440 | tf_op jit(solution)/shard_map/ppermute | solution.py:283
  29.8 7.7 %collective-permute-start.9 = (bf16[3,128,256]{2,1,0:T(8,128)(2,1)S(1)}, bf16[3,128,256]{2,1,0:T(8,128)(2,1)S(1)}, u32[]{:S(2)}, u32[]{:S(2)}) collective-permute-start(bf16[3,128,256]{2,1,0:T(8,128)(2,1)S(1)} %slice.67), channel_id=1, source_target_pairs={{0,2},{1,3},{2,0},{3,1},{4,6},{5,7},{6,4},{7,5},{8,10},{9,11},{10,... | collective-permute-start | bytes 589832 | tf_op jit(solution)/shard_map/ppermute | solution.py:283
  31.4 10.8 %collective-permute-start.8 = (bf16[128,256]{1,0:T(8,128)(2,1)S(1)}, bf16[128,256]{1,0:T(8,128)(2,1)S(1)}, u32[]{:S(2)}, u32[]{:S(2)}) collective-permute-start(bf16[128,256]{1,0:T(8,128)(2,1)S(1)} %slice_bitcast_fusion.3), channel_id=1, source_target_pairs={{0,2},{1,3},{2,0},{3,1},{4,6},{5,7},{6,4},{7,5},{8,10},{9,11},{10,... | collective-permute-start | bytes 196616 | tf_op jit(solution)/shard_map/ppermute | solution.py:283
  37.6 4.7 %collective-permute-start.10 = (bf16[128,256]{1,0:T(8,128)(2,1)S(1)}, bf16[128,256]{1,0:T(8,128)(2,1)S(1)}, u32[]{:S(2)}, u32[]{:S(2)}) collective-permute-start(bf16[128,256]{1,0:T(8,128)(2,1)S(1)} %get-tuple-element.28), channel_id=1, source_target_pairs={{0,4},{1,5},{2,6},{3,7},{4,0},{5,1},{6,2},{7,3},{8,12},{9,13},{10,... | collective-permute-start | bytes 196616 | tf_op jit(solution)/shard_map/ppermute | solution.py:283
  39.3 6.5 %collective-permute-start.12 = (bf16[128,256]{1,0:T(8,128)(2,1)S(1)}, bf16[128,256]{1,0:T(8,128)(2,1)S(1)}, u32[]{:S(2)}, u32[]{:S(2)}) collective-permute-start(bf16[128,256]{1,0:T(8,128)(2,1)S(1)} %get-tuple-element.29), channel_id=1, source_target_pairs={{0,12},{1,13},{2,14},{3,15},{4,8},{5,9},{6,10},{7,11},{8,4},{9,5},... | collective-permute-start | bytes 196616 | tf_op jit(solution)/shard_map/ppermute | solution.py:283
  42.0 5.9 %collective-permute-start.11 = (bf16[128,256]{1,0:T(8,128)(2,1)S(1)}, bf16[128,256]{1,0:T(8,128)(2,1)S(1)}, u32[]{:S(2)}, u32[]{:S(2)}) collective-permute-start(bf16[128,256]{1,0:T(8,128)(2,1)S(1)} %get-tuple-element.30), channel_id=1, source_target_pairs={{0,8},{1,9},{2,10},{3,11},{4,12},{5,13},{6,14},{7,15},{8,0},{9,1},... | collective-permute-start | bytes 196616 | tf_op jit(solution)/shard_map/ppermute | solution.py:283
  48.0 5.3 %collective-permute-start.18 = (bf16[128,256]{1,0:T(8,128)(2,1)S(1)}, bf16[128,256]{1,0:T(8,128)(2,1)S(1)}, u32[]{:S(2)}, u32[]{:S(2)}) collective-permute-start(bf16[128,256]{1,0:T(8,128)(2,1)S(1)} %fusion.9.refs_0_), channel_id=1, source_target_pairs={{0,20},{1,21},{2,22},{3,23},{4,16},{5,17},{6,18},{7,19},{8,28},{9,... | collective-permute-start | bytes 196616 | tf_op jit(solution)/shard_map/ppermute | solution.py:291
  49.1 4.8 %collective-permute-start.16 = (bf16[128,256]{1,0:T(8,128)(2,1)S(1)}, bf16[128,256]{1,0:T(8,128)(2,1)S(1)}, u32[]{:S(2)}, u32[]{:S(2)}) collective-permute-start(bf16[128,256]{1,0:T(8,128)(2,1)S(1)} %fusion.9.refs_0_), channel_id=1, source_target_pairs={{0,16},{1,17},{2,18},{3,19},{4,20},{5,21},{6,22},{7,23},{8,24},{9,... | collective-permute-start | bytes 196616 | tf_op jit(solution)/shard_map/ppermute | solution.py:291
  49.8 4.3 %collective-permute-start.14 = (bf16[128,256]{1,0:T(8,128)(2,1)S(1)}, bf16[128,256]{1,0:T(8,128)(2,1)S(1)}, u32[]{:S(2)}, u32[]{:S(2)}) collective-permute-start(bf16[128,256]{1,0:T(8,128)(2,1)S(1)} %fusion.9.refs_0_), channel_id=1, source_target_pairs={{0,4},{1,5},{2,6},{3,7},{4,0},{5,1},{6,2},{7,3},{8,12},{9,13},{10,... | collective-permute-start | bytes 196616 | tf_op jit(solution)/shard_map/ppermute | solution.py:291
  51.5 2.9 %collective-permute-start.13 = (bf16[128,256]{1,0:T(8,128)(2,1)S(1)}, bf16[128,256]{1,0:T(8,128)(2,1)S(1)}, u32[]{:S(2)}, u32[]{:S(2)}) collective-permute-start(bf16[128,256]{1,0:T(8,128)(2,1)S(1)} %fusion.9.refs_0_), channel_id=1, source_target_pairs={{0,1},{1,0},{2,3},{3,2},{4,5},{5,4},{6,7},{7,6},{8,9},{9,8},{10,11... | collective-permute-start | bytes 196616 | tf_op jit(solution)/shard_map/ppermute | solution.py:283
  53.2 1.3 %collective-permute-start.19 = (bf16[128,256]{1,0:T(8,128)(2,1)S(1)}, bf16[128,256]{1,0:T(8,128)(2,1)S(1)}, u32[]{:S(2)}, u32[]{:S(2)}) collective-permute-start(bf16[128,256]{1,0:T(8,128)(2,1)S(1)} %collective-permute-done.18.refs_6_), channel_id=1, source_target_pairs={{0,1},{1,0},{2,3},{3,2},{4,5},{5,4},{6,7},{7,6},{8,9},{9,8},{10,11... | collective-permute-start | bytes 196616 | tf_op jit(solution)/shard_map/ppermute | solution.py:283
  53.9 1.3 %collective-permute-start.17 = (bf16[128,256]{1,0:T(8,128)(2,1)S(1)}, bf16[128,256]{1,0:T(8,128)(2,1)S(1)}, u32[]{:S(2)}, u32[]{:S(2)}) collective-permute-start(bf16[128,256]{1,0:T(8,128)(2,1)S(1)} %collective-permute-done.16.refs_4_), channel_id=1, source_target_pairs={{0,1},{1,0},{2,3},{3,2},{4,5},{5,4},{6,7},{7,6},{8,9},{9,8},{10,11... | collective-permute-start | bytes 196616 | tf_op jit(solution)/shard_map/ppermute | solution.py:283
  54.1 1.3 %collective-permute-start.15 = (bf16[128,256]{1,0:T(8,128)(2,1)S(1)}, bf16[128,256]{1,0:T(8,128)(2,1)S(1)}, u32[]{:S(2)}, u32[]{:S(2)}) collective-permute-start(bf16[128,256]{1,0:T(8,128)(2,1)S(1)} %collective-permute-done.14.refs_2_), channel_id=1, source_target_pairs={{0,1},{1,0},{2,3},{3,2},{4,5},{5,4},{6,7},{7,6},{8,9},{9,8},{10,11... | collective-permute-start | bytes 196616 | tf_op jit(solution)/shard_map/ppermute | solution.py:283
  56.6 7.2 %collective-permute-start.20 = (bf16[384,256]{1,0:T(8,128)(2,1)S(1)}, bf16[384,256]{1,0:T(8,128)(2,1)S(1)}, u32[]{:S(2)}, u32[]{:S(2)}) collective-permute-start(bf16[384,256]{1,0:T(8,128)(2,1)S(1)} %get-tuple-element.22), channel_id=1, source_target_pairs={{0,2},{1,3},{2,0},{3,1},{4,6},{5,7},{6,4},{7,5},{8,10},{9,11},{10,... | collective-permute-start | bytes 589832 | tf_op jit(solution)/shard_map/ppermute | solution.py:283
  58.2 8.9 %collective-permute-start.21 = (bf16[128,256]{1,0:T(8,128)(2,1)S(1)}, bf16[128,256]{1,0:T(8,128)(2,1)S(1)}, u32[]{:S(2)}, u32[]{:S(2)}) collective-permute-start(bf16[128,256]{1,0:T(8,128)(2,1)S(1)} %get-tuple-element.23), channel_id=1, source_target_pairs={{0,8},{1,9},{2,10},{3,11},{4,12},{5,13},{6,14},{7,15},{8,0},{9,1},... | collective-permute-start | bytes 196616 | tf_op jit(solution)/shard_map/ppermute | solution.py:283
  60.2 7.3 %collective-permute-start.22 = (bf16[128,256]{1,0:T(8,128)(2,1)S(1)}, bf16[128,256]{1,0:T(8,128)(2,1)S(1)}, u32[]{:S(2)}, u32[]{:S(2)}) collective-permute-start(bf16[128,256]{1,0:T(8,128)(2,1)S(1)} %get-tuple-element.24), channel_id=1, source_target_pairs={{0,10},{1,11},{2,8},{3,9},{4,14},{5,15},{6,12},{7,13},{8,2},{9,3},... | collective-permute-start | bytes 196616 | tf_op jit(solution)/shard_map/ppermute | solution.py:283
  63.9 5.8 %collective-permute-start.23 = (bf16[128,256]{1,0:T(8,128)(2,1)S(1)}, bf16[128,256]{1,0:T(8,128)(2,1)S(1)}, u32[]{:S(2)}, u32[]{:S(2)}) collective-permute-start(bf16[128,256]{1,0:T(8,128)(2,1)S(1)} %fusion), channel_id=1, source_target_pairs={{0,8},{1,9},{2,10},{3,11},{4,12},{5,13},{6,14},{7,15},{8,0},{9,1},... | collective-permute-start | bytes 196616 | tf_op jit(solution)/shard_map/ppermute | solution.py:283

commit v5 on v4

--- a/solution.py
+++ b/solution.py
@@ -130,17 +130,17 @@
             pltpu.SMEM((blocks,), jnp.int32),
         ],
         cost_estimate=pl.CostEstimate(
-            flops=200 * elements * head_dim, bytes_accessed=4 << 20, transcendentals=elements
+            flops=220 * elements * head_dim, bytes_accessed=4 << 20, transcendentals=elements
         ),
         compiler_params=pltpu.CompilerParams(vmem_limit_bytes=40 << 20),
         name="attention_grads",
     )(order, lengths, q, d, *kv_parts)
 
 
-def weight_kernel(x_ref, *refs, members, spread):
+def weight_kernel(x_ref, *refs, members, spread, close):
     count = len(members)
     g_refs = refs[:count]
-    keep, near, *rest = refs[count:-1]
+    out_refs = refs[count:-1]
     g_all = refs[-1]
     mask = members[-1][1]
     my_dp, my_ctx = lax.axis_index("dp"), lax.axis_index("ctx")
@@ -170,19 +170,23 @@
             )
         return total
 
-    near[:height, :] = terms(2).astype(near.dtype)
+    if close:
+        keep, near = out_refs
+        near[...] = terms(2).astype(near.dtype)
+        keep[...] = terms(0)
+        return
+    relay, *rest = out_refs
     for k, s in enumerate(far):
         straight, across, later = rest[3 * k : 3 * k + 3]
         total = terms(s | 2)
         across[...] = total[:part].astype(across.dtype)
-        near[height + k * part : height + (k + 1) * part, :] = total[part:].astype(near.dtype)
+        relay[k * part : (k + 1) * part, :] = total[part:].astype(relay.dtype)
         total = terms(s)
         straight[...] = total[:part].astype(straight.dtype)
         later[...] = total[part:]
-    keep[...] = terms(0)
-
-
-def weight_terms(x, g_parts, members, spread):
+
+
+def weight_terms(x, g_parts, members, spread, close):
     count, height, rows = x.shape
     width = g_parts[0].shape[1]
     vmem = pl.BlockSpec(memory_space=pltpu.VMEM)
@@ -191,19 +195,21 @@
     far = len(spread) // 2 - 1
     out = [
         jax.ShapeDtypeStruct((height, width), jnp.float32),
-        jax.ShapeDtypeStruct((height + far * part, width), jnp.bfloat16),
+        jax.ShapeDtypeStruct((height, width), jnp.bfloat16),
     ]
-    for _ in range(far):
+    if not close:
+        out = [jax.ShapeDtypeStruct((far * part, width), jnp.bfloat16)]
+    for _ in range(0 if close else far):
         out += [jax.ShapeDtypeStruct((part, width), jnp.bfloat16)] * 2
         out += [jax.ShapeDtypeStruct((part, width), jnp.float32)]
     return pl.pallas_call(
-        functools.partial(weight_kernel, members=members, spread=spread),
+        functools.partial(weight_kernel, members=members, spread=spread, close=close),
         out_shape=out,
         in_specs=[vmem] * (count + 1),
         out_specs=[vmem] * len(out),
         scratch_shapes=[pltpu.VMEM((count * rows, width), jnp.bfloat16)],
         cost_estimate=pl.CostEstimate(
-            flops=2 * x.size * width, bytes_accessed=4 << 20, transcendentals=0
+            flops=x.size * width, bytes_accessed=4 << 20, transcendentals=0
         ),
         compiler_params=pltpu.CompilerParams(vmem_limit_bytes=24 << 20),
         name="weight_terms",
@@ -330,17 +336,20 @@
         if m & 1:
             gathered[i, m] = swap(gathered[i, m ^ 1], 1)
 
-    keep, close, *rest = weight_terms(xt, [gathered[k] for k in members], members, spread)
+    terms = functools.partial(weight_terms, xt, [gathered[k] for k in members], members, spread)
+    relay, *rest = terms(False)
+    keep, close = terms(True)
     height = keep.shape[0]
     part = height // 2
-    came = swap(close, 2).astype(jnp.float32)
-    upper = keep[:part] + came[:part]
-    lower = keep[part:] + came[part:height]
+    came = swap(relay, 2).astype(jnp.float32)
+    close = swap(close, 2).astype(jnp.float32)
+    upper = keep[:part] + close[:part]
+    lower = keep[part:] + close[part:]
     for k, s in enumerate(s for s in spread if s and not s & 2):
         straight, across, later = rest[3 * k : 3 * k + 3]
         upper = upper + swap(straight, s).astype(jnp.float32)
         upper = upper + swap(across, s | 2).astype(jnp.float32)
-        later = later + came[height + k * part : height + (k + 1) * part]
+        later = later + came[k * part : (k + 1) * part]
         lower = lower + swap(later.astype(jnp.bfloat16), s).astype(jnp.float32)
     weight = jnp.concatenate([upper, lower], axis=0)
     weight = weight * (1.0 / math.sqrt(dps * rows * n))

time: 70.8 us -> 70.5 us (level)
  starting transfers between devices: 29.6 us -> 26.6 us
  waiting for transfers between devices: 29.6 us -> 32.1 us
    ppermute x21 -> x22, starting transfers between devices: 22.3 us -> 19.4 us  [swap(): return lax.ppermute(x, 'ctx', [(i, i ^ k) for i in range(n)])]
    ppermute x21 -> x22, waiting for transfers between devices: 27 us -> 28.4 us  [swap(): return lax.ppermute(x, 'ctx', [(i, i ^ k) for i in range(n)])]
    ppermute x3, waiting for transfers between devices: 2.57 us -> 3.72 us  [cross(): lax.ppermute(x, joint, [(a * n + b, (a ^ i) * n + (b ^ m)) for a in range...]
    pallas_call x1 -> x2, Pallas kernels: 1.27 us -> 1.45 us  [weight_terms(): pl.pallas_call(functools.partial(weight_kernel, members=members, spread=s...]
  transfers between devices with their start and end apart: 25 -> 26, of which waited for: 15 -> 15; matrix products, arithmetic and copies ran while one was open for 1% -> 1% of each run, Pallas kernels for 10% -> 11%
where the time goes in v5:
time: 70.5 us; the launch traced here: 70.3 us
  waiting for transfers between devices  32.1 us (46%)
  starting transfers between devices  26.6 us (38%)
  Pallas kernels  8.24 us (12%)
  other arithmetic  1.81 us (3%)
  between operations  0.81 us (1%)
    ppermute x22, waiting for transfers between devices, swap(): return lax.ppermute(x, 'ctx', [(i, i ^ k) for i in range(n)])  28.4 us
    ppermute x22, starting transfers between devices, swap(): return lax.ppermute(x, 'ctx', [(i, i ^ k) for i in range(n)])  19.4 us
    pallas_call x1, Pallas kernels, attention(): pl.pallas_call(body, out_shape=[jax.ShapeDtypeStruct((rows, width), jnp.b...  3.84 us
    ppermute x3, waiting for transfers between devices, cross(): lax.ppermute(x, joint, [(a * n + b, (a ^ i) * n + (b ^ m)) for a in range...  3.72 us
    all_to_all x1, starting transfers between devices, per_device(): xt = lax.all_to_all(xt, joint, 0, 0, axis_index_groups=groups, tiled=True)  3.6 us
    ppermute x3, starting transfers between devices, cross(): lax.ppermute(x, joint, [(a * n + b, (a ^ i) * n + (b ^ m)) for a in range...  3.55 us
    pallas_call x1, Pallas kernels, columns_first(): pl.pallas_call(functools.partial(columns_kernel, places=places, height=he...  2.95 us
    pallas_call x2, Pallas kernels, weight_terms(): pl.pallas_call(functools.partial(weight_kernel, members=members, spread=s...  1.45 us
  transfers between devices with their start and end apart: 26, of which 15 were waited for; matrix products, arithmetic and copies ran while one was open for 1% of the time, Pallas kernels for 11%

profile of v5, /device:TPU:0, one launch (start us, length us, event | category | flops | bytes accessed | tf_op | source)
XLA Modules:
  0.0 70.3 jit_solution(11689767564412840868)
XLA Ops:
  0.6 0.8 %fusion.9 = (bf16[1,128,256]{2,1,0:T(8,128)(2,1)S(1)}, bf16[128,256]{1,0:T(8,128)(2,1)S(1)}) fusion(bf16[128,128]{1,0:T(8,128)(2,1)} %bitcast.43, bf16[128,128]{1,0:T(8,128)(2,1)} %bitcast.44), kind=kLoop, calls=%fused_computation.24 | loop fusion | flops 131072 | bytes 196608 | tf_op jit(solution)/shard_map/stack | solution.py:303
  1.4 0.0 copy-start.4
  1.4 5.1 %collective-permute-start.2 = (bf16[128,256]{1,0:T(8,128)(2,1)S(1)}, bf16[128,256]{1,0:T(8,128)(2,1)S(1)}, u32[]{:S(2)}, u32[]{:S(2)}) collective-permute-start(bf16[128,256]{1,0:T(8,128)(2,1)S(1)} %get-tuple-element.36._), channel_id=1, source_target_pairs={{0,12},{1,13},{2,14},{3,15},{4,8},{5,9},{6,10},{7,11},{8,4},{9,5},... | collective-permute-start | bytes 196616 | tf_op jit(solution)/shard_map/ppermute | solution.py:289
  6.5 0.0 collective-permute-start.1
  6.5 0.6 collective-permute-start
  7.2 3.0 %columns_first.1 = bf16[8,1024,128]{2,1,0:T(8,128)(2,1)} custom-call(bf16[128,8192]{1,0:T(8,128)(2,1)} %bitcast.39, bf16[128,256]{1,0:T(8,128)(2,1)} %copy-done.4), custom_call_target="tpu_custom_call" | custom-call | bytes 4194304 | tf_op jit(solution)/shard_map/columns_first/pallas_call | solution.py:256
  10.2 0.0 collective-permute-done.2
  10.2 2.0 %collective-permute-done.1 = bf16[128,256]{1,0:T(8,128)(2,1)S(1)} collective-permute-done((bf16[128,256]{1,0:T(8,128)(2,1)S(1)}, bf16[128,256]{1,0:T(8,128)(2,1)S(1)}, u32[]{:S(2)}, u32[]{:S(2)}) %collective-permute-start.1) | collective-permute-done | bytes 65568 | tf_op jit(solution)/shard_map/ppermute | solution.py:289
  12.2 0.0 collective-permute-done
  12.2 0.0 copy-start
  12.2 0.0 copy-start.1
  12.2 0.0 copy-start.2
  12.2 0.0 copy-start.3
  12.2 1.6 %collective-permute-start.3 = (bf16[4,128,256]{2,1,0:T(8,128)(2,1)S(1)}, bf16[4,128,256]{2,1,0:T(8,128)(2,1)S(1)}, u32[]{:S(2)}, u32[]{:S(2)}) collective-permute-start(bf16[4,128,256]{2,1,0:T(8,128)(2,1)S(1)} %pad_maximum_fusion.refs_0_), channel_id=1, source_target_pairs={{0,2},{1,3},{2,0},{3,1},{4,6},{5,7},{6,4},{7,5},{8,10},{9,11},{10,... | collective-permute-start | bytes 786440 | tf_op jit(solution)/shard_map/ppermute | solution.py:289
  13.8 3.6 %all-to-all-start = ((bf16[8,1024,128]{2,1,0:T(8,128)(2,1)}), bf16[8,1024,128]{2,1,0:T(8,128)(2,1)S(1)}, u32[]{:S(2)}, u32[]{:S(2)}) async-start(bf16[8,1024,128]{2,1,0:T(8,128)(2,1)} %columns_first.1), calls=%async_computation | async-start | bytes 4194304 | tf_op jit(solution)/shard_map/all_to_all | solution.py:311
  17.4 0.4 collective-permute-start.4
  17.8 2.3 %collective-permute-done.3.refs_1_ = bf16[4,128,256]{2,1,0:T(8,128)(2,1)S(1)} collective-permute-done((bf16[4,128,256]{2,1,0:T(8,128)(2,1)S(1)}, bf16[4,128,256]{2,1,0:T(8,128)(2,1)S(1)}, u32[]{:S(2)}, u32[]{:S(2)}) %collective-permute-start.3) | collective-permute-done | bytes 262176 | tf_op jit(solution)/shard_map/ppermute | solution.py:289
  20.2 0.0 collective-permute-start.5
  20.2 0.0 collective-permute-done.4.refs_2_
  20.2 1.5 %collective-permute-done.5.refs_3_ = bf16[4,128,256]{2,1,0:T(8,128)(2,1)S(1)} collective-permute-done((bf16[4,128,256]{2,1,0:T(8,128)(2,1)S(1)}, bf16[4,128,256]{2,1,0:T(8,128)(2,1)S(1)}, u32[]{:S(2)}, u32[]{:S(2)}) %collective-permute-start.5) | collective-permute-done | bytes 262176 | tf_op jit(solution)/shard_map/ppermute | solution.py:289
  21.7 3.8 %attention_grads.1 = (bf16[128,1024]{1,0:T(8,128)(2,1)}, f32[4,128,256]{2,1,0:T(8,128)S(1)}, bf16[4,128,256]{2,1,0:T(8,128)(2,1)S(1)}, bf16[4,128,256]{2,1,0:T(8,128)(2,1)S(1)}, bf16[4,128,256]{2,1,0:T(8,128)(2,1)S(1)}) custom-call(s32[32]{0:T(128)S(1)} %copy-done.2, s32[1,8]{1,0:T(1,128)S(1)} %copy-done.3, bf16[128,1024]{1,0:T(8,128)(2,1)S(1)} %bitcast.37, ...), custom_call_target="tpu_custom_call" | custom-call | flops 16609443840 | bytes 4194304 | tf_op jit(solution)/shard_map/attention_grads/pallas_call | solution.py:117
  25.6 0.1 collective-permute-start.7
  25.7 0.4 collective-permute-start.6
  26.1 1.0 %collective-permute-done.7 = bf16[4,128,256]{2,1,0:T(8,128)(2,1)S(1)} collective-permute-done((bf16[4,128,256]{2,1,0:T(8,128)(2,1)S(1)}, bf16[4,128,256]{2,1,0:T(8,128)(2,1)S(1)}, u32[]{:S(2)}, u32[]{:S(2)}) %collective-permute-start.7) | collective-permute-done | bytes 262176 | tf_op jit(solution)/shard_map/ppermute | solution.py:289
  27.1 0.1 add_convert_fusion
  27.2 1.8 %collective-permute-start.9 = (bf16[3,128,256]{2,1,0:T(8,128)(2,1)S(1)}, bf16[3,128,256]{2,1,0:T(8,128)(2,1)S(1)}, u32[]{:S(2)}, u32[]{:S(2)}) collective-permute-start(bf16[3,128,256]{2,1,0:T(8,128)(2,1)S(1)} %slice.63), channel_id=1, source_target_pairs={{0,2},{1,3},{2,0},{3,1},{4,6},{5,7},{6,4},{7,5},{8,10},{9,11},{10,... | collective-permute-start | bytes 589832 | tf_op jit(solution)/shard_map/ppermute | solution.py:289
  29.0 0.3 collective-permute-start.8
  29.3 0.0 collective-permute-done.6
  29.3 5.6 %collective-permute-done.9 = bf16[3,128,256]{2,1,0:T(8,128)(2,1)S(1)} collective-permute-done((bf16[3,128,256]{2,1,0:T(8,128)(2,1)S(1)}, bf16[3,128,256]{2,1,0:T(8,128)(2,1)S(1)}, u32[]{:S(2)}, u32[]{:S(2)}) %collective-permute-start.9) | collective-permute-done | bytes 196640 | tf_op jit(solution)/shard_map/ppermute | solution.py:289
  34.9 0.1 add_convert_fusion.1
  35.0 0.2 collective-permute-start.10
  35.2 1.7 %collective-permute-start.12 = (bf16[128,256]{1,0:T(8,128)(2,1)S(1)}, bf16[128,256]{1,0:T(8,128)(2,1)S(1)}, u32[]{:S(2)}, u32[]{:S(2)}) collective-permute-start(bf16[128,256]{1,0:T(8,128)(2,1)S(1)} %get-tuple-element.31), channel_id=1, source_target_pairs={{0,12},{1,13},{2,14},{3,15},{4,8},{5,9},{6,10},{7,11},{8,4},{9,5},... | collective-permute-start | bytes 196616 | tf_op jit(solution)/shard_map/ppermute | solution.py:289
  36.9 1.7 %collective-permute-start.11 = (bf16[128,256]{1,0:T(8,128)(2,1)S(1)}, bf16[128,256]{1,0:T(8,128)(2,1)S(1)}, u32[]{:S(2)}, u32[]{:S(2)}) collective-permute-start(bf16[128,256]{1,0:T(8,128)(2,1)S(1)} %get-tuple-element.32), channel_id=1, source_target_pairs={{0,8},{1,9},{2,10},{3,11},{4,12},{5,13},{6,14},{7,15},{8,0},{9,1},... | collective-permute-start | bytes 196616 | tf_op jit(solution)/shard_map/ppermute | solution.py:289
  38.6 0.0 collective-permute-done.8
  38.6 7.8 %collective-permute-done.10 = bf16[128,256]{1,0:T(8,128)(2,1)S(1)} collective-permute-done((bf16[128,256]{1,0:T(8,128)(2,1)S(1)}, bf16[128,256]{1,0:T(8,128)(2,1)S(1)}, u32[]{:S(2)}, u32[]{:S(2)}) %collective-permute-start.10) | collective-permute-done | bytes 65568 | tf_op jit(solution)/shard_map/ppermute | solution.py:289
  46.4 1.4 %collective-permute-done.12 = bf16[128,256]{1,0:T(8,128)(2,1)S(1)} collective-permute-done((bf16[128,256]{1,0:T(8,128)(2,1)S(1)}, bf16[128,256]{1,0:T(8,128)(2,1)S(1)}, u32[]{:S(2)}, u32[]{:S(2)}) %collective-permute-start.12) | collective-permute-done | bytes 65568 | tf_op jit(solution)/shard_map/ppermute | solution.py:289
  47.8 0.0 collective-permute-done.11
  47.8 0.1 fusion.8.refs_0_
  47.8 2.5 %collective-permute-start.18 = (bf16[128,256]{1,0:T(8,128)(2,1)S(1)}, bf16[128,256]{1,0:T(8,128)(2,1)S(1)}, u32[]{:S(2)}, u32[]{:S(2)}) collective-permute-start(bf16[128,256]{1,0:T(8,128)(2,1)S(1)} %fusion.8.refs_0_), channel_id=1, source_target_pairs={{0,20},{1,21},{2,22},{3,23},{4,16},{5,17},{6,18},{7,19},{8,28},{9,... | collective-permute-start | bytes 196616 | tf_op jit(solution)/shard_map/ppermute | solution.py:297
  50.3 0.6 collective-permute-start.16
  50.8 0.5 collective-permute-start.14
  51.4 0.0 collective-permute-start.13
  51.4 1.8 %collective-permute-done.18.refs_6_ = bf16[128,256]{1,0:T(8,128)(2,1)S(1)} collective-permute-done((bf16[128,256]{1,0:T(8,128)(2,1)S(1)}, bf16[128,256]{1,0:T(8,128)(2,1)S(1)}, u32[]{:S(2)}, u32[]{:S(2)}) %collective-permute-start.18) | collective-permute-done | bytes 65568 | tf_op jit(solution)/shard_map/ppermute | solution.py:297
  53.2 0.0 collective-permute-start.19
  53.2 1.4 %collective-permute-done.16.refs_4_ = bf16[128,256]{1,0:T(8,128)(2,1)S(1)} collective-permute-done((bf16[128,256]{1,0:T(8,128)(2,1)S(1)}, bf16[128,256]{1,0:T(8,128)(2,1)S(1)}, u32[]{:S(2)}, u32[]{:S(2)}) %collective-permute-start.16) | collective-permute-done | bytes 65568 | tf_op jit(solution)/shard_map/ppermute | solution.py:297
  54.6 0.0 collective-permute-start.17
  54.6 0.6 collective-permute-done.14.refs_2_
  55.1 0.7 collective-permute-done.17.refs_5_
  55.8 0.6 collective-permute-done.15.refs_3_
  56.4 0.0 all-to-all-done.x_ref
  56.4 0.7 %weight_terms.3 = (bf16[128,256]{1,0:T(8,128)(2,1)S(1)}, bf16[128,256]{1,0:T(8,128)(2,1)S(1)}, bf16[128,256]{1,0:T(8,128)(2,1)S(1)}, f32[128,256]{1,0:T(8,128)S(1)}) custom-call(bf16[8,1024,128]{2,1,0:T(8,128)(2,1)S(1)} %all-to-all-done.x_ref, bf16[128,256]{1,0:T(8,128)(2,1)S(1)} %fusion.8.refs_0_, bf16[128,256]{1,0:T(8,128)(2,1)S(1)} %collective-permute-done.13.refs_1_, ...), custom_call_target="tpu_custom_call" | custom-call | flops 268435456 | bytes 4194304 | tf_op jit(solution)/shard_map/weight_terms/pallas_call | solution.py:205
  57.1 0.6 collective-permute-start.23
  57.7 0.4 collective-permute-start.21
  58.1 3.5 %collective-permute-start.22 = (bf16[128,256]{1,0:T(8,128)(2,1)S(1)}, bf16[128,256]{1,0:T(8,128)(2,1)S(1)}, u32[]{:S(2)}, u32[]{:S(2)}) collective-permute-start(bf16[128,256]{1,0:T(8,128)(2,1)S(1)} %get-tuple-element.25), channel_id=1, source_target_pairs={{0,10},{1,11},{2,8},{3,9},{4,14},{5,15},{6,12},{7,13},{8,2},{9,3},... | collective-permute-start | bytes 196616 | tf_op jit(solution)/shard_map/ppermute | solution.py:289
  61.6 0.7 %weight_terms.2 = (f32[256,256]{1,0:T(8,128)S(1)}, bf16[256,256]{1,0:T(8,128)(2,1)S(1)}) custom-call(bf16[8,1024,128]{2,1,0:T(8,128)(2,1)S(1)} %all-to-all-done.x_ref, bf16[128,256]{1,0:T(8,128)(2,1)S(1)} %fusion.8.refs_0_, bf16[128,256]{1,0:T(8,128)(2,1)S(1)} %collective-permute-done.13.refs_1_, bf16[128,256]{1,0:T(8,128)(2,1)S(1)} %collective-permute-done.14.refs_2_, ...), custom_call_target="tpu_custom_call" | custom-call | flops 268435456 | bytes 4194304 | tf_op jit(solution)/shard_map/weight_terms/pallas_call | solution.py:205
  62.3 0.6 collective-permute-start.20
  62.9 0.0 collective-permute-done.23
  62.9 0.5 collective-permute-start.24
  63.4 0.6 slice_bitcast_fusion.4
  64.0 4.7 %collective-permute-done.20 = bf16[256,256]{1,0:T(8,128)(2,1)S(1)} collective-permute-done((bf16[256,256]{1,0:T(8,128)(2,1)S(1)}, bf16[256,256]{1,0:T(8,128)(2,1)S(1)}, u32[]{:S(2)}, u32[]{:S(2)}) %collective-permute-start.20) | collective-permute-done | bytes 131104 | tf_op jit(solution)/shard_map/ppermute | solution.py:289
  68.7 0.6 collective-permute-done.22
  69.3 0.1 collective-permute-done.24
  69.5 0.1 fusion.4
  69.5 0.7 %maximum_multiply_fusion = f32[1,256,256]{2,1,0:T(8,128)} fusion(f32[1,128,256]{2,1,0:T(8,128)S(1)} %get-tuple-element.29, f32[1,128,256]{2,1,0:T(8,128)S(1)} %get-tuple-element.28), kind=kLoop, calls=%fused_computation.3 | loop fusion | flops 131072 | bytes 524288 | tf_op jit(solution)/shard_map/mul | solution.py:355
  (15 shorter events, 0.1 us)
Async XLA Ops:
  1.4 5.8 %copy-start.4 = (bf16[128,256]{1,0:T(8,128)(2,1)}, bf16[128,256]{1,0:T(8,128)(2,1)S(1)}, u32[]{:S(2)}) copy-start(bf16[128,256]{1,0:T(8,128)(2,1)S(1)} %get-tuple-element.36._) | copy-start | bytes 196612
  1.4 8.7 %collective-permute-start.2 = (bf16[128,256]{1,0:T(8,128)(2,1)S(1)}, bf16[128,256]{1,0:T(8,128)(2,1)S(1)}, u32[]{:S(2)}, u32[]{:S(2)}) collective-permute-start(bf16[128,256]{1,0:T(8,128)(2,1)S(1)} %get-tuple-element.36._), channel_id=1, source_target_pairs={{0,12},{1,13},{2,14},{3,15},{4,8},{5,9},{6,10},{7,11},{8,4},{9,5},... | collective-permute-start | bytes 196616 | tf_op jit(solution)/shard_map/ppermute | solution.py:289
  6.5 5.6 %collective-permute-start.1 = (bf16[128,256]{1,0:T(8,128)(2,1)S(1)}, bf16[128,256]{1,0:T(8,128)(2,1)S(1)}, u32[]{:S(2)}, u32[]{:S(2)}) collective-permute-start(bf16[128,256]{1,0:T(8,128)(2,1)S(1)} %get-tuple-element.36._), channel_id=1, source_target_pairs={{0,8},{1,9},{2,10},{3,11},{4,12},{5,13},{6,14},{7,15},{8,0},{9,1},... | collective-permute-start | bytes 196616 | tf_op jit(solution)/shard_map/ppermute | solution.py:289
  6.5 5.6 %collective-permute-start = (bf16[128,256]{1,0:T(8,128)(2,1)S(1)}, bf16[128,256]{1,0:T(8,128)(2,1)S(1)}, u32[]{:S(2)}, u32[]{:S(2)}) collective-permute-start(bf16[128,256]{1,0:T(8,128)(2,1)S(1)} %get-tuple-element.36._), channel_id=1, source_target_pairs={{0,4},{1,5},{2,6},{3,7},{4,0},{5,1},{6,2},{7,3},{8,12},{9,13},{10,... | collective-permute-start | bytes 196616 | tf_op jit(solution)/shard_map/ppermute | solution.py:289
  12.2 9.5 %copy-start = (bf16[1,128,1024]{2,1,0:T(8,128)(2,1)S(1)}, bf16[1,128,1024]{2,1,0:T(8,128)(2,1)}, u32[]{:S(2)}) copy-start(bf16[1,128,1024]{2,1,0:T(8,128)(2,1)} %param.8) | copy-start | bytes 786436
  12.2 9.5 %copy-start.1 = (bf16[1,128,1024]{2,1,0:T(8,128)(2,1)S(1)}, bf16[1,128,1024]{2,1,0:T(8,128)(2,1)}, u32[]{:S(2)}) copy-start(bf16[1,128,1024]{2,1,0:T(8,128)(2,1)} %param.11) | copy-start | bytes 786436
  12.2 9.5 %copy-start.2 = (s32[32]{0:T(128)S(1)}, s32[32]{0:T(128)}, u32[]{:S(2)}) copy-start(s32[32]{0:T(128)} %order.1) | copy-start | bytes 388
  12.2 9.5 %copy-start.3 = (s32[1,8]{1,0:T(1,128)S(1)}, s32[1,8]{1,0:T(1,128)}, u32[]{:S(2)}) copy-start(s32[1,8]{1,0:T(1,128)} %lengths.1) | copy-start | bytes 100
  12.2 7.9 %collective-permute-start.3 = (bf16[4,128,256]{2,1,0:T(8,128)(2,1)S(1)}, bf16[4,128,256]{2,1,0:T(8,128)(2,1)S(1)}, u32[]{:S(2)}, u32[]{:S(2)}) collective-permute-start(bf16[4,128,256]{2,1,0:T(8,128)(2,1)S(1)} %pad_maximum_fusion.refs_0_), channel_id=1, source_target_pairs={{0,2},{1,3},{2,0},{3,1},{4,6},{5,7},{6,4},{7,5},{8,10},{9,11},{10,... | collective-permute-start | bytes 786440 | tf_op jit(solution)/shard_map/ppermute | solution.py:289
  13.8 42.5 %all-to-all-start = ((bf16[8,1024,128]{2,1,0:T(8,128)(2,1)}), bf16[8,1024,128]{2,1,0:T(8,128)(2,1)S(1)}, u32[]{:S(2)}, u32[]{:S(2)}) async-start(bf16[8,1024,128]{2,1,0:T(8,128)(2,1)} %columns_first.1), calls=%async_computation | async-start | bytes 4194304 | tf_op jit(solution)/shard_map/all_to_all | solution.py:311
  17.4 2.8 %collective-permute-start.4 = (bf16[4,128,256]{2,1,0:T(8,128)(2,1)S(1)}, bf16[4,128,256]{2,1,0:T(8,128)(2,1)S(1)}, u32[]{:S(2)}, u32[]{:S(2)}) collective-permute-start(bf16[4,128,256]{2,1,0:T(8,128)(2,1)S(1)} %pad_maximum_fusion.refs_0_), channel_id=1, source_target_pairs={{0,1},{1,0},{2,3},{3,2},{4,5},{5,4},{6,7},{7,6},{8,9},{9,8},{10,11... | collective-permute-start | bytes 786440 | tf_op jit(solution)/shard_map/ppermute | solution.py:289
  20.2 1.5 %collective-permute-start.5 = (bf16[4,128,256]{2,1,0:T(8,128)(2,1)S(1)}, bf16[4,128,256]{2,1,0:T(8,128)(2,1)S(1)}, u32[]{:S(2)}, u32[]{:S(2)}) collective-permute-start(bf16[4,128,256]{2,1,0:T(8,128)(2,1)S(1)} %collective-permute-done.3.refs_1_), channel_id=1, source_target_pairs={{0,1},{1,0},{2,3},{3,2},{4,5},{5,4},{6,7},{7,6},{8,9},{9,8},{10,11... | collective-permute-start | bytes 786440 | tf_op jit(solution)/shard_map/ppermute | solution.py:289
  25.6 1.5 %collective-permute-start.7 = (bf16[4,128,256]{2,1,0:T(8,128)(2,1)S(1)}, bf16[4,128,256]{2,1,0:T(8,128)(2,1)S(1)}, u32[]{:S(2)}, u32[]{:S(2)}) collective-permute-start(bf16[4,128,256]{2,1,0:T(8,128)(2,1)S(1)} %get-tuple-element.21), channel_id=1, source_target_pairs={{0,1},{1,0},{2,3},{3,2},{4,5},{5,4},{6,7},{7,6},{8,9},{9,8},{10,11... | collective-permute-start | bytes 786440 | tf_op jit(solution)/shard_map/ppermute | solution.py:289
  25.7 3.6 %collective-permute-start.6 = (bf16[4,128,256]{2,1,0:T(8,128)(2,1)S(1)}, bf16[4,128,256]{2,1,0:T(8,128)(2,1)S(1)}, u32[]{:S(2)}, u32[]{:S(2)}) collective-permute-start(bf16[4,128,256]{2,1,0:T(8,128)(2,1)S(1)} %get-tuple-element.19), channel_id=1, source_target_pairs={{0,1},{1,0},{2,3},{3,2},{4,5},{5,4},{6,7},{7,6},{8,9},{9,8},{10,11... | collective-permute-start | bytes 786440 | tf_op jit(solution)/shard_map/ppermute | solution.py:289
  27.2 7.7 %collective-permute-start.9 = (bf16[3,128,256]{2,1,0:T(8,128)(2,1)S(1)}, bf16[3,128,256]{2,1,0:T(8,128)(2,1)S(1)}, u32[]{:S(2)}, u32[]{:S(2)}) collective-permute-start(bf16[3,128,256]{2,1,0:T(8,128)(2,1)S(1)} %slice.63), channel_id=1, source_target_pairs={{0,2},{1,3},{2,0},{3,1},{4,6},{5,7},{6,4},{7,5},{8,10},{9,11},{10,... | collective-permute-start | bytes 589832 | tf_op jit(solution)/shard_map/ppermute | solution.py:289
  29.0 9.6 %collective-permute-start.8 = (bf16[128,256]{1,0:T(8,128)(2,1)S(1)}, bf16[128,256]{1,0:T(8,128)(2,1)S(1)}, u32[]{:S(2)}, u32[]{:S(2)}) collective-permute-start(bf16[128,256]{1,0:T(8,128)(2,1)S(1)} %slice_bitcast_fusion.3), channel_id=1, source_target_pairs={{0,2},{1,3},{2,0},{3,1},{4,6},{5,7},{6,4},{7,5},{8,10},{9,11},{10,... | collective-permute-start | bytes 196616 | tf_op jit(solution)/shard_map/ppermute | solution.py:289
  35.0 11.4 %collective-permute-start.10 = (bf16[128,256]{1,0:T(8,128)(2,1)S(1)}, bf16[128,256]{1,0:T(8,128)(2,1)S(1)}, u32[]{:S(2)}, u32[]{:S(2)}) collective-permute-start(bf16[128,256]{1,0:T(8,128)(2,1)S(1)} %get-tuple-element.30), channel_id=1, source_target_pairs={{0,4},{1,5},{2,6},{3,7},{4,0},{5,1},{6,2},{7,3},{8,12},{9,13},{10,... | collective-permute-start | bytes 196616 | tf_op jit(solution)/shard_map/ppermute | solution.py:289
  35.2 12.6 %collective-permute-start.12 = (bf16[128,256]{1,0:T(8,128)(2,1)S(1)}, bf16[128,256]{1,0:T(8,128)(2,1)S(1)}, u32[]{:S(2)}, u32[]{:S(2)}) collective-permute-start(bf16[128,256]{1,0:T(8,128)(2,1)S(1)} %get-tuple-element.31), channel_id=1, source_target_pairs={{0,12},{1,13},{2,14},{3,15},{4,8},{5,9},{6,10},{7,11},{8,4},{9,5},... | collective-permute-start | bytes 196616 | tf_op jit(solution)/shard_map/ppermute | solution.py:289
  36.9 10.9 %collective-permute-start.11 = (bf16[128,256]{1,0:T(8,128)(2,1)S(1)}, bf16[128,256]{1,0:T(8,128)(2,1)S(1)}, u32[]{:S(2)}, u32[]{:S(2)}) collective-permute-start(bf16[128,256]{1,0:T(8,128)(2,1)S(1)} %get-tuple-element.32), channel_id=1, source_target_pairs={{0,8},{1,9},{2,10},{3,11},{4,12},{5,13},{6,14},{7,15},{8,0},{9,1},... | collective-permute-start | bytes 196616 | tf_op jit(solution)/shard_map/ppermute | solution.py:289
  47.8 5.3 %collective-permute-start.18 = (bf16[128,256]{1,0:T(8,128)(2,1)S(1)}, bf16[128,256]{1,0:T(8,128)(2,1)S(1)}, u32[]{:S(2)}, u32[]{:S(2)}) collective-permute-start(bf16[128,256]{1,0:T(8,128)(2,1)S(1)} %fusion.8.refs_0_), channel_id=1, source_target_pairs={{0,20},{1,21},{2,22},{3,23},{4,16},{5,17},{6,18},{7,19},{8,28},{9,... | collective-permute-start | bytes 196616 | tf_op jit(solution)/shard_map/ppermute | solution.py:297
  50.3 4.3 %collective-permute-start.16 = (bf16[128,256]{1,0:T(8,128)(2,1)S(1)}, bf16[128,256]{1,0:T(8,128)(2,1)S(1)}, u32[]{:S(2)}, u32[]{:S(2)}) collective-permute-start(bf16[128,256]{1,0:T(8,128)(2,1)S(1)} %fusion.8.refs_0_), channel_id=1, source_target_pairs={{0,16},{1,17},{2,18},{3,19},{4,20},{5,21},{6,22},{7,23},{8,24},{9,... | collective-permute-start | bytes 196616 | tf_op jit(solution)/shard_map/ppermute | solution.py:297
  50.8 4.3 %collective-permute-start.14 = (bf16[128,256]{1,0:T(8,128)(2,1)S(1)}, bf16[128,256]{1,0:T(8,128)(2,1)S(1)}, u32[]{:S(2)}, u32[]{:S(2)}) collective-permute-start(bf16[128,256]{1,0:T(8,128)(2,1)S(1)} %fusion.8.refs_0_), channel_id=1, source_target_pairs={{0,4},{1,5},{2,6},{3,7},{4,0},{5,1},{6,2},{7,3},{8,12},{9,13},{10,... | collective-permute-start | bytes 196616 | tf_op jit(solution)/shard_map/ppermute | solution.py:297
  51.4 3.7 %collective-permute-start.13 = (bf16[128,256]{1,0:T(8,128)(2,1)S(1)}, bf16[128,256]{1,0:T(8,128)(2,1)S(1)}, u32[]{:S(2)}, u32[]{:S(2)}) collective-permute-start(bf16[128,256]{1,0:T(8,128)(2,1)S(1)} %fusion.8.refs_0_), channel_id=1, source_target_pairs={{0,1},{1,0},{2,3},{3,2},{4,5},{5,4},{6,7},{7,6},{8,9},{9,8},{10,11... | collective-permute-start | bytes 196616 | tf_op jit(solution)/shard_map/ppermute | solution.py:289
  53.2 2.0 %collective-permute-start.19 = (bf16[128,256]{1,0:T(8,128)(2,1)S(1)}, bf16[128,256]{1,0:T(8,128)(2,1)S(1)}, u32[]{:S(2)}, u32[]{:S(2)}) collective-permute-start(bf16[128,256]{1,0:T(8,128)(2,1)S(1)} %collective-permute-done.18.refs_6_), channel_id=1, source_target_pairs={{0,1},{1,0},{2,3},{3,2},{4,5},{5,4},{6,7},{7,6},{8,9},{9,8},{10,11... | collective-permute-start | bytes 196616 | tf_op jit(solution)/shard_map/ppermute | solution.py:289
  54.6 1.3 %collective-permute-start.17 = (bf16[128,256]{1,0:T(8,128)(2,1)S(1)}, bf16[128,256]{1,0:T(8,128)(2,1)S(1)}, u32[]{:S(2)}, u32[]{:S(2)}) collective-permute-start(bf16[128,256]{1,0:T(8,128)(2,1)S(1)} %collective-permute-done.16.refs_4_), channel_id=1, source_target_pairs={{0,1},{1,0},{2,3},{3,2},{4,5},{5,4},{6,7},{7,6},{8,9},{9,8},{10,11... | collective-permute-start | bytes 196616 | tf_op jit(solution)/shard_map/ppermute | solution.py:289
  55.1 1.3 %collective-permute-start.15 = (bf16[128,256]{1,0:T(8,128)(2,1)S(1)}, bf16[128,256]{1,0:T(8,128)(2,1)S(1)}, u32[]{:S(2)}, u32[]{:S(2)}) collective-permute-start(bf16[128,256]{1,0:T(8,128)(2,1)S(1)} %collective-permute-done.14.refs_2_), channel_id=1, source_target_pairs={{0,1},{1,0},{2,3},{3,2},{4,5},{5,4},{6,7},{7,6},{8,9},{9,8},{10,11... | collective-permute-start | bytes 196616 | tf_op jit(solution)/shard_map/ppermute | solution.py:289
  57.1 5.8 %collective-permute-start.23 = (bf16[128,256]{1,0:T(8,128)(2,1)S(1)}, bf16[128,256]{1,0:T(8,128)(2,1)S(1)}, u32[]{:S(2)}, u32[]{:S(2)}) collective-permute-start(bf16[128,256]{1,0:T(8,128)(2,1)S(1)} %get-tuple-element.27), channel_id=1, source_target_pairs={{0,2},{1,3},{2,0},{3,1},{4,6},{5,7},{6,4},{7,5},{8,10},{9,11},{10,... | collective-permute-start | bytes 196616 | tf_op jit(solution)/shard_map/ppermute | solution.py:289
  57.7 11.0 %collective-permute-start.21 = (bf16[128,256]{1,0:T(8,128)(2,1)S(1)}, bf16[128,256]{1,0:T(8,128)(2,1)S(1)}, u32[]{:S(2)}, u32[]{:S(2)}) collective-permute-start(bf16[128,256]{1,0:T(8,128)(2,1)S(1)} %get-tuple-element.24), channel_id=1, source_target_pairs={{0,8},{1,9},{2,10},{3,11},{4,12},{5,13},{6,14},{7,15},{8,0},{9,1},... | collective-permute-start | bytes 196616 | tf_op jit(solution)/shard_map/ppermute | solution.py:289
  58.1 11.2 %collective-permute-start.22 = (bf16[128,256]{1,0:T(8,128)(2,1)S(1)}, bf16[128,256]{1,0:T(8,128)(2,1)S(1)}, u32[]{:S(2)}, u32[]{:S(2)}) collective-permute-start(bf16[128,256]{1,0:T(8,128)(2,1)S(1)} %get-tuple-element.25), channel_id=1, source_target_pairs={{0,10},{1,11},{2,8},{3,9},{4,14},{5,15},{6,12},{7,13},{8,2},{9,3},... | collective-permute-start | bytes 196616 | tf_op jit(solution)/shard_map/ppermute | solution.py:289
  62.3 6.4 %collective-permute-start.20 = (bf16[256,256]{1,0:T(8,128)(2,1)S(1)}, bf16[256,256]{1,0:T(8,128)(2,1)S(1)}, u32[]{:S(2)}, u32[]{:S(2)}) collective-permute-start(bf16[256,256]{1,0:T(8,128)(2,1)S(1)} %get-tuple-element.23), channel_id=1, source_target_pairs={{0,2},{1,3},{2,0},{3,1},{4,6},{5,7},{6,4},{7,5},{8,10},{9,11},{10,... | collective-permute-start | bytes 393224 | tf_op jit(solution)/shard_map/ppermute | solution.py:289
  62.9 6.6 %collective-permute-start.24 = (bf16[128,256]{1,0:T(8,128)(2,1)S(1)}, bf16[128,256]{1,0:T(8,128)(2,1)S(1)}, u32[]{:S(2)}, u32[]{:S(2)}) collective-permute-start(bf16[128,256]{1,0:T(8,128)(2,1)S(1)} %add_convert_fusion.2), channel_id=1, source_target_pairs={{0,8},{1,9},{2,10},{3,11},{4,12},{5,13},{6,14},{7,15},{8,0},{9,1},... | collective-permute-start | bytes 196616 | tf_op jit(solution)/shard_map/ppermute | solution.py:289

commit v6 on v5

--- a/solution.py
+++ b/solution.py
@@ -14,7 +14,7 @@
 
 
 def attention_kernel(
-    order, lengths, q_ref, d_ref, *refs, n, mid, top, heads, head_dim, half, blocks, window, group
+    order, lengths, q_ref, d_ref, *refs, mid, top, heads, head_dim, half, blocks, window, group
 ):
     count = 2 * mid
     kv_refs = refs[:count]
@@ -101,7 +101,6 @@
     part = (top, rows, 2 * head_dim)
     body = functools.partial(
         attention_kernel,
-        n=n,
         mid=mid,
         top=top,
         heads=heads,

time: 70.5 us -> 70.5 us (level)
  no operation moved by 1% of the time
where the time goes in v6:
time: 70.5 us; the launch traced here: 70.3 us
  waiting for transfers between devices  32.1 us (46%)
  starting transfers between devices  26.6 us (38%)
  Pallas kernels  8.24 us (12%)
  other arithmetic  1.81 us (3%)
  between operations  0.81 us (1%)
    ppermute x22, waiting for transfers between devices, swap(): return lax.ppermute(x, 'ctx', [(i, i ^ k) for i in range(n)])  28.4 us
    ppermute x22, starting transfers between devices, swap(): return lax.ppermute(x, 'ctx', [(i, i ^ k) for i in range(n)])  19.4 us
    pallas_call x1, Pallas kernels, attention(): pl.pallas_call(body, out_shape=[jax.ShapeDtypeStruct((rows, width), jnp.b...  3.84 us
    ppermute x3, waiting for transfers between devices, cross(): lax.ppermute(x, joint, [(a * n + b, (a ^ i) * n + (b ^ m)) for a in range...  3.72 us
    all_to_all x1, starting transfers between devices, per_device(): xt = lax.all_to_all(xt, joint, 0, 0, axis_index_groups=groups, tiled=True)  3.6 us
    ppermute x3, starting transfers between devices, cross(): lax.ppermute(x, joint, [(a * n + b, (a ^ i) * n + (b ^ m)) for a in range...  3.55 us
    pallas_call x1, Pallas kernels, columns_first(): pl.pallas_call(functools.partial(columns_kernel, places=places, height=he...  2.95 us
    pallas_call x2, Pallas kernels, weight_terms(): pl.pallas_call(functools.partial(weight_kernel, members=members, spread=s...  1.45 us
  transfers between devices with their start and end apart: 26, of which 15 were waited for; matrix products, arithmetic and copies ran while one was open for 1% of the time, Pallas kernels for 11%

profile of v6, /device:TPU:0, one launch (start us, length us, event | category | flops | bytes accessed | tf_op | source)
XLA Modules:
  0.0 70.3 jit_solution(11689767564412840868)
XLA Ops:
  0.6 0.8 %fusion.9 = (bf16[1,128,256]{2,1,0:T(8,128)(2,1)S(1)}, bf16[128,256]{1,0:T(8,128)(2,1)S(1)}) fusion(bf16[128,128]{1,0:T(8,128)(2,1)} %bitcast.43, bf16[128,128]{1,0:T(8,128)(2,1)} %bitcast.44), kind=kLoop, calls=%fused_computation.24 | loop fusion | flops 131072 | bytes 196608 | tf_op jit(solution)/shard_map/stack | solution.py:302
  1.4 0.0 copy-start.4
  1.4 5.1 %collective-permute-start.2 = (bf16[128,256]{1,0:T(8,128)(2,1)S(1)}, bf16[128,256]{1,0:T(8,128)(2,1)S(1)}, u32[]{:S(2)}, u32[]{:S(2)}) collective-permute-start(bf16[128,256]{1,0:T(8,128)(2,1)S(1)} %get-tuple-element.36._), channel_id=1, source_target_pairs={{0,12},{1,13},{2,14},{3,15},{4,8},{5,9},{6,10},{7,11},{8,4},{9,5},... | collective-permute-start | bytes 196616 | tf_op jit(solution)/shard_map/ppermute | solution.py:288
  6.5 0.0 collective-permute-start.1
  6.5 0.6 collective-permute-start
  7.2 3.0 %columns_first.1 = bf16[8,1024,128]{2,1,0:T(8,128)(2,1)} custom-call(bf16[128,8192]{1,0:T(8,128)(2,1)} %bitcast.39, bf16[128,256]{1,0:T(8,128)(2,1)} %copy-done.4), custom_call_target="tpu_custom_call" | custom-call | bytes 4194304 | tf_op jit(solution)/shard_map/columns_first/pallas_call | solution.py:255
  10.2 0.0 collective-permute-done.2
  10.2 2.0 %collective-permute-done.1 = bf16[128,256]{1,0:T(8,128)(2,1)S(1)} collective-permute-done((bf16[128,256]{1,0:T(8,128)(2,1)S(1)}, bf16[128,256]{1,0:T(8,128)(2,1)S(1)}, u32[]{:S(2)}, u32[]{:S(2)}) %collective-permute-start.1) | collective-permute-done | bytes 65568 | tf_op jit(solution)/shard_map/ppermute | solution.py:288
  12.2 0.0 collective-permute-done
  12.2 0.0 copy-start
  12.2 0.0 copy-start.1
  12.2 0.0 copy-start.2
  12.2 0.0 copy-start.3
  12.2 1.6 %collective-permute-start.3 = (bf16[4,128,256]{2,1,0:T(8,128)(2,1)S(1)}, bf16[4,128,256]{2,1,0:T(8,128)(2,1)S(1)}, u32[]{:S(2)}, u32[]{:S(2)}) collective-permute-start(bf16[4,128,256]{2,1,0:T(8,128)(2,1)S(1)} %pad_maximum_fusion.refs_0_), channel_id=1, source_target_pairs={{0,2},{1,3},{2,0},{3,1},{4,6},{5,7},{6,4},{7,5},{8,10},{9,11},{10,... | collective-permute-start | bytes 786440 | tf_op jit(solution)/shard_map/ppermute | solution.py:288
  13.8 3.6 %all-to-all-start = ((bf16[8,1024,128]{2,1,0:T(8,128)(2,1)}), bf16[8,1024,128]{2,1,0:T(8,128)(2,1)S(1)}, u32[]{:S(2)}, u32[]{:S(2)}) async-start(bf16[8,1024,128]{2,1,0:T(8,128)(2,1)} %columns_first.1), calls=%async_computation | async-start | bytes 4194304 | tf_op jit(solution)/shard_map/all_to_all | solution.py:310
  17.4 0.4 collective-permute-start.4
  17.8 2.3 %collective-permute-done.3.refs_1_ = bf16[4,128,256]{2,1,0:T(8,128)(2,1)S(1)} collective-permute-done((bf16[4,128,256]{2,1,0:T(8,128)(2,1)S(1)}, bf16[4,128,256]{2,1,0:T(8,128)(2,1)S(1)}, u32[]{:S(2)}, u32[]{:S(2)}) %collective-permute-start.3) | collective-permute-done | bytes 262176 | tf_op jit(solution)/shard_map/ppermute | solution.py:288
  20.2 0.0 collective-permute-start.5
  20.2 0.0 collective-permute-done.4.refs_2_
  20.2 1.5 %collective-permute-done.5.refs_3_ = bf16[4,128,256]{2,1,0:T(8,128)(2,1)S(1)} collective-permute-done((bf16[4,128,256]{2,1,0:T(8,128)(2,1)S(1)}, bf16[4,128,256]{2,1,0:T(8,128)(2,1)S(1)}, u32[]{:S(2)}, u32[]{:S(2)}) %collective-permute-start.5) | collective-permute-done | bytes 262176 | tf_op jit(solution)/shard_map/ppermute | solution.py:288
  21.7 3.8 %attention_grads.1 = (bf16[128,1024]{1,0:T(8,128)(2,1)}, f32[4,128,256]{2,1,0:T(8,128)S(1)}, bf16[4,128,256]{2,1,0:T(8,128)(2,1)S(1)}, bf16[4,128,256]{2,1,0:T(8,128)(2,1)S(1)}, bf16[4,128,256]{2,1,0:T(8,128)(2,1)S(1)}) custom-call(s32[32]{0:T(128)S(1)} %copy-done.2, s32[1,8]{1,0:T(1,128)S(1)} %copy-done.3, bf16[128,1024]{1,0:T(8,128)(2,1)S(1)} %bitcast.37, ...), custom_call_target="tpu_custom_call" | custom-call | flops 16609443840 | bytes 4194304 | tf_op jit(solution)/shard_map/attention_grads/pallas_call | solution.py:116
  25.6 0.1 collective-permute-start.7
  25.7 0.4 collective-permute-start.6
  26.1 1.0 %collective-permute-done.7 = bf16[4,128,256]{2,1,0:T(8,128)(2,1)S(1)} collective-permute-done((bf16[4,128,256]{2,1,0:T(8,128)(2,1)S(1)}, bf16[4,128,256]{2,1,0:T(8,128)(2,1)S(1)}, u32[]{:S(2)}, u32[]{:S(2)}) %collective-permute-start.7) | collective-permute-done | bytes 262176 | tf_op jit(solution)/shard_map/ppermute | solution.py:288
  27.1 0.1 add_convert_fusion
  27.2 1.8 %collective-permute-start.9 = (bf16[3,128,256]{2,1,0:T(8,128)(2,1)S(1)}, bf16[3,128,256]{2,1,0:T(8,128)(2,1)S(1)}, u32[]{:S(2)}, u32[]{:S(2)}) collective-permute-start(bf16[3,128,256]{2,1,0:T(8,128)(2,1)S(1)} %slice.63), channel_id=1, source_target_pairs={{0,2},{1,3},{2,0},{3,1},{4,6},{5,7},{6,4},{7,5},{8,10},{9,11},{10,... | collective-permute-start | bytes 589832 | tf_op jit(solution)/shard_map/ppermute | solution.py:288
  29.0 0.3 collective-permute-start.8
  29.3 0.0 collective-permute-done.6
  29.3 5.6 %collective-permute-done.9 = bf16[3,128,256]{2,1,0:T(8,128)(2,1)S(1)} collective-permute-done((bf16[3,128,256]{2,1,0:T(8,128)(2,1)S(1)}, bf16[3,128,256]{2,1,0:T(8,128)(2,1)S(1)}, u32[]{:S(2)}, u32[]{:S(2)}) %collective-permute-start.9) | collective-permute-done | bytes 196640 | tf_op jit(solution)/shard_map/ppermute | solution.py:288
  34.9 0.1 add_convert_fusion.1
  35.0 0.2 collective-permute-start.10
  35.2 1.7 %collective-permute-start.12 = (bf16[128,256]{1,0:T(8,128)(2,1)S(1)}, bf16[128,256]{1,0:T(8,128)(2,1)S(1)}, u32[]{:S(2)}, u32[]{:S(2)}) collective-permute-start(bf16[128,256]{1,0:T(8,128)(2,1)S(1)} %get-tuple-element.31), channel_id=1, source_target_pairs={{0,12},{1,13},{2,14},{3,15},{4,8},{5,9},{6,10},{7,11},{8,4},{9,5},... | collective-permute-start | bytes 196616 | tf_op jit(solution)/shard_map/ppermute | solution.py:288
  36.9 1.7 %collective-permute-start.11 = (bf16[128,256]{1,0:T(8,128)(2,1)S(1)}, bf16[128,256]{1,0:T(8,128)(2,1)S(1)}, u32[]{:S(2)}, u32[]{:S(2)}) collective-permute-start(bf16[128,256]{1,0:T(8,128)(2,1)S(1)} %get-tuple-element.32), channel_id=1, source_target_pairs={{0,8},{1,9},{2,10},{3,11},{4,12},{5,13},{6,14},{7,15},{8,0},{9,1},... | collective-permute-start | bytes 196616 | tf_op jit(solution)/shard_map/ppermute | solution.py:288
  38.6 0.0 collective-permute-done.8
  38.6 7.8 %collective-permute-done.10 = bf16[128,256]{1,0:T(8,128)(2,1)S(1)} collective-permute-done((bf16[128,256]{1,0:T(8,128)(2,1)S(1)}, bf16[128,256]{1,0:T(8,128)(2,1)S(1)}, u32[]{:S(2)}, u32[]{:S(2)}) %collective-permute-start.10) | collective-permute-done | bytes 65568 | tf_op jit(solution)/shard_map/ppermute | solution.py:288
  46.4 1.4 %collective-permute-done.12 = bf16[128,256]{1,0:T(8,128)(2,1)S(1)} collective-permute-done((bf16[128,256]{1,0:T(8,128)(2,1)S(1)}, bf16[128,256]{1,0:T(8,128)(2,1)S(1)}, u32[]{:S(2)}, u32[]{:S(2)}) %collective-permute-start.12) | collective-permute-done | bytes 65568 | tf_op jit(solution)/shard_map/ppermute | solution.py:288
  47.8 0.0 collective-permute-done.11
  47.8 0.1 fusion.8.refs_0_
  47.8 2.5 %collective-permute-start.18 = (bf16[128,256]{1,0:T(8,128)(2,1)S(1)}, bf16[128,256]{1,0:T(8,128)(2,1)S(1)}, u32[]{:S(2)}, u32[]{:S(2)}) collective-permute-start(bf16[128,256]{1,0:T(8,128)(2,1)S(1)} %fusion.8.refs_0_), channel_id=1, source_target_pairs={{0,20},{1,21},{2,22},{3,23},{4,16},{5,17},{6,18},{7,19},{8,28},{9,... | collective-permute-start | bytes 196616 | tf_op jit(solution)/shard_map/ppermute | solution.py:296
  50.3 0.6 collective-permute-start.16
  50.8 0.5 collective-permute-start.14
  51.4 0.0 collective-permute-start.13
  51.4 1.8 %collective-permute-done.18.refs_6_ = bf16[128,256]{1,0:T(8,128)(2,1)S(1)} collective-permute-done((bf16[128,256]{1,0:T(8,128)(2,1)S(1)}, bf16[128,256]{1,0:T(8,128)(2,1)S(1)}, u32[]{:S(2)}, u32[]{:S(2)}) %collective-permute-start.18) | collective-permute-done | bytes 65568 | tf_op jit(solution)/shard_map/ppermute | solution.py:296
  53.2 0.0 collective-permute-start.19
  53.2 1.4 %collective-permute-done.16.refs_4_ = bf16[128,256]{1,0:T(8,128)(2,1)S(1)} collective-permute-done((bf16[128,256]{1,0:T(8,128)(2,1)S(1)}, bf16[128,256]{1,0:T(8,128)(2,1)S(1)}, u32[]{:S(2)}, u32[]{:S(2)}) %collective-permute-start.16) | collective-permute-done | bytes 65568 | tf_op jit(solution)/shard_map/ppermute | solution.py:296
  54.6 0.0 collective-permute-start.17
  54.6 0.6 collective-permute-done.14.refs_2_
  55.1 0.7 collective-permute-done.17.refs_5_
  55.8 0.6 collective-permute-done.15.refs_3_
  56.4 0.0 all-to-all-done.x_ref
  56.4 0.7 %weight_terms.3 = (bf16[128,256]{1,0:T(8,128)(2,1)S(1)}, bf16[128,256]{1,0:T(8,128)(2,1)S(1)}, bf16[128,256]{1,0:T(8,128)(2,1)S(1)}, f32[128,256]{1,0:T(8,128)S(1)}) custom-call(bf16[8,1024,128]{2,1,0:T(8,128)(2,1)S(1)} %all-to-all-done.x_ref, bf16[128,256]{1,0:T(8,128)(2,1)S(1)} %fusion.8.refs_0_, bf16[128,256]{1,0:T(8,128)(2,1)S(1)} %collective-permute-done.13.refs_1_, ...), custom_call_target="tpu_custom_call" | custom-call | flops 268435456 | bytes 4194304 | tf_op jit(solution)/shard_map/weight_terms/pallas_call | solution.py:204
  57.1 0.6 collective-permute-start.23
  57.7 0.4 collective-permute-start.21
  58.1 3.5 %collective-permute-start.22 = (bf16[128,256]{1,0:T(8,128)(2,1)S(1)}, bf16[128,256]{1,0:T(8,128)(2,1)S(1)}, u32[]{:S(2)}, u32[]{:S(2)}) collective-permute-start(bf16[128,256]{1,0:T(8,128)(2,1)S(1)} %get-tuple-element.25), channel_id=1, source_target_pairs={{0,10},{1,11},{2,8},{3,9},{4,14},{5,15},{6,12},{7,13},{8,2},{9,3},... | collective-permute-start | bytes 196616 | tf_op jit(solution)/shard_map/ppermute | solution.py:288
  61.6 0.7 %weight_terms.2 = (f32[256,256]{1,0:T(8,128)S(1)}, bf16[256,256]{1,0:T(8,128)(2,1)S(1)}) custom-call(bf16[8,1024,128]{2,1,0:T(8,128)(2,1)S(1)} %all-to-all-done.x_ref, bf16[128,256]{1,0:T(8,128)(2,1)S(1)} %fusion.8.refs_0_, bf16[128,256]{1,0:T(8,128)(2,1)S(1)} %collective-permute-done.13.refs_1_, bf16[128,256]{1,0:T(8,128)(2,1)S(1)} %collective-permute-done.14.refs_2_, ...), custom_call_target="tpu_custom_call" | custom-call | flops 268435456 | bytes 4194304 | tf_op jit(solution)/shard_map/weight_terms/pallas_call | solution.py:204
  62.3 0.6 collective-permute-start.20
  62.9 0.0 collective-permute-done.23
  62.9 0.5 collective-permute-start.24
  63.4 0.6 slice_bitcast_fusion.4
  64.0 4.7 %collective-permute-done.20 = bf16[256,256]{1,0:T(8,128)(2,1)S(1)} collective-permute-done((bf16[256,256]{1,0:T(8,128)(2,1)S(1)}, bf16[256,256]{1,0:T(8,128)(2,1)S(1)}, u32[]{:S(2)}, u32[]{:S(2)}) %collective-permute-start.20) | collective-permute-done | bytes 131104 | tf_op jit(solution)/shard_map/ppermute | solution.py:288
  68.7 0.6 collective-permute-done.22
  69.3 0.1 collective-permute-done.24
  69.5 0.1 fusion.4
  69.5 0.7 %maximum_multiply_fusion = f32[1,256,256]{2,1,0:T(8,128)} fusion(f32[1,128,256]{2,1,0:T(8,128)S(1)} %get-tuple-element.29, f32[1,128,256]{2,1,0:T(8,128)S(1)} %get-tuple-element.28), kind=kLoop, calls=%fused_computation.3 | loop fusion | flops 131072 | bytes 524288 | tf_op jit(solution)/shard_map/mul | solution.py:354
  (15 shorter events, 0.1 us)
Async XLA Ops:
  1.4 5.8 %copy-start.4 = (bf16[128,256]{1,0:T(8,128)(2,1)}, bf16[128,256]{1,0:T(8,128)(2,1)S(1)}, u32[]{:S(2)}) copy-start(bf16[128,256]{1,0:T(8,128)(2,1)S(1)} %get-tuple-element.36._) | copy-start | bytes 196612
  1.4 8.7 %collective-permute-start.2 = (bf16[128,256]{1,0:T(8,128)(2,1)S(1)}, bf16[128,256]{1,0:T(8,128)(2,1)S(1)}, u32[]{:S(2)}, u32[]{:S(2)}) collective-permute-start(bf16[128,256]{1,0:T(8,128)(2,1)S(1)} %get-tuple-element.36._), channel_id=1, source_target_pairs={{0,12},{1,13},{2,14},{3,15},{4,8},{5,9},{6,10},{7,11},{8,4},{9,5},... | collective-permute-start | bytes 196616 | tf_op jit(solution)/shard_map/ppermute | solution.py:288
  6.5 5.6 %collective-permute-start.1 = (bf16[128,256]{1,0:T(8,128)(2,1)S(1)}, bf16[128,256]{1,0:T(8,128)(2,1)S(1)}, u32[]{:S(2)}, u32[]{:S(2)}) collective-permute-start(bf16[128,256]{1,0:T(8,128)(2,1)S(1)} %get-tuple-element.36._), channel_id=1, source_target_pairs={{0,8},{1,9},{2,10},{3,11},{4,12},{5,13},{6,14},{7,15},{8,0},{9,1},... | collective-permute-start | bytes 196616 | tf_op jit(solution)/shard_map/ppermute | solution.py:288
  6.5 5.6 %collective-permute-start = (bf16[128,256]{1,0:T(8,128)(2,1)S(1)}, bf16[128,256]{1,0:T(8,128)(2,1)S(1)}, u32[]{:S(2)}, u32[]{:S(2)}) collective-permute-start(bf16[128,256]{1,0:T(8,128)(2,1)S(1)} %get-tuple-element.36._), channel_id=1, source_target_pairs={{0,4},{1,5},{2,6},{3,7},{4,0},{5,1},{6,2},{7,3},{8,12},{9,13},{10,... | collective-permute-start | bytes 196616 | tf_op jit(solution)/shard_map/ppermute | solution.py:288
  12.2 9.5 %copy-start = (bf16[1,128,1024]{2,1,0:T(8,128)(2,1)S(1)}, bf16[1,128,1024]{2,1,0:T(8,128)(2,1)}, u32[]{:S(2)}) copy-start(bf16[1,128,1024]{2,1,0:T(8,128)(2,1)} %param.8) | copy-start | bytes 786436
  12.2 9.5 %copy-start.1 = (bf16[1,128,1024]{2,1,0:T(8,128)(2,1)S(1)}, bf16[1,128,1024]{2,1,0:T(8,128)(2,1)}, u32[]{:S(2)}) copy-start(bf16[1,128,1024]{2,1,0:T(8,128)(2,1)} %param.11) | copy-start | bytes 786436
  12.2 9.5 %copy-start.2 = (s32[32]{0:T(128)S(1)}, s32[32]{0:T(128)}, u32[]{:S(2)}) copy-start(s32[32]{0:T(128)} %order.1) | copy-start | bytes 388
  12.2 9.5 %copy-start.3 = (s32[1,8]{1,0:T(1,128)S(1)}, s32[1,8]{1,0:T(1,128)}, u32[]{:S(2)}) copy-start(s32[1,8]{1,0:T(1,128)} %lengths.1) | copy-start | bytes 100
  12.2 7.9 %collective-permute-start.3 = (bf16[4,128,256]{2,1,0:T(8,128)(2,1)S(1)}, bf16[4,128,256]{2,1,0:T(8,128)(2,1)S(1)}, u32[]{:S(2)}, u32[]{:S(2)}) collective-permute-start(bf16[4,128,256]{2,1,0:T(8,128)(2,1)S(1)} %pad_maximum_fusion.refs_0_), channel_id=1, source_target_pairs={{0,2},{1,3},{2,0},{3,1},{4,6},{5,7},{6,4},{7,5},{8,10},{9,11},{10,... | collective-permute-start | bytes 786440 | tf_op jit(solution)/shard_map/ppermute | solution.py:288
  13.8 42.5 %all-to-all-start = ((bf16[8,1024,128]{2,1,0:T(8,128)(2,1)}), bf16[8,1024,128]{2,1,0:T(8,128)(2,1)S(1)}, u32[]{:S(2)}, u32[]{:S(2)}) async-start(bf16[8,1024,128]{2,1,0:T(8,128)(2,1)} %columns_first.1), calls=%async_computation | async-start | bytes 4194304 | tf_op jit(solution)/shard_map/all_to_all | solution.py:310
  17.4 2.8 %collective-permute-start.4 = (bf16[4,128,256]{2,1,0:T(8,128)(2,1)S(1)}, bf16[4,128,256]{2,1,0:T(8,128)(2,1)S(1)}, u32[]{:S(2)}, u32[]{:S(2)}) collective-permute-start(bf16[4,128,256]{2,1,0:T(8,128)(2,1)S(1)} %pad_maximum_fusion.refs_0_), channel_id=1, source_target_pairs={{0,1},{1,0},{2,3},{3,2},{4,5},{5,4},{6,7},{7,6},{8,9},{9,8},{10,11... | collective-permute-start | bytes 786440 | tf_op jit(solution)/shard_map/ppermute | solution.py:288
  20.2 1.5 %collective-permute-start.5 = (bf16[4,128,256]{2,1,0:T(8,128)(2,1)S(1)}, bf16[4,128,256]{2,1,0:T(8,128)(2,1)S(1)}, u32[]{:S(2)}, u32[]{:S(2)}) collective-permute-start(bf16[4,128,256]{2,1,0:T(8,128)(2,1)S(1)} %collective-permute-done.3.refs_1_), channel_id=1, source_target_pairs={{0,1},{1,0},{2,3},{3,2},{4,5},{5,4},{6,7},{7,6},{8,9},{9,8},{10,11... | collective-permute-start | bytes 786440 | tf_op jit(solution)/shard_map/ppermute | solution.py:288
  25.6 1.5 %collective-permute-start.7 = (bf16[4,128,256]{2,1,0:T(8,128)(2,1)S(1)}, bf16[4,128,256]{2,1,0:T(8,128)(2,1)S(1)}, u32[]{:S(2)}, u32[]{:S(2)}) collective-permute-start(bf16[4,128,256]{2,1,0:T(8,128)(2,1)S(1)} %get-tuple-element.21), channel_id=1, source_target_pairs={{0,1},{1,0},{2,3},{3,2},{4,5},{5,4},{6,7},{7,6},{8,9},{9,8},{10,11... | collective-permute-start | bytes 786440 | tf_op jit(solution)/shard_map/ppermute | solution.py:288
  25.7 3.6 %collective-permute-start.6 = (bf16[4,128,256]{2,1,0:T(8,128)(2,1)S(1)}, bf16[4,128,256]{2,1,0:T(8,128)(2,1)S(1)}, u32[]{:S(2)}, u32[]{:S(2)}) collective-permute-start(bf16[4,128,256]{2,1,0:T(8,128)(2,1)S(1)} %get-tuple-element.19), channel_id=1, source_target_pairs={{0,1},{1,0},{2,3},{3,2},{4,5},{5,4},{6,7},{7,6},{8,9},{9,8},{10,11... | collective-permute-start | bytes 786440 | tf_op jit(solution)/shard_map/ppermute | solution.py:288
  27.2 7.7 %collective-permute-start.9 = (bf16[3,128,256]{2,1,0:T(8,128)(2,1)S(1)}, bf16[3,128,256]{2,1,0:T(8,128)(2,1)S(1)}, u32[]{:S(2)}, u32[]{:S(2)}) collective-permute-start(bf16[3,128,256]{2,1,0:T(8,128)(2,1)S(1)} %slice.63), channel_id=1, source_target_pairs={{0,2},{1,3},{2,0},{3,1},{4,6},{5,7},{6,4},{7,5},{8,10},{9,11},{10,... | collective-permute-start | bytes 589832 | tf_op jit(solution)/shard_map/ppermute | solution.py:288
  29.0 9.6 %collective-permute-start.8 = (bf16[128,256]{1,0:T(8,128)(2,1)S(1)}, bf16[128,256]{1,0:T(8,128)(2,1)S(1)}, u32[]{:S(2)}, u32[]{:S(2)}) collective-permute-start(bf16[128,256]{1,0:T(8,128)(2,1)S(1)} %slice_bitcast_fusion.3), channel_id=1, source_target_pairs={{0,2},{1,3},{2,0},{3,1},{4,6},{5,7},{6,4},{7,5},{8,10},{9,11},{10,... | collective-permute-start | bytes 196616 | tf_op jit(solution)/shard_map/ppermute | solution.py:288
  35.0 11.4 %collective-permute-start.10 = (bf16[128,256]{1,0:T(8,128)(2,1)S(1)}, bf16[128,256]{1,0:T(8,128)(2,1)S(1)}, u32[]{:S(2)}, u32[]{:S(2)}) collective-permute-start(bf16[128,256]{1,0:T(8,128)(2,1)S(1)} %get-tuple-element.30), channel_id=1, source_target_pairs={{0,4},{1,5},{2,6},{3,7},{4,0},{5,1},{6,2},{7,3},{8,12},{9,13},{10,... | collective-permute-start | bytes 196616 | tf_op jit(solution)/shard_map/ppermute | solution.py:288
  35.2 12.6 %collective-permute-start.12 = (bf16[128,256]{1,0:T(8,128)(2,1)S(1)}, bf16[128,256]{1,0:T(8,128)(2,1)S(1)}, u32[]{:S(2)}, u32[]{:S(2)}) collective-permute-start(bf16[128,256]{1,0:T(8,128)(2,1)S(1)} %get-tuple-element.31), channel_id=1, source_target_pairs={{0,12},{1,13},{2,14},{3,15},{4,8},{5,9},{6,10},{7,11},{8,4},{9,5},... | collective-permute-start | bytes 196616 | tf_op jit(solution)/shard_map/ppermute | solution.py:288
  36.9 10.9 %collective-permute-start.11 = (bf16[128,256]{1,0:T(8,128)(2,1)S(1)}, bf16[128,256]{1,0:T(8,128)(2,1)S(1)}, u32[]{:S(2)}, u32[]{:S(2)}) collective-permute-start(bf16[128,256]{1,0:T(8,128)(2,1)S(1)} %get-tuple-element.32), channel_id=1, source_target_pairs={{0,8},{1,9},{2,10},{3,11},{4,12},{5,13},{6,14},{7,15},{8,0},{9,1},... | collective-permute-start | bytes 196616 | tf_op jit(solution)/shard_map/ppermute | solution.py:288
  47.8 5.3 %collective-permute-start.18 = (bf16[128,256]{1,0:T(8,128)(2,1)S(1)}, bf16[128,256]{1,0:T(8,128)(2,1)S(1)}, u32[]{:S(2)}, u32[]{:S(2)}) collective-permute-start(bf16[128,256]{1,0:T(8,128)(2,1)S(1)} %fusion.8.refs_0_), channel_id=1, source_target_pairs={{0,20},{1,21},{2,22},{3,23},{4,16},{5,17},{6,18},{7,19},{8,28},{9,... | collective-permute-start | bytes 196616 | tf_op jit(solution)/shard_map/ppermute | solution.py:296
  50.3 4.3 %collective-permute-start.16 = (bf16[128,256]{1,0:T(8,128)(2,1)S(1)}, bf16[128,256]{1,0:T(8,128)(2,1)S(1)}, u32[]{:S(2)}, u32[]{:S(2)}) collective-permute-start(bf16[128,256]{1,0:T(8,128)(2,1)S(1)} %fusion.8.refs_0_), channel_id=1, source_target_pairs={{0,16},{1,17},{2,18},{3,19},{4,20},{5,21},{6,22},{7,23},{8,24},{9,... | collective-permute-start | bytes 196616 | tf_op jit(solution)/shard_map/ppermute | solution.py:296
  50.8 4.3 %collective-permute-start.14 = (bf16[128,256]{1,0:T(8,128)(2,1)S(1)}, bf16[128,256]{1,0:T(8,128)(2,1)S(1)}, u32[]{:S(2)}, u32[]{:S(2)}) collective-permute-start(bf16[128,256]{1,0:T(8,128)(2,1)S(1)} %fusion.8.refs_0_), channel_id=1, source_target_pairs={{0,4},{1,5},{2,6},{3,7},{4,0},{5,1},{6,2},{7,3},{8,12},{9,13},{10,... | collective-permute-start | bytes 196616 | tf_op jit(solution)/shard_map/ppermute | solution.py:296
  51.4 3.7 %collective-permute-start.13 = (bf16[128,256]{1,0:T(8,128)(2,1)S(1)}, bf16[128,256]{1,0:T(8,128)(2,1)S(1)}, u32[]{:S(2)}, u32[]{:S(2)}) collective-permute-start(bf16[128,256]{1,0:T(8,128)(2,1)S(1)} %fusion.8.refs_0_), channel_id=1, source_target_pairs={{0,1},{1,0},{2,3},{3,2},{4,5},{5,4},{6,7},{7,6},{8,9},{9,8},{10,11... | collective-permute-start | bytes 196616 | tf_op jit(solution)/shard_map/ppermute | solution.py:288
  53.2 2.0 %collective-permute-start.19 = (bf16[128,256]{1,0:T(8,128)(2,1)S(1)}, bf16[128,256]{1,0:T(8,128)(2,1)S(1)}, u32[]{:S(2)}, u32[]{:S(2)}) collective-permute-start(bf16[128,256]{1,0:T(8,128)(2,1)S(1)} %collective-permute-done.18.refs_6_), channel_id=1, source_target_pairs={{0,1},{1,0},{2,3},{3,2},{4,5},{5,4},{6,7},{7,6},{8,9},{9,8},{10,11... | collective-permute-start | bytes 196616 | tf_op jit(solution)/shard_map/ppermute | solution.py:288
  54.6 1.3 %collective-permute-start.17 = (bf16[128,256]{1,0:T(8,128)(2,1)S(1)}, bf16[128,256]{1,0:T(8,128)(2,1)S(1)}, u32[]{:S(2)}, u32[]{:S(2)}) collective-permute-start(bf16[128,256]{1,0:T(8,128)(2,1)S(1)} %collective-permute-done.16.refs_4_), channel_id=1, source_target_pairs={{0,1},{1,0},{2,3},{3,2},{4,5},{5,4},{6,7},{7,6},{8,9},{9,8},{10,11... | collective-permute-start | bytes 196616 | tf_op jit(solution)/shard_map/ppermute | solution.py:288
  55.1 1.3 %collective-permute-start.15 = (bf16[128,256]{1,0:T(8,128)(2,1)S(1)}, bf16[128,256]{1,0:T(8,128)(2,1)S(1)}, u32[]{:S(2)}, u32[]{:S(2)}) collective-permute-start(bf16[128,256]{1,0:T(8,128)(2,1)S(1)} %collective-permute-done.14.refs_2_), channel_id=1, source_target_pairs={{0,1},{1,0},{2,3},{3,2},{4,5},{5,4},{6,7},{7,6},{8,9},{9,8},{10,11... | collective-permute-start | bytes 196616 | tf_op jit(solution)/shard_map/ppermute | solution.py:288
  57.1 5.8 %collective-permute-start.23 = (bf16[128,256]{1,0:T(8,128)(2,1)S(1)}, bf16[128,256]{1,0:T(8,128)(2,1)S(1)}, u32[]{:S(2)}, u32[]{:S(2)}) collective-permute-start(bf16[128,256]{1,0:T(8,128)(2,1)S(1)} %get-tuple-element.27), channel_id=1, source_target_pairs={{0,2},{1,3},{2,0},{3,1},{4,6},{5,7},{6,4},{7,5},{8,10},{9,11},{10,... | collective-permute-start | bytes 196616 | tf_op jit(solution)/shard_map/ppermute | solution.py:288
  57.7 11.0 %collective-permute-start.21 = (bf16[128,256]{1,0:T(8,128)(2,1)S(1)}, bf16[128,256]{1,0:T(8,128)(2,1)S(1)}, u32[]{:S(2)}, u32[]{:S(2)}) collective-permute-start(bf16[128,256]{1,0:T(8,128)(2,1)S(1)} %get-tuple-element.24), channel_id=1, source_target_pairs={{0,8},{1,9},{2,10},{3,11},{4,12},{5,13},{6,14},{7,15},{8,0},{9,1},... | collective-permute-start | bytes 196616 | tf_op jit(solution)/shard_map/ppermute | solution.py:288
  58.1 11.2 %collective-permute-start.22 = (bf16[128,256]{1,0:T(8,128)(2,1)S(1)}, bf16[128,256]{1,0:T(8,128)(2,1)S(1)}, u32[]{:S(2)}, u32[]{:S(2)}) collective-permute-start(bf16[128,256]{1,0:T(8,128)(2,1)S(1)} %get-tuple-element.25), channel_id=1, source_target_pairs={{0,10},{1,11},{2,8},{3,9},{4,14},{5,15},{6,12},{7,13},{8,2},{9,3},... | collective-permute-start | bytes 196616 | tf_op jit(solution)/shard_map/ppermute | solution.py:288
  62.3 6.4 %collective-permute-start.20 = (bf16[256,256]{1,0:T(8,128)(2,1)S(1)}, bf16[256,256]{1,0:T(8,128)(2,1)S(1)}, u32[]{:S(2)}, u32[]{:S(2)}) collective-permute-start(bf16[256,256]{1,0:T(8,128)(2,1)S(1)} %get-tuple-element.23), channel_id=1, source_target_pairs={{0,2},{1,3},{2,0},{3,1},{4,6},{5,7},{6,4},{7,5},{8,10},{9,11},{10,... | collective-permute-start | bytes 393224 | tf_op jit(solution)/shard_map/ppermute | solution.py:288
  62.9 6.6 %collective-permute-start.24 = (bf16[128,256]{1,0:T(8,128)(2,1)S(1)}, bf16[128,256]{1,0:T(8,128)(2,1)S(1)}, u32[]{:S(2)}, u32[]{:S(2)}) collective-permute-start(bf16[128,256]{1,0:T(8,128)(2,1)S(1)} %add_convert_fusion.2), channel_id=1, source_target_pairs={{0,8},{1,9},{2,10},{3,11},{4,12},{5,13},{6,14},{7,15},{8,0},{9,1},... | collective-permute-start | bytes 196616 | tf_op jit(solution)/shard_map/ppermute | solution.py:288

commit v7 on v6

--- a/solution.py
+++ b/solution.py
@@ -298,7 +298,8 @@
         )
 
     kv = jnp.concatenate([keys[0], values[0]], axis=1)
-    tops = [kv] + [swap(kv, 2 * mid * j) for j in range(1, top)]
+    tops = {j: swap(kv, 2 * mid * j) for j in (1, 3, 2)}
+    tops = [kv] + [tops[j] for j in range(1, top)]
     base = jnp.stack(tops)
 
     xt = columns_first(layer_input[0], kv, members, spread, n, dps)

time: 70.5 us -> 70.5 us (level)
  no operation moved by 1% of the time
where the time goes in v7:
time: 70.5 us; the launch traced here: 70.3 us
  waiting for transfers between devices  32.1 us (46%)
  starting transfers between devices  26.6 us (38%)
  Pallas kernels  8.24 us (12%)
  other arithmetic  1.81 us (3%)
  between operations  0.81 us (1%)
    ppermute x22, waiting for transfers between devices, swap(): return lax.ppermute(x, 'ctx', [(i, i ^ k) for i in range(n)])  28.4 us
    ppermute x22, starting transfers between devices, swap(): return lax.ppermute(x, 'ctx', [(i, i ^ k) for i in range(n)])  19.4 us
    pallas_call x1, Pallas kernels, attention(): pl.pallas_call(body, out_shape=[jax.ShapeDtypeStruct((rows, width), jnp.b...  3.84 us
    ppermute x3, waiting for transfers between devices, cross(): lax.ppermute(x, joint, [(a * n + b, (a ^ i) * n + (b ^ m)) for a in range...  3.72 us
    all_to_all x1, starting transfers between devices, per_device(): xt = lax.all_to_all(xt, joint, 0, 0, axis_index_groups=groups, tiled=True)  3.6 us
    ppermute x3, starting transfers between devices, cross(): lax.ppermute(x, joint, [(a * n + b, (a ^ i) * n + (b ^ m)) for a in range...  3.55 us
    pallas_call x1, Pallas kernels, columns_first(): pl.pallas_call(functools.partial(columns_kernel, places=places, height=he...  2.95 us
    pallas_call x2, Pallas kernels, weight_terms(): pl.pallas_call(functools.partial(weight_kernel, members=members, spread=s...  1.45 us
  transfers between devices with their start and end apart: 26, of which 15 were waited for; matrix products, arithmetic and copies ran while one was open for 1% of the time, Pallas kernels for 11%

profile of v7, /device:TPU:0, one launch (start us, length us, event | category | flops | bytes accessed | tf_op | source)
XLA Modules:
  0.0 70.3 jit_solution(11689767564412840868)
XLA Ops:
  0.6 0.8 %fusion.9 = (bf16[1,128,256]{2,1,0:T(8,128)(2,1)S(1)}, bf16[128,256]{1,0:T(8,128)(2,1)S(1)}) fusion(bf16[128,128]{1,0:T(8,128)(2,1)} %bitcast.43, bf16[128,128]{1,0:T(8,128)(2,1)} %bitcast.44), kind=kLoop, calls=%fused_computation.24 | loop fusion | flops 131072 | bytes 196608 | tf_op jit(solution)/shard_map/stack | solution.py:303
  1.4 0.0 copy-start.4
  1.4 5.1 %collective-permute-start.2 = (bf16[128,256]{1,0:T(8,128)(2,1)S(1)}, bf16[128,256]{1,0:T(8,128)(2,1)S(1)}, u32[]{:S(2)}, u32[]{:S(2)}) collective-permute-start(bf16[128,256]{1,0:T(8,128)(2,1)S(1)} %get-tuple-element.36._), channel_id=1, source_target_pairs={{0,12},{1,13},{2,14},{3,15},{4,8},{5,9},{6,10},{7,11},{8,4},{9,5},... | collective-permute-start | bytes 196616 | tf_op jit(solution)/shard_map/ppermute | solution.py:288
  6.5 0.0 collective-permute-start.1
  6.5 0.6 collective-permute-start
  7.2 3.0 %columns_first.1 = bf16[8,1024,128]{2,1,0:T(8,128)(2,1)} custom-call(bf16[128,8192]{1,0:T(8,128)(2,1)} %bitcast.39, bf16[128,256]{1,0:T(8,128)(2,1)} %copy-done.4), custom_call_target="tpu_custom_call" | custom-call | bytes 4194304 | tf_op jit(solution)/shard_map/columns_first/pallas_call | solution.py:255
  10.2 0.0 collective-permute-done.2
  10.2 2.0 %collective-permute-done.1 = bf16[128,256]{1,0:T(8,128)(2,1)S(1)} collective-permute-done((bf16[128,256]{1,0:T(8,128)(2,1)S(1)}, bf16[128,256]{1,0:T(8,128)(2,1)S(1)}, u32[]{:S(2)}, u32[]{:S(2)}) %collective-permute-start.1) | collective-permute-done | bytes 65568 | tf_op jit(solution)/shard_map/ppermute | solution.py:288
  12.2 0.0 collective-permute-done
  12.2 0.0 copy-start
  12.2 0.0 copy-start.1
  12.2 0.0 copy-start.2
  12.2 0.0 copy-start.3
  12.2 1.6 %collective-permute-start.3 = (bf16[4,128,256]{2,1,0:T(8,128)(2,1)S(1)}, bf16[4,128,256]{2,1,0:T(8,128)(2,1)S(1)}, u32[]{:S(2)}, u32[]{:S(2)}) collective-permute-start(bf16[4,128,256]{2,1,0:T(8,128)(2,1)S(1)} %pad_maximum_fusion.refs_0_), channel_id=1, source_target_pairs={{0,2},{1,3},{2,0},{3,1},{4,6},{5,7},{6,4},{7,5},{8,10},{9,11},{10,... | collective-permute-start | bytes 786440 | tf_op jit(solution)/shard_map/ppermute | solution.py:288
  13.8 3.6 %all-to-all-start = ((bf16[8,1024,128]{2,1,0:T(8,128)(2,1)}), bf16[8,1024,128]{2,1,0:T(8,128)(2,1)S(1)}, u32[]{:S(2)}, u32[]{:S(2)}) async-start(bf16[8,1024,128]{2,1,0:T(8,128)(2,1)} %columns_first.1), calls=%async_computation | async-start | bytes 4194304 | tf_op jit(solution)/shard_map/all_to_all | solution.py:311
  17.4 0.4 collective-permute-start.4
  17.8 2.3 %collective-permute-done.3.refs_1_ = bf16[4,128,256]{2,1,0:T(8,128)(2,1)S(1)} collective-permute-done((bf16[4,128,256]{2,1,0:T(8,128)(2,1)S(1)}, bf16[4,128,256]{2,1,0:T(8,128)(2,1)S(1)}, u32[]{:S(2)}, u32[]{:S(2)}) %collective-permute-start.3) | collective-permute-done | bytes 262176 | tf_op jit(solution)/shard_map/ppermute | solution.py:288
  20.2 0.0 collective-permute-start.5
  20.2 0.0 collective-permute-done.4.refs_2_
  20.2 1.5 %collective-permute-done.5.refs_3_ = bf16[4,128,256]{2,1,0:T(8,128)(2,1)S(1)} collective-permute-done((bf16[4,128,256]{2,1,0:T(8,128)(2,1)S(1)}, bf16[4,128,256]{2,1,0:T(8,128)(2,1)S(1)}, u32[]{:S(2)}, u32[]{:S(2)}) %collective-permute-start.5) | collective-permute-done | bytes 262176 | tf_op jit(solution)/shard_map/ppermute | solution.py:288
  21.7 3.8 %attention_grads.1 = (bf16[128,1024]{1,0:T(8,128)(2,1)}, f32[4,128,256]{2,1,0:T(8,128)S(1)}, bf16[4,128,256]{2,1,0:T(8,128)(2,1)S(1)}, bf16[4,128,256]{2,1,0:T(8,128)(2,1)S(1)}, bf16[4,128,256]{2,1,0:T(8,128)(2,1)S(1)}) custom-call(s32[32]{0:T(128)S(1)} %copy-done.2, s32[1,8]{1,0:T(1,128)S(1)} %copy-done.3, bf16[128,1024]{1,0:T(8,128)(2,1)S(1)} %bitcast.37, ...), custom_call_target="tpu_custom_call" | custom-call | flops 16609443840 | bytes 4194304 | tf_op jit(solution)/shard_map/attention_grads/pallas_call | solution.py:116
  25.6 0.1 collective-permute-start.7
  25.7 0.4 collective-permute-start.6
  26.1 1.0 %collective-permute-done.7 = bf16[4,128,256]{2,1,0:T(8,128)(2,1)S(1)} collective-permute-done((bf16[4,128,256]{2,1,0:T(8,128)(2,1)S(1)}, bf16[4,128,256]{2,1,0:T(8,128)(2,1)S(1)}, u32[]{:S(2)}, u32[]{:S(2)}) %collective-permute-start.7) | collective-permute-done | bytes 262176 | tf_op jit(solution)/shard_map/ppermute | solution.py:288
  27.1 0.1 add_convert_fusion
  27.2 1.8 %collective-permute-start.9 = (bf16[3,128,256]{2,1,0:T(8,128)(2,1)S(1)}, bf16[3,128,256]{2,1,0:T(8,128)(2,1)S(1)}, u32[]{:S(2)}, u32[]{:S(2)}) collective-permute-start(bf16[3,128,256]{2,1,0:T(8,128)(2,1)S(1)} %slice.63), channel_id=1, source_target_pairs={{0,2},{1,3},{2,0},{3,1},{4,6},{5,7},{6,4},{7,5},{8,10},{9,11},{10,... | collective-permute-start | bytes 589832 | tf_op jit(solution)/shard_map/ppermute | solution.py:288
  29.0 0.3 collective-permute-start.8
  29.3 0.0 collective-permute-done.6
  29.3 5.6 %collective-permute-done.9 = bf16[3,128,256]{2,1,0:T(8,128)(2,1)S(1)} collective-permute-done((bf16[3,128,256]{2,1,0:T(8,128)(2,1)S(1)}, bf16[3,128,256]{2,1,0:T(8,128)(2,1)S(1)}, u32[]{:S(2)}, u32[]{:S(2)}) %collective-permute-start.9) | collective-permute-done | bytes 196640 | tf_op jit(solution)/shard_map/ppermute | solution.py:288
  34.9 0.1 add_convert_fusion.1
  35.0 0.2 collective-permute-start.10
  35.2 1.7 %collective-permute-start.12 = (bf16[128,256]{1,0:T(8,128)(2,1)S(1)}, bf16[128,256]{1,0:T(8,128)(2,1)S(1)}, u32[]{:S(2)}, u32[]{:S(2)}) collective-permute-start(bf16[128,256]{1,0:T(8,128)(2,1)S(1)} %get-tuple-element.31), channel_id=1, source_target_pairs={{0,12},{1,13},{2,14},{3,15},{4,8},{5,9},{6,10},{7,11},{8,4},{9,5},... | collective-permute-start | bytes 196616 | tf_op jit(solution)/shard_map/ppermute | solution.py:288
  36.9 1.7 %collective-permute-start.11 = (bf16[128,256]{1,0:T(8,128)(2,1)S(1)}, bf16[128,256]{1,0:T(8,128)(2,1)S(1)}, u32[]{:S(2)}, u32[]{:S(2)}) collective-permute-start(bf16[128,256]{1,0:T(8,128)(2,1)S(1)} %get-tuple-element.32), channel_id=1, source_target_pairs={{0,8},{1,9},{2,10},{3,11},{4,12},{5,13},{6,14},{7,15},{8,0},{9,1},... | collective-permute-start | bytes 196616 | tf_op jit(solution)/shard_map/ppermute | solution.py:288
  38.6 0.0 collective-permute-done.8
  38.6 7.8 %collective-permute-done.10 = bf16[128,256]{1,0:T(8,128)(2,1)S(1)} collective-permute-done((bf16[128,256]{1,0:T(8,128)(2,1)S(1)}, bf16[128,256]{1,0:T(8,128)(2,1)S(1)}, u32[]{:S(2)}, u32[]{:S(2)}) %collective-permute-start.10) | collective-permute-done | bytes 65568 | tf_op jit(solution)/shard_map/ppermute | solution.py:288
  46.4 1.4 %collective-permute-done.12 = bf16[128,256]{1,0:T(8,128)(2,1)S(1)} collective-permute-done((bf16[128,256]{1,0:T(8,128)(2,1)S(1)}, bf16[128,256]{1,0:T(8,128)(2,1)S(1)}, u32[]{:S(2)}, u32[]{:S(2)}) %collective-permute-start.12) | collective-permute-done | bytes 65568 | tf_op jit(solution)/shard_map/ppermute | solution.py:288
  47.8 0.0 collective-permute-done.11
  47.8 0.1 fusion.8.refs_0_
  47.8 2.5 %collective-permute-start.18 = (bf16[128,256]{1,0:T(8,128)(2,1)S(1)}, bf16[128,256]{1,0:T(8,128)(2,1)S(1)}, u32[]{:S(2)}, u32[]{:S(2)}) collective-permute-start(bf16[128,256]{1,0:T(8,128)(2,1)S(1)} %fusion.8.refs_0_), channel_id=1, source_target_pairs={{0,20},{1,21},{2,22},{3,23},{4,16},{5,17},{6,18},{7,19},{8,28},{9,... | collective-permute-start | bytes 196616 | tf_op jit(solution)/shard_map/ppermute | solution.py:296
  50.3 0.6 collective-permute-start.16
  50.8 0.5 collective-permute-start.14
  51.4 0.0 collective-permute-start.13
  51.4 1.8 %collective-permute-done.18.refs_6_ = bf16[128,256]{1,0:T(8,128)(2,1)S(1)} collective-permute-done((bf16[128,256]{1,0:T(8,128)(2,1)S(1)}, bf16[128,256]{1,0:T(8,128)(2,1)S(1)}, u32[]{:S(2)}, u32[]{:S(2)}) %collective-permute-start.18) | collective-permute-done | bytes 65568 | tf_op jit(solution)/shard_map/ppermute | solution.py:296
  53.2 0.0 collective-permute-start.19
  53.2 1.4 %collective-permute-done.16.refs_4_ = bf16[128,256]{1,0:T(8,128)(2,1)S(1)} collective-permute-done((bf16[128,256]{1,0:T(8,128)(2,1)S(1)}, bf16[128,256]{1,0:T(8,128)(2,1)S(1)}, u32[]{:S(2)}, u32[]{:S(2)}) %collective-permute-start.16) | collective-permute-done | bytes 65568 | tf_op jit(solution)/shard_map/ppermute | solution.py:296
  54.6 0.0 collective-permute-start.17
  54.6 0.6 collective-permute-done.14.refs_2_
  55.1 0.7 collective-permute-done.17.refs_5_
  55.8 0.6 collective-permute-done.15.refs_3_
  56.4 0.0 all-to-all-done.x_ref
  56.4 0.7 %weight_terms.3 = (bf16[128,256]{1,0:T(8,128)(2,1)S(1)}, bf16[128,256]{1,0:T(8,128)(2,1)S(1)}, bf16[128,256]{1,0:T(8,128)(2,1)S(1)}, f32[128,256]{1,0:T(8,128)S(1)}) custom-call(bf16[8,1024,128]{2,1,0:T(8,128)(2,1)S(1)} %all-to-all-done.x_ref, bf16[128,256]{1,0:T(8,128)(2,1)S(1)} %fusion.8.refs_0_, bf16[128,256]{1,0:T(8,128)(2,1)S(1)} %collective-permute-done.13.refs_1_, ...), custom_call_target="tpu_custom_call" | custom-call | flops 268435456 | bytes 4194304 | tf_op jit(solution)/shard_map/weight_terms/pallas_call | solution.py:204
  57.1 0.6 collective-permute-start.23
  57.7 0.4 collective-permute-start.21
  58.1 3.5 %collective-permute-start.22 = (bf16[128,256]{1,0:T(8,128)(2,1)S(1)}, bf16[128,256]{1,0:T(8,128)(2,1)S(1)}, u32[]{:S(2)}, u32[]{:S(2)}) collective-permute-start(bf16[128,256]{1,0:T(8,128)(2,1)S(1)} %get-tuple-element.25), channel_id=1, source_target_pairs={{0,10},{1,11},{2,8},{3,9},{4,14},{5,15},{6,12},{7,13},{8,2},{9,3},... | collective-permute-start | bytes 196616 | tf_op jit(solution)/shard_map/ppermute | solution.py:288
  61.6 0.7 %weight_terms.2 = (f32[256,256]{1,0:T(8,128)S(1)}, bf16[256,256]{1,0:T(8,128)(2,1)S(1)}) custom-call(bf16[8,1024,128]{2,1,0:T(8,128)(2,1)S(1)} %all-to-all-done.x_ref, bf16[128,256]{1,0:T(8,128)(2,1)S(1)} %fusion.8.refs_0_, bf16[128,256]{1,0:T(8,128)(2,1)S(1)} %collective-permute-done.13.refs_1_, bf16[128,256]{1,0:T(8,128)(2,1)S(1)} %collective-permute-done.14.refs_2_, ...), custom_call_target="tpu_custom_call" | custom-call | flops 268435456 | bytes 4194304 | tf_op jit(solution)/shard_map/weight_terms/pallas_call | solution.py:204
  62.3 0.6 collective-permute-start.20
  62.9 0.0 collective-permute-done.23
  62.9 0.5 collective-permute-start.24
  63.4 0.6 slice_bitcast_fusion.4
  64.0 4.7 %collective-permute-done.20 = bf16[256,256]{1,0:T(8,128)(2,1)S(1)} collective-permute-done((bf16[256,256]{1,0:T(8,128)(2,1)S(1)}, bf16[256,256]{1,0:T(8,128)(2,1)S(1)}, u32[]{:S(2)}, u32[]{:S(2)}) %collective-permute-start.20) | collective-permute-done | bytes 131104 | tf_op jit(solution)/shard_map/ppermute | solution.py:288
  68.7 0.6 collective-permute-done.22
  69.3 0.1 collective-permute-done.24
  69.5 0.1 fusion.4
  69.5 0.7 %maximum_multiply_fusion = f32[1,256,256]{2,1,0:T(8,128)} fusion(f32[1,128,256]{2,1,0:T(8,128)S(1)} %get-tuple-element.29, f32[1,128,256]{2,1,0:T(8,128)S(1)} %get-tuple-element.28), kind=kLoop, calls=%fused_computation.3 | loop fusion | flops 131072 | bytes 524288 | tf_op jit(solution)/shard_map/mul | solution.py:355
  (15 shorter events, 0.1 us)
Async XLA Ops:
  1.4 5.8 %copy-start.4 = (bf16[128,256]{1,0:T(8,128)(2,1)}, bf16[128,256]{1,0:T(8,128)(2,1)S(1)}, u32[]{:S(2)}) copy-start(bf16[128,256]{1,0:T(8,128)(2,1)S(1)} %get-tuple-element.36._) | copy-start | bytes 196612
  1.4 8.7 %collective-permute-start.2 = (bf16[128,256]{1,0:T(8,128)(2,1)S(1)}, bf16[128,256]{1,0:T(8,128)(2,1)S(1)}, u32[]{:S(2)}, u32[]{:S(2)}) collective-permute-start(bf16[128,256]{1,0:T(8,128)(2,1)S(1)} %get-tuple-element.36._), channel_id=1, source_target_pairs={{0,12},{1,13},{2,14},{3,15},{4,8},{5,9},{6,10},{7,11},{8,4},{9,5},... | collective-permute-start | bytes 196616 | tf_op jit(solution)/shard_map/ppermute | solution.py:288
  6.5 5.6 %collective-permute-start.1 = (bf16[128,256]{1,0:T(8,128)(2,1)S(1)}, bf16[128,256]{1,0:T(8,128)(2,1)S(1)}, u32[]{:S(2)}, u32[]{:S(2)}) collective-permute-start(bf16[128,256]{1,0:T(8,128)(2,1)S(1)} %get-tuple-element.36._), channel_id=1, source_target_pairs={{0,8},{1,9},{2,10},{3,11},{4,12},{5,13},{6,14},{7,15},{8,0},{9,1},... | collective-permute-start | bytes 196616 | tf_op jit(solution)/shard_map/ppermute | solution.py:288
  6.5 5.6 %collective-permute-start = (bf16[128,256]{1,0:T(8,128)(2,1)S(1)}, bf16[128,256]{1,0:T(8,128)(2,1)S(1)}, u32[]{:S(2)}, u32[]{:S(2)}) collective-permute-start(bf16[128,256]{1,0:T(8,128)(2,1)S(1)} %get-tuple-element.36._), channel_id=1, source_target_pairs={{0,4},{1,5},{2,6},{3,7},{4,0},{5,1},{6,2},{7,3},{8,12},{9,13},{10,... | collective-permute-start | bytes 196616 | tf_op jit(solution)/shard_map/ppermute | solution.py:288
  12.2 9.5 %copy-start = (bf16[1,128,1024]{2,1,0:T(8,128)(2,1)S(1)}, bf16[1,128,1024]{2,1,0:T(8,128)(2,1)}, u32[]{:S(2)}) copy-start(bf16[1,128,1024]{2,1,0:T(8,128)(2,1)} %param.8) | copy-start | bytes 786436
  12.2 9.5 %copy-start.1 = (bf16[1,128,1024]{2,1,0:T(8,128)(2,1)S(1)}, bf16[1,128,1024]{2,1,0:T(8,128)(2,1)}, u32[]{:S(2)}) copy-start(bf16[1,128,1024]{2,1,0:T(8,128)(2,1)} %param.11) | copy-start | bytes 786436
  12.2 9.5 %copy-start.2 = (s32[32]{0:T(128)S(1)}, s32[32]{0:T(128)}, u32[]{:S(2)}) copy-start(s32[32]{0:T(128)} %order.1) | copy-start | bytes 388
  12.2 9.5 %copy-start.3 = (s32[1,8]{1,0:T(1,128)S(1)}, s32[1,8]{1,0:T(1,128)}, u32[]{:S(2)}) copy-start(s32[1,8]{1,0:T(1,128)} %lengths.1) | copy-start | bytes 100
  12.2 7.9 %collective-permute-start.3 = (bf16[4,128,256]{2,1,0:T(8,128)(2,1)S(1)}, bf16[4,128,256]{2,1,0:T(8,128)(2,1)S(1)}, u32[]{:S(2)}, u32[]{:S(2)}) collective-permute-start(bf16[4,128,256]{2,1,0:T(8,128)(2,1)S(1)} %pad_maximum_fusion.refs_0_), channel_id=1, source_target_pairs={{0,2},{1,3},{2,0},{3,1},{4,6},{5,7},{6,4},{7,5},{8,10},{9,11},{10,... | collective-permute-start | bytes 786440 | tf_op jit(solution)/shard_map/ppermute | solution.py:288
  13.8 42.5 %all-to-all-start = ((bf16[8,1024,128]{2,1,0:T(8,128)(2,1)}), bf16[8,1024,128]{2,1,0:T(8,128)(2,1)S(1)}, u32[]{:S(2)}, u32[]{:S(2)}) async-start(bf16[8,1024,128]{2,1,0:T(8,128)(2,1)} %columns_first.1), calls=%async_computation | async-start | bytes 4194304 | tf_op jit(solution)/shard_map/all_to_all | solution.py:311
  17.4 2.8 %collective-permute-start.4 = (bf16[4,128,256]{2,1,0:T(8,128)(2,1)S(1)}, bf16[4,128,256]{2,1,0:T(8,128)(2,1)S(1)}, u32[]{:S(2)}, u32[]{:S(2)}) collective-permute-start(bf16[4,128,256]{2,1,0:T(8,128)(2,1)S(1)} %pad_maximum_fusion.refs_0_), channel_id=1, source_target_pairs={{0,1},{1,0},{2,3},{3,2},{4,5},{5,4},{6,7},{7,6},{8,9},{9,8},{10,11... | collective-permute-start | bytes 786440 | tf_op jit(solution)/shard_map/ppermute | solution.py:288
  20.2 1.5 %collective-permute-start.5 = (bf16[4,128,256]{2,1,0:T(8,128)(2,1)S(1)}, bf16[4,128,256]{2,1,0:T(8,128)(2,1)S(1)}, u32[]{:S(2)}, u32[]{:S(2)}) collective-permute-start(bf16[4,128,256]{2,1,0:T(8,128)(2,1)S(1)} %collective-permute-done.3.refs_1_), channel_id=1, source_target_pairs={{0,1},{1,0},{2,3},{3,2},{4,5},{5,4},{6,7},{7,6},{8,9},{9,8},{10,11... | collective-permute-start | bytes 786440 | tf_op jit(solution)/shard_map/ppermute | solution.py:288
  25.6 1.5 %collective-permute-start.7 = (bf16[4,128,256]{2,1,0:T(8,128)(2,1)S(1)}, bf16[4,128,256]{2,1,0:T(8,128)(2,1)S(1)}, u32[]{:S(2)}, u32[]{:S(2)}) collective-permute-start(bf16[4,128,256]{2,1,0:T(8,128)(2,1)S(1)} %get-tuple-element.21), channel_id=1, source_target_pairs={{0,1},{1,0},{2,3},{3,2},{4,5},{5,4},{6,7},{7,6},{8,9},{9,8},{10,11... | collective-permute-start | bytes 786440 | tf_op jit(solution)/shard_map/ppermute | solution.py:288
  25.7 3.6 %collective-permute-start.6 = (bf16[4,128,256]{2,1,0:T(8,128)(2,1)S(1)}, bf16[4,128,256]{2,1,0:T(8,128)(2,1)S(1)}, u32[]{:S(2)}, u32[]{:S(2)}) collective-permute-start(bf16[4,128,256]{2,1,0:T(8,128)(2,1)S(1)} %get-tuple-element.19), channel_id=1, source_target_pairs={{0,1},{1,0},{2,3},{3,2},{4,5},{5,4},{6,7},{7,6},{8,9},{9,8},{10,11... | collective-permute-start | bytes 786440 | tf_op jit(solution)/shard_map/ppermute | solution.py:288
  27.2 7.7 %collective-permute-start.9 = (bf16[3,128,256]{2,1,0:T(8,128)(2,1)S(1)}, bf16[3,128,256]{2,1,0:T(8,128)(2,1)S(1)}, u32[]{:S(2)}, u32[]{:S(2)}) collective-permute-start(bf16[3,128,256]{2,1,0:T(8,128)(2,1)S(1)} %slice.63), channel_id=1, source_target_pairs={{0,2},{1,3},{2,0},{3,1},{4,6},{5,7},{6,4},{7,5},{8,10},{9,11},{10,... | collective-permute-start | bytes 589832 | tf_op jit(solution)/shard_map/ppermute | solution.py:288
  29.0 9.6 %collective-permute-start.8 = (bf16[128,256]{1,0:T(8,128)(2,1)S(1)}, bf16[128,256]{1,0:T(8,128)(2,1)S(1)}, u32[]{:S(2)}, u32[]{:S(2)}) collective-permute-start(bf16[128,256]{1,0:T(8,128)(2,1)S(1)} %slice_bitcast_fusion.3), channel_id=1, source_target_pairs={{0,2},{1,3},{2,0},{3,1},{4,6},{5,7},{6,4},{7,5},{8,10},{9,11},{10,... | collective-permute-start | bytes 196616 | tf_op jit(solution)/shard_map/ppermute | solution.py:288
  35.0 11.4 %collective-permute-start.10 = (bf16[128,256]{1,0:T(8,128)(2,1)S(1)}, bf16[128,256]{1,0:T(8,128)(2,1)S(1)}, u32[]{:S(2)}, u32[]{:S(2)}) collective-permute-start(bf16[128,256]{1,0:T(8,128)(2,1)S(1)} %get-tuple-element.30), channel_id=1, source_target_pairs={{0,4},{1,5},{2,6},{3,7},{4,0},{5,1},{6,2},{7,3},{8,12},{9,13},{10,... | collective-permute-start | bytes 196616 | tf_op jit(solution)/shard_map/ppermute | solution.py:288
  35.2 12.6 %collective-permute-start.12 = (bf16[128,256]{1,0:T(8,128)(2,1)S(1)}, bf16[128,256]{1,0:T(8,128)(2,1)S(1)}, u32[]{:S(2)}, u32[]{:S(2)}) collective-permute-start(bf16[128,256]{1,0:T(8,128)(2,1)S(1)} %get-tuple-element.31), channel_id=1, source_target_pairs={{0,12},{1,13},{2,14},{3,15},{4,8},{5,9},{6,10},{7,11},{8,4},{9,5},... | collective-permute-start | bytes 196616 | tf_op jit(solution)/shard_map/ppermute | solution.py:288
  36.9 10.9 %collective-permute-start.11 = (bf16[128,256]{1,0:T(8,128)(2,1)S(1)}, bf16[128,256]{1,0:T(8,128)(2,1)S(1)}, u32[]{:S(2)}, u32[]{:S(2)}) collective-permute-start(bf16[128,256]{1,0:T(8,128)(2,1)S(1)} %get-tuple-element.32), channel_id=1, source_target_pairs={{0,8},{1,9},{2,10},{3,11},{4,12},{5,13},{6,14},{7,15},{8,0},{9,1},... | collective-permute-start | bytes 196616 | tf_op jit(solution)/shard_map/ppermute | solution.py:288
  47.8 5.3 %collective-permute-start.18 = (bf16[128,256]{1,0:T(8,128)(2,1)S(1)}, bf16[128,256]{1,0:T(8,128)(2,1)S(1)}, u32[]{:S(2)}, u32[]{:S(2)}) collective-permute-start(bf16[128,256]{1,0:T(8,128)(2,1)S(1)} %fusion.8.refs_0_), channel_id=1, source_target_pairs={{0,20},{1,21},{2,22},{3,23},{4,16},{5,17},{6,18},{7,19},{8,28},{9,... | collective-permute-start | bytes 196616 | tf_op jit(solution)/shard_map/ppermute | solution.py:296
  50.3 4.3 %collective-permute-start.16 = (bf16[128,256]{1,0:T(8,128)(2,1)S(1)}, bf16[128,256]{1,0:T(8,128)(2,1)S(1)}, u32[]{:S(2)}, u32[]{:S(2)}) collective-permute-start(bf16[128,256]{1,0:T(8,128)(2,1)S(1)} %fusion.8.refs_0_), channel_id=1, source_target_pairs={{0,16},{1,17},{2,18},{3,19},{4,20},{5,21},{6,22},{7,23},{8,24},{9,... | collective-permute-start | bytes 196616 | tf_op jit(solution)/shard_map/ppermute | solution.py:296
  50.8 4.3 %collective-permute-start.14 = (bf16[128,256]{1,0:T(8,128)(2,1)S(1)}, bf16[128,256]{1,0:T(8,128)(2,1)S(1)}, u32[]{:S(2)}, u32[]{:S(2)}) collective-permute-start(bf16[128,256]{1,0:T(8,128)(2,1)S(1)} %fusion.8.refs_0_), channel_id=1, source_target_pairs={{0,4},{1,5},{2,6},{3,7},{4,0},{5,1},{6,2},{7,3},{8,12},{9,13},{10,... | collective-permute-start | bytes 196616 | tf_op jit(solution)/shard_map/ppermute | solution.py:296
  51.4 3.7 %collective-permute-start.13 = (bf16[128,256]{1,0:T(8,128)(2,1)S(1)}, bf16[128,256]{1,0:T(8,128)(2,1)S(1)}, u32[]{:S(2)}, u32[]{:S(2)}) collective-permute-start(bf16[128,256]{1,0:T(8,128)(2,1)S(1)} %fusion.8.refs_0_), channel_id=1, source_target_pairs={{0,1},{1,0},{2,3},{3,2},{4,5},{5,4},{6,7},{7,6},{8,9},{9,8},{10,11... | collective-permute-start | bytes 196616 | tf_op jit(solution)/shard_map/ppermute | solution.py:288
  53.2 2.0 %collective-permute-start.19 = (bf16[128,256]{1,0:T(8,128)(2,1)S(1)}, bf16[128,256]{1,0:T(8,128)(2,1)S(1)}, u32[]{:S(2)}, u32[]{:S(2)}) collective-permute-start(bf16[128,256]{1,0:T(8,128)(2,1)S(1)} %collective-permute-done.18.refs_6_), channel_id=1, source_target_pairs={{0,1},{1,0},{2,3},{3,2},{4,5},{5,4},{6,7},{7,6},{8,9},{9,8},{10,11... | collective-permute-start | bytes 196616 | tf_op jit(solution)/shard_map/ppermute | solution.py:288
  54.6 1.3 %collective-permute-start.17 = (bf16[128,256]{1,0:T(8,128)(2,1)S(1)}, bf16[128,256]{1,0:T(8,128)(2,1)S(1)}, u32[]{:S(2)}, u32[]{:S(2)}) collective-permute-start(bf16[128,256]{1,0:T(8,128)(2,1)S(1)} %collective-permute-done.16.refs_4_), channel_id=1, source_target_pairs={{0,1},{1,0},{2,3},{3,2},{4,5},{5,4},{6,7},{7,6},{8,9},{9,8},{10,11... | collective-permute-start | bytes 196616 | tf_op jit(solution)/shard_map/ppermute | solution.py:288
  55.1 1.3 %collective-permute-start.15 = (bf16[128,256]{1,0:T(8,128)(2,1)S(1)}, bf16[128,256]{1,0:T(8,128)(2,1)S(1)}, u32[]{:S(2)}, u32[]{:S(2)}) collective-permute-start(bf16[128,256]{1,0:T(8,128)(2,1)S(1)} %collective-permute-done.14.refs_2_), channel_id=1, source_target_pairs={{0,1},{1,0},{2,3},{3,2},{4,5},{5,4},{6,7},{7,6},{8,9},{9,8},{10,11... | collective-permute-start | bytes 196616 | tf_op jit(solution)/shard_map/ppermute | solution.py:288
  57.1 5.8 %collective-permute-start.23 = (bf16[128,256]{1,0:T(8,128)(2,1)S(1)}, bf16[128,256]{1,0:T(8,128)(2,1)S(1)}, u32[]{:S(2)}, u32[]{:S(2)}) collective-permute-start(bf16[128,256]{1,0:T(8,128)(2,1)S(1)} %get-tuple-element.27), channel_id=1, source_target_pairs={{0,2},{1,3},{2,0},{3,1},{4,6},{5,7},{6,4},{7,5},{8,10},{9,11},{10,... | collective-permute-start | bytes 196616 | tf_op jit(solution)/shard_map/ppermute | solution.py:288
  57.7 11.0 %collective-permute-start.21 = (bf16[128,256]{1,0:T(8,128)(2,1)S(1)}, bf16[128,256]{1,0:T(8,128)(2,1)S(1)}, u32[]{:S(2)}, u32[]{:S(2)}) collective-permute-start(bf16[128,256]{1,0:T(8,128)(2,1)S(1)} %get-tuple-element.24), channel_id=1, source_target_pairs={{0,8},{1,9},{2,10},{3,11},{4,12},{5,13},{6,14},{7,15},{8,0},{9,1},... | collective-permute-start | bytes 196616 | tf_op jit(solution)/shard_map/ppermute | solution.py:288
  58.1 11.2 %collective-permute-start.22 = (bf16[128,256]{1,0:T(8,128)(2,1)S(1)}, bf16[128,256]{1,0:T(8,128)(2,1)S(1)}, u32[]{:S(2)}, u32[]{:S(2)}) collective-permute-start(bf16[128,256]{1,0:T(8,128)(2,1)S(1)} %get-tuple-element.25), channel_id=1, source_target_pairs={{0,10},{1,11},{2,8},{3,9},{4,14},{5,15},{6,12},{7,13},{8,2},{9,3},... | collective-permute-start | bytes 196616 | tf_op jit(solution)/shard_map/ppermute | solution.py:288
  62.3 6.4 %collective-permute-start.20 = (bf16[256,256]{1,0:T(8,128)(2,1)S(1)}, bf16[256,256]{1,0:T(8,128)(2,1)S(1)}, u32[]{:S(2)}, u32[]{:S(2)}) collective-permute-start(bf16[256,256]{1,0:T(8,128)(2,1)S(1)} %get-tuple-element.23), channel_id=1, source_target_pairs={{0,2},{1,3},{2,0},{3,1},{4,6},{5,7},{6,4},{7,5},{8,10},{9,11},{10,... | collective-permute-start | bytes 393224 | tf_op jit(solution)/shard_map/ppermute | solution.py:288
  62.9 6.6 %collective-permute-start.24 = (bf16[128,256]{1,0:T(8,128)(2,1)S(1)}, bf16[128,256]{1,0:T(8,128)(2,1)S(1)}, u32[]{:S(2)}, u32[]{:S(2)}) collective-permute-start(bf16[128,256]{1,0:T(8,128)(2,1)S(1)} %add_convert_fusion.2), channel_id=1, source_target_pairs={{0,8},{1,9},{2,10},{3,11},{4,12},{5,13},{6,14},{7,15},{8,0},{9,1},... | collective-permute-start | bytes 196616 | tf_op jit(solution)/shard_map/ppermute | solution.py:288
